TPU v7x, 256 devices: a whole 4x4x8 slice. The times are simulated.
256 devices in a mesh: ctx: 16 (over z, core), exp: 16 (over y, x).
Axes of the slice: x: 4, y: 4, z: 8, core: 2. Of those that a mesh axis runs over, the one named last changes fastest.
Arguments:
- cache: bfloat16 [96, 6144, 576], P('exp', 'ctx'), may hold values from -6 to 6
- idx_keys: bfloat16 [96, 6144, 128], P('exp', 'ctx'), may hold values from -6 to 6
- lat_query: bfloat16 [96, 128, 576], P('exp'), may hold values from -240 to 240
- idx_query: bfloat16 [96, 64, 128], P('exp'), may hold values from -6 to 6
- idx_weight: float32 [96, 64], P('exp'), may hold values from -6 to 6
- chosen_blocks: int32 [96, 32], P('exp'), may hold values from 0 to 95, as said below
- w_uv: bfloat16 [128, 512, 128], P('ctx'), may hold values from -2.390625 to 2.390625
- w_o: bfloat16 [16384, 7168], P('ctx', 'exp'), may hold values from -0.046875 to 0.046875
- hidden_in: bfloat16 [96, 7168], P(None, 'exp'), may hold values from -6 to 6
- norm_gain: float32 [7168], P('exp'), may hold values from 0.5 to 1.5
- route: int32 [96, 4], replicated, may hold values from 0 to 15, all different within a row; in each aligned block of 96 rows (0 to 95, 96 to 191, ...) at most 48 rows name the same one
- route_weight: float32 [96, 4], replicated, may hold values from 0.2 to 1
- w_in: bfloat16 [16, 7168, 4096], P('ctx', 'exp'), may hold values from -0.0625 to 0.0625
- w_down: bfloat16 [16, 2048, 7168], P('ctx', None, 'exp'), may hold values from -0.125 to 0.125
Outputs:
- index_scores: float32 [96, 6144], P('exp', 'ctx')
- layer_out: bfloat16 [96, 7168], P('ctx', 'exp')
Inputs may be any that keep to these rules, and one draw needn't show every extreme that they name: `chosen_blocks`: each row names 32 different blocks. `route`: each row names 4 different experts; no expert is named by more than 48 rows, a bound that some block reaches.
All inputs are finite; a program needn't handle non-finite values.
Results may differ from a plain program's by a relative error of at most 0.029.
Values may be sent and summed in bfloat16 or wider, within the bound.
No kernel may reach another device: no remote copies, remote signals or barrier semaphores. Data moves between devices by JAX's collectives and lax.ppermute only.
A program may use at most 128 MiB of HBM per device.

v0:
```python
import jax
import jax.numpy as jnp
from jax import lax
from jax.sharding import PartitionSpec as P

D = 7168
BLOCK = 64


neg_big = -1e30
score_scale = 192.0 ** (-0.5)
eps = 1e-06


def merged(part, axis, combine):
    gathered = jax.tree.map(lambda a: lax.all_gather(a, axis), part)

    def take(source):
        return jax.tree.map(lambda a: lax.dynamic_index_in_dim(a, source, 0, False), gathered)

    return lax.fori_loop(
        1, lax.axis_size(axis), lambda source, state: combine(state, take(source)), take(0)
    )


def combine(first, second):
    peak_one, total_one, summed_one = first
    peak_two, total_two, summed_two = second
    peak_new = jnp.maximum(peak_one, peak_two)
    factor_one = jnp.exp(peak_one - peak_new)
    factor_two = jnp.exp(peak_two - peak_new)
    total_new = total_one * factor_one + total_two * factor_two
    summed_new = summed_one * factor_one[..., None] + summed_two * factor_two[..., None]
    return (peak_new, total_new, summed_new)


def local(
    cache,
    idx_keys,
    lat_query,
    idx_query,
    idx_weight,
    chosen_blocks,
    w_uv,
    w_o,
    hidden_in,
    norm_gain,
    route,
    route_weight,
    w_in,
    w_down,
):
    ctx_index = lax.axis_index("ctx")
    n_ctx = lax.axis_size("ctx")
    rows_here, shard_tok, _ = cache.shape
    heads_here, latent, _ = w_uv.shape
    token_ids = ctx_index * shard_tok + jnp.arange(shard_tok, dtype=jnp.int32)
    block_ids = token_ids // BLOCK
    chosen = jnp.any(block_ids[None, :, None] == chosen_blocks[:, None, :], axis=-1)
    raw = jnp.einsum(
        "rjd,rtd->rjt", idx_query, idx_keys, preferred_element_type=jnp.float32
    ) * idx_query.shape[2] ** (-0.5)
    index_scores = jnp.einsum(
        "rj,rjt->rt", idx_weight, jnp.maximum(raw, 0.0), precision=lax.Precision.HIGHEST
    )
    scores = (
        jnp.einsum("rhd,rtd->rht", lat_query, cache, preferred_element_type=jnp.float32)
        * score_scale
    )
    masked = jnp.where(chosen[:, None, :], scores, neg_big)
    peak_local = jnp.max(masked, axis=-1)
    expo = jnp.where(chosen[:, None, :], jnp.exp(masked - peak_local[..., None]), 0.0)
    total_local = jnp.sum(expo, axis=-1)
    weighted = jnp.einsum(
        "rht,rtd->rhd",
        expo.astype(jnp.bfloat16),
        cache[:, :, :latent],
        preferred_element_type=jnp.float32,
    )
    peak_all, total_all, summed_all = merged((peak_local, total_local, weighted), "ctx", combine)
    summed = lax.dynamic_slice_in_dim(summed_all, ctx_index * heads_here, heads_here, 1)
    total = lax.dynamic_slice_in_dim(total_all, ctx_index * heads_here, heads_here, 1)
    attn_lat = (summed / total[..., None]).astype(jnp.bfloat16)
    values = jnp.einsum("rhd,hdv->rhv", attn_lat, w_uv, preferred_element_type=jnp.float32)
    values = values.astype(jnp.bfloat16).reshape(rows_here, heads_here * w_uv.shape[2])
    head_part = jnp.dot(
        lax.all_gather(values, "exp", axis=0, tiled=True), w_o, preferred_element_type=jnp.float32
    )
    attn_out = lax.psum(head_part.astype(jnp.bfloat16), "ctx").astype(jnp.float32)
    resid = (hidden_in.astype(jnp.float32) + attn_out).astype(jnp.bfloat16)
    resid32 = lax.optimization_barrier(resid).astype(jnp.float32)
    scaled = (resid32 * norm_gain[None, :]).astype(jnp.bfloat16)
    squares = jnp.sum(resid32 * resid32, axis=1)
    rows_all = resid.shape[0]
    top_count = route.shape[1]
    capacity = min(rows_all, 2 * rows_all * top_count // n_ctx)
    is_mine = route == ctx_index
    hit = jnp.any(is_mine, axis=1)
    hit_weight = jnp.sum(jnp.where(is_mine, route_weight, 0.0), axis=1)
    slot_pos = jnp.cumsum(hit.astype(jnp.int32)) - 1
    select = (slot_pos[None, :] == jnp.arange(capacity, dtype=jnp.int32)[:, None]) & hit[None, :]
    pick_half = select.astype(jnp.bfloat16)
    pick_full = select.astype(jnp.float32)
    rows_in = jnp.dot(pick_half, scaled, preferred_element_type=jnp.float32).astype(jnp.bfloat16)
    slot_stats = jnp.dot(
        pick_full, jnp.stack([squares, hit_weight], axis=1), precision=lax.Precision.HIGHEST
    )
    hidden_units = w_down.shape[1]
    in_weight = w_in[0]
    down_weight = w_down[0]
    part_in = jnp.dot(rows_in, in_weight, preferred_element_type=jnp.float32)
    summed_in, slot_squares = (
        lax.psum(part_in.astype(jnp.bfloat16), "exp").astype(jnp.float32),
        lax.psum(slot_stats[:, 0].astype(jnp.bfloat16), "exp").astype(jnp.float32),
    )
    hidden_pre = summed_in * lax.rsqrt(slot_squares / D + eps)[:, None]
    act = (jax.nn.silu(hidden_pre[:, :hidden_units]) * hidden_pre[:, hidden_units:]).astype(
        jnp.bfloat16
    )
    out_slots = jnp.dot(act, down_weight, preferred_element_type=jnp.float32)
    out_slots = out_slots * slot_stats[:, 1:2]
    back_rows = jnp.dot(pick_full.T, out_slots, precision=lax.Precision.HIGHEST)
    moe_rows = lax.psum_scatter(
        back_rows.astype(jnp.bfloat16), "ctx", scatter_dimension=0, tiled=True
    ).astype(jnp.float32)
    row_block = moe_rows.shape[0]
    resid_rows = lax.dynamic_slice_in_dim(resid32, ctx_index * row_block, row_block, 0)
    layer_out = (resid_rows + moe_rows).astype(jnp.bfloat16)
    return (index_scores, layer_out)


def solution(mesh):
    return jax.shard_map(
        local,
        mesh=mesh,
        in_specs=(
            P("exp", "ctx", None),
            P("exp", "ctx", None),
            P("exp", None, None),
            P("exp", None, None),
            P("exp", None),
            P("exp", None),
            P("ctx", None, None),
            P("ctx", "exp"),
            P(None, "exp"),
            P("exp"),
            P(),
            P(),
            P("ctx", "exp", None),
            P("ctx", None, "exp"),
        ),
        out_specs=(P("exp", "ctx"), P("ctx", "exp")),
        check_vma=False,
    )
```

profile of v0, /device:TPU:1, one launch (start us, length us, event | category | flops | bytes accessed | tf_op | source)
XLA Modules:
  0.0 470.1 jit_solution(15919141131729983892)
XLA Ops:
  8.2 3.1 fusion.55
  11.3 2.2 fusion.5
  14.8 21.5 %all-gather.4 = f32[16,6,128]{2,1,0:T(8,128)S(1)} all-gather(f32[1,6,128]{2,1,0:T(8,128)S(1)} %bitcast.64), channel_id=3, replica_groups=mesh['ctx'=16,'exp'=16] {'ctx'}, dimensions={0}, use_global_device_ids=true | all-gather | bytes 52224 | tf_op jit(solution)/shard_map/all_gather | solution.py:16
  36.4 14.8 %all-gather.3 = f32[16,6,128]{2,1,0:T(8,128)S(1)} all-gather(f32[1,6,128]{2,1,0:T(8,128)S(1)} %bitcast.63), channel_id=2, replica_groups=mesh['ctx'=16,'exp'=16] {'ctx'}, dimensions={0}, use_global_device_ids=true | all-gather | bytes 52224 | tf_op jit(solution)/shard_map/all_gather | solution.py:16
  53.0 100.2 %all-gather.8.cloned.1.call-done = f32[96,128,512]{2,1,0:T(8,128)} async-done(((f32[6,128,512]{2,1,0:T(8,128)}), f32[96,128,512]{2,1,0:T(8,128)}) %all-gather.8.cloned.1.call-update) | async-done | bytes 25165840 | tf_op jit(solution)/shard_map/all_gather | solution.py:16
  154.7 38.4 %while.19 = (s32[]{:T(128)}, f32[6,128]{1,0:T(8,128)S(1)}, f32[6,128]{1,0:T(8,128)S(1)}, f32[6,128,512]{2,1,0:T(8,128)S(1)}, f32[16,6,128]{2,1,0:T(8,128)}, /*in...) while((s32[]{:T(128)}, f32[6,128]{1,0:T(8,128)S(1)}, ...), condition=%wide.region_4.5_spmd, body=%wide.region_3.4_spmd.sunk | while | flops 1184261 | bytes 4749463 | solution.py:21
  155.4 1.8 fusion.69
  158.0 1.8 fusion.69
  160.6 1.8 fusion.69
  163.1 1.8 fusion.69
  165.7 1.8 fusion.69
  168.2 1.8 fusion.69
  170.8 1.8 fusion.69
  183.6 1.8 fusion.69
  188.7 1.8 fusion.69
  194.9 18.5 %all-gather.5 = bf16[16,6,1024]{2,1,0:T(8,128)(2,1)S(1)} all-gather(bf16[1,6,1024]{2,1,0:T(8,128)(2,1)S(1)} %fusion.14), channel_id=1, replica_groups=mesh['ctx'=16,'exp'=16] {'exp'}, dimensions={0}, use_global_device_ids=true | all-gather | bytes 208896 | tf_op jit(solution)/shard_map/all_gather | solution.py:87
  214.8 105.2 %all-reduce.5.cloned.1.call-done = bf16[96,448]{1,0:T(8,128)(2,1)} async-done(((bf16[96,448]{1,0:T(8,128)(2,1)}), bf16[96,448]{1,0:T(8,128)(2,1)}) %all-reduce.5.cloned.1.call-update) | async-done | bytes 86032 | tf_op jit(solution)/shard_map/psum | solution.py:89
  321.1 3.7 convolution_convert_fusion
  324.9 33.2 %psum.23 = bf16[48]{0:T(256)(128)(2,1)S(1)} all-reduce(bf16[48]{0:T(256)(128)(2,1)S(1)} %slice_bitcast_fusion.3), channel_id=1, replica_groups=mesh['ctx'=16,'exp'=16] {'exp'}, use_global_device_ids=true, to_apply=%region_11.12 | all-reduce | flops 48 | bytes 192 | tf_op jit(solution)/shard_map/psum | solution.py:114
  358.1 59.9 %all-reduce.7.cloned.1.call-done = bf16[48,4096]{1,0:T(8,128)(2,1)} async-done(((bf16[48,4096]{1,0:T(8,128)(2,1)}), bf16[48,4096]{1,0:T(8,128)(2,1)}) %all-reduce.7.cloned.1.call-update) | async-done | bytes 393232 | tf_op jit(solution)/shard_map/psum | solution.py:113
  420.0 26.7 %fusion = bf16[8,448]{1,0:T(8,128)(2,1)S(1)} fusion(bf16[96,448]{1,0:T(8,128)(2,1)S(1)} %convolution_convert_fusion.1), kind=kCustom, calls=%all-reduce-scatter | all-reduce-scatter fusion | flops 57345 | bytes 94208
  446.7 2.7 collective-permute-start
  450.7 4.6 collective-permute-start.2
  455.3 4.7 %collective-permute-start.3 = (bf16[6,448]{1,0:T(8,128)(2,1)S(1)}, bf16[6,448]{1,0:T(8,128)(2,1)S(1)}, u32[]{:S(2)}, u32[]{:S(2)}) collective-permute-start(bf16[6,448]{1,0:T(8,128)(2,1)S(1)} %slice.34), channel_id=1, source_target_pairs={{0,64},{16,80},{32,96},{48,112},{64,128},{80,144},{96,160},{112,17... | collective-permute-start | bytes 16136
  (92 shorter events, 37.5 us)
Async XLA Ops:
  7.2 411.9 %copy-start = (bf16[1,2048,448]{1,2,0:T(8,128)(2,1)S(1)}, bf16[1,2048,448]{1,2,0:T(8,128)(2,1)}, u32[]{:S(2)}) copy-start(bf16[1,2048,448]{1,2,0:T(8,128)(2,1)} %param.29) | copy-start | bytes 5505028
  7.2 146.0 %all-gather.8.cloned.1.call-start = ((), (), s32[]{:S(2)}) async-start(), calls=%async_computation.2 | async-start | bytes 26738688 | tf_op jit(solution)/shard_map/all_gather | solution.py:16
  8.2 3.1 copy-start.1
  13.4 0.7 copy-start.10
  13.4 0.7 copy-start.11
  13.4 38.4 %copy-start.6 = (bf16[6,64,128]{2,1,0:T(8,128)(2,1)S(1)}, bf16[6,64,128]{2,1,0:T(8,128)(2,1)}, u32[]{:S(2)}) copy-start(bf16[6,64,128]{2,1,0:T(8,128)(2,1)} %param.19) | copy-start | bytes 294916
  13.5 306.5 %all-reduce.5.cloned.1.call-start = ((), (), s32[]{:S(2)}) async-start(), calls=%async_computation | async-start | bytes 196608 | tf_op jit(solution)/shard_map/psum | solution.py:89
  14.4 37.4 %copy-start.4 = (bf16[6,384,128]{2,1,0:T(8,128)(2,1)S(1)}, bf16[6,384,128]{2,1,0:T(8,128)(2,1)}, u32[]{:S(2)}) copy-start(bf16[6,384,128]{2,1,0:T(8,128)(2,1)} %param.17) | copy-start | bytes 1769476
  51.2 0.6 copy-start.5
  193.3 20.2 %copy-start.3 = (bf16[1024,448]{0,1:T(8,128)(2,1)S(1)}, bf16[1024,448]{0,1:T(8,128)(2,1)}, u32[]{:S(2)}) copy-start(bf16[1024,448]{0,1:T(8,128)(2,1)} %param.23) | copy-start | bytes 2752516
  193.3 126.6 %copy-start.7 = (bf16[96,448]{1,0:T(8,128)(2,1)S(1)}, bf16[96,448]{1,0:T(8,128)(2,1)}, u32[]{:S(2)}) copy-start(bf16[96,448]{1,0:T(8,128)(2,1)} %param.24) | copy-start | bytes 258052
  193.3 127.8 %copy-start.9 = (f32[448]{0:T(512)S(1)}, f32[448]{0:T(512)}, u32[]{:S(2)}) copy-start(f32[448]{0:T(512)} %param.25) | copy-start | bytes 5380
  214.6 203.3 %all-reduce.7.cloned.1.call-start = ((), (), s32[]{:S(2)}) async-start(), calls=%async_computation.1 | async-start | bytes 786432 | tf_op jit(solution)/shard_map/psum | solution.py:113
  419.1 41.0 %copy-start.2 = (f32[6,64,384]{2,1,0:T(8,128)S(1)}, f32[6,64,384]{2,1,0:T(8,128)}, u32[]{:S(2)}) copy-start(f32[6,64,384]{2,1,0:T(8,128)} %fusion.10) | copy-start | bytes 1769476
  419.1 41.0 %copy-start.8 = (f32[6,64]{1,0:T(8,128)S(1)}, f32[6,64]{1,0:T(8,128)}, u32[]{:S(2)}) copy-start(f32[6,64]{1,0:T(8,128)} %param.20) | copy-start | bytes 4612
  419.1 42.1 %copy-start.12 = (u32[256]{0:T(256)S(1)}, u32[256]{0:T(256)}, u32[]{:S(2)}) copy-start(u32[256]{0:T(256)} %constant.119) | copy-start | bytes 3076
  446.7 15.7 %collective-permute-start = (bf16[8,448]{1,0:T(8,128)(2,1)S(1)}, bf16[8,448]{1,0:T(8,128)(2,1)S(1)}, u32[]{:S(2)}, u32[]{:S(2)}) collective-permute-start(bf16[8,448]{1,0:T(8,128)(2,1)S(1)} %fusion), channel_id=1, source_target_pairs={{0,16},{16,32},{32,48},{48,64},{64,80},{80,96},{96,112},{112,128},... | collective-permute-start | bytes 21512
  449.4 13.1 %collective-permute-start.1 = (bf16[8,448]{1,0:T(8,128)(2,1)S(1)}, bf16[8,448]{1,0:T(8,128)(2,1)S(1)}, u32[]{:S(2)}, u32[]{:S(2)}) collective-permute-start(bf16[8,448]{1,0:T(8,128)(2,1)S(1)} %fusion), channel_id=1, source_target_pairs={{0,32},{16,48},{32,64},{48,80},{64,96},{80,112},{96,128},{112,144}... | collective-permute-start | bytes 21512
  450.7 11.8 %collective-permute-start.2 = (bf16[8,448]{1,0:T(8,128)(2,1)S(1)}, bf16[8,448]{1,0:T(8,128)(2,1)S(1)}, u32[]{:S(2)}, u32[]{:S(2)}) collective-permute-start(bf16[8,448]{1,0:T(8,128)(2,1)S(1)} %fusion), channel_id=1, source_target_pairs={{0,48},{16,64},{32,80},{48,96},{64,112},{80,128},{96,144},{112,160... | collective-permute-start | bytes 21512
  455.3 7.1 %collective-permute-start.3 = (bf16[6,448]{1,0:T(8,128)(2,1)S(1)}, bf16[6,448]{1,0:T(8,128)(2,1)S(1)}, u32[]{:S(2)}, u32[]{:S(2)}) collective-permute-start(bf16[6,448]{1,0:T(8,128)(2,1)S(1)} %slice.34), channel_id=1, source_target_pairs={{0,64},{16,80},{32,96},{48,112},{64,128},{80,144},{96,160},{112,17... | collective-permute-start | bytes 16136
Sparse Core Ops, SparseCore 0:
  13.6 139.5 all-gather.7
  214.7 105.1 all-reduce.4
  325.0 92.8 all-reduce.6
where the time goes:
time: 471 us; the launch traced here: 470 us
  waiting for transfers between devices  265 us (56%)
  blocking collectives  115 us (24%)
  other arithmetic  42.5 us (9%)
  between operations  14.7 us (3%)
  matrix products  14.3 us (3%)
  starting transfers between devices  13.4 us (3%)
    psum x1, waiting for transfers between devices, local(): lax.psum(head_part.astype(jnp.bfloat16), 'ctx').astype(jnp.float32)  105 us
    all_gather x1, waiting for transfers between devices, merged(): gathered = jax.tree.map(lambda a: lax.all_gather(a, axis), part)  100 us
    psum x1, waiting for transfers between devices, local(): lax.psum(part_in.astype(jnp.bfloat16), 'exp').astype(jnp.float32)  59.9 us
    all_gather x2, blocking collectives, merged(): gathered = jax.tree.map(lambda a: lax.all_gather(a, axis), part)  36.4 us
    psum x1, blocking collectives, local(): lax.psum(slot_stats[:, 0].astype(jnp.bfloat16), 'exp').astype(jnp.float32)  33.2 us
    add x15, other arithmetic, combine(): summed_one * factor_one[..., None] + summed_two * factor_two[..., None]  27.6 us
    unnamed x1, blocking collectives  26.7 us
    all_gather x1, blocking collectives, local(): lax.all_gather(values, 'exp', axis=0, tiled=True)  18.5 us
  transfers between devices with their start and end apart: 7, of which 3 were waited for; matrix products, arithmetic and copies ran while one was open for 1% of the time, Pallas kernels for 0%

commit v1 on v0

v1 whole, which is shorter than its diff:
```python
import functools

import jax
import jax.numpy as jnp
from jax import lax
from jax.experimental import pallas as pl
from jax.experimental.pallas import tpu as pltpu
from jax.sharding import PartitionSpec as P

f32 = jnp.float32
bf16 = jnp.bfloat16
D = 7168
BLOCK = 64
LAT = 512
WIDE = 640
CAP = 48
NEG = -1e30
SCORE_SCALE = 192.0 ** (-0.5)
EPS = 1e-06
HIGH = lax.Precision.HIGHEST
MB = 1 << 20

VMEM = pl.BlockSpec(memory_space=pltpu.VMEM)
SMEM = pl.BlockSpec(memory_space=pltpu.SMEM)


def params(mb=32):
    return pltpu.CompilerParams(vmem_limit_bytes=mb * MB)


def iota(shape, dim):
    return lax.broadcasted_iota(jnp.int32, shape, dim)


def dot(a, b, dims=((1,), (0,)), precision=None):
    return lax.dot_general(a, b, (dims, ((), ())), precision=precision, preferred_element_type=f32)


def split3(x):
    hi = x.astype(bf16).astype(f32)
    mid = (x - hi).astype(bf16).astype(f32)
    low = (x - hi - mid).astype(bf16).astype(f32)
    return hi, mid, low


def stats_tile(peak, total):
    lane = iota(peak.shape[:-1] + (128,), len(peak.shape) - 1)
    tile = jnp.zeros(peak.shape[:-1] + (128,), f32)
    for place, part in enumerate(split3(peak) + split3(total)):
        tile = jnp.where(lane == place, part, tile)
    return tile


def read_stats(x):
    tile = x[..., LAT:WIDE]
    lane = iota(tile.shape, len(tile.shape) - 1)
    peak = jnp.sum(jnp.where(lane < 3, tile, 0.0), axis=-1, keepdims=True)
    total = jnp.sum(jnp.where((lane >= 3) & (lane < 6), tile, 0.0), axis=-1, keepdims=True)
    return peak, total


def attention_kernel(ctx_ref, blocks_ref, query_ref, cache_ref, mine_ref, other_ref, mask_ref):
    step = pl.program_id(0)
    ctx = ctx_ref[0]
    core = lax.rem(ctx, 2)
    tokens = cache_ref.shape[1]
    per = tokens // BLOCK

    @pl.when(step == 0)
    def _():
        rows = blocks_ref.shape[0]
        block_of = iota((rows, tokens), 1) // BLOCK
        mask = jnp.zeros((rows, tokens), f32)
        picked = blocks_ref[...]
        for b in range(per):
            hit = jnp.max(jnp.where(picked == ctx * per + b, 1.0, 0.0), axis=1, keepdims=True)
            mask = jnp.where(block_of == b, hit, mask)
        mask_ref[...] = mask

    mine, other = [], []
    for i in range(2):
        chosen = mask_ref[pl.ds(step * 2 + i, 1), :] > 0.0
        keys = cache_ref[i]
        scores = dot(query_ref[i], keys, ((1,), (1,))) * SCORE_SCALE
        masked = jnp.where(chosen, scores, NEG)
        peak = jnp.max(masked, axis=1, keepdims=True)
        expo = jnp.where(chosen, jnp.exp(masked - peak), 0.0)
        total = jnp.sum(expo, axis=1, keepdims=True)
        weighted = dot(expo.astype(bf16), keys[:, :LAT])
        wide = jnp.concatenate([weighted, stats_tile(peak, total)], axis=1)
        wide = wide.reshape(8, 2, 8, WIDE)
        mine.append(jnp.where(core == 0, wide[:, 0], wide[:, 1]))
        other.append(jnp.where(core == 0, wide[:, 1], wide[:, 0]))
    mine_ref[...] = jnp.concatenate(mine, axis=1)
    other_ref[...] = jnp.concatenate(other, axis=1).astype(bf16)


def attention(ctx, blocks, query, cache):
    rows, heads, width = query.shape
    tokens = cache.shape[1]
    return pl.pallas_call(
        attention_kernel,
        grid=(rows // 2,),
        in_specs=[
            SMEM,
            pl.BlockSpec((rows, blocks.shape[1]), lambda i: (0, 0)),
            pl.BlockSpec((2, heads, width), lambda i: (i, 0, 0)),
            pl.BlockSpec((2, tokens, width), lambda i: (i, 0, 0)),
        ],
        out_specs=[pl.BlockSpec((8, 16, WIDE), lambda i: (0, i, 0))] * 2,
        out_shape=[
            jax.ShapeDtypeStruct((8, rows * 8, WIDE), f32),
            jax.ShapeDtypeStruct((8, rows * 8, WIDE), bf16),
        ],
        scratch_shapes=[pltpu.VMEM((rows, tokens), f32)],
        compiler_params=params(),
        name="attention",
    )(ctx, blocks, query, cache)


def side_kernel(ctx_ref, route_ref, gate_ref, iq_ref, iw_ref, keys_ref, score_ref, pick_ref, back_ref, slot_ref):
    rows = iq_ref.shape[0]
    for r in range(rows):
        raw = dot(iq_ref[r], keys_ref[r], ((1,), (1,))) * (iq_ref.shape[2] ** (-0.5))
        score_ref[r : r + 1, :] = dot(iw_ref[r : r + 1, :], jnp.maximum(raw, 0.0), precision=HIGH)
    n = route_ref.shape[1]
    is_mine = route_ref[...] == ctx_ref[0]
    hit = jnp.max(jnp.where(is_mine, 1.0, 0.0), axis=0, keepdims=True)
    gate = jnp.sum(jnp.where(is_mine, gate_ref[...], 0.0), axis=0, keepdims=True)
    upto = jnp.where(iota((n, n), 0) <= iota((n, n), 1), 1.0, 0.0).astype(bf16)
    slot = dot(jnp.broadcast_to(hit, (8, n)).astype(bf16), upto)[0:1].astype(jnp.int32) - 1
    pick = jnp.where((iota((CAP, n), 0) == slot) & (hit > 0.0), 1.0, 0.0)
    pick_ref[...] = pick.astype(bf16)
    row, col = iota((128, n), 0), iota((128, n), 1)
    spread = (row // 8 * 6 + row % 8 == col) & (row % 8 < 6)
    spread = jnp.where(spread, 1.0, 0.0).astype(bf16)
    back_ref[...] = dot(spread, pick.astype(bf16), ((1,), (1,))).astype(bf16)
    slot_ref[...] = jnp.broadcast_to(jnp.sum(pick * gate, axis=1, keepdims=True), (CAP, 128))


def side(ctx, route, gate, iq, iw, keys):
    return pl.pallas_call(
        side_kernel,
        in_specs=[SMEM] + [VMEM] * 5,
        out_specs=[VMEM] * 4,
        out_shape=[
            jax.ShapeDtypeStruct((iq.shape[0], keys.shape[1]), f32),
            jax.ShapeDtypeStruct((CAP, route.shape[1]), bf16),
            jax.ShapeDtypeStruct((128, CAP), bf16),
            jax.ShapeDtypeStruct((CAP, 128), f32),
        ],
        compiler_params=params(),
        name="side",
    )(ctx, route, gate, iq, iw, keys)


def pair_kernel(mine_ref, other_ref, out_ref):
    one = mine_ref[...]
    two = other_ref[...].astype(f32)
    peak_one, total_one = read_stats(one)
    peak_two, total_two = read_stats(two)
    peak = jnp.maximum(peak_one, peak_two)
    f_one, f_two = jnp.exp(peak_one - peak), jnp.exp(peak_two - peak)
    out_ref[..., :LAT] = (one[..., :LAT] * f_one + two[..., :LAT] * f_two).astype(bf16)
    out_ref[..., LAT:] = stats_tile(peak, total_one * f_one + total_two * f_two).astype(bf16)


def pair(mine, other):
    spec = pl.BlockSpec((2,) + mine.shape[1:], lambda i: (i, 0, 0))
    return pl.pallas_call(
        pair_kernel,
        grid=(mine.shape[0] // 2,),
        in_specs=[spec, spec],
        out_specs=spec,
        out_shape=jax.ShapeDtypeStruct(mine.shape, bf16),
        compiler_params=params(),
        name="pair",
    )(mine, other)


def values_kernel(parts_ref, w_ref, out_ref):
    n, rows, _ = parts_ref.shape
    peaks, totals = [], []
    for i in range(n):
        p, t = read_stats(parts_ref[i].astype(f32))
        peaks.append(p)
        totals.append(t)
    peak = functools.reduce(jnp.maximum, peaks)
    summed = jnp.zeros((rows, LAT), f32)
    total = jnp.zeros((rows, 1), f32)
    for i in range(n):
        factor = jnp.exp(peaks[i] - peak)
        summed = summed + parts_ref[i, :, :LAT].astype(f32) * factor
        total = total + totals[i] * factor
    lat = (summed / total).astype(bf16)
    row, col = iota((64, rows), 0), iota((64, rows), 1)
    by_head = jnp.where((row % 8) * 8 + row // 8 == col, 1.0, 0.0).astype(bf16)
    lat = dot(by_head, lat)
    out = [dot(lat[8 * h : 8 * h + 8].astype(bf16), w_ref[h]) for h in range(8)]
    half = jnp.concatenate([jnp.concatenate(out[:4], axis=1), jnp.concatenate(out[4:], axis=1)], axis=0)
    half = half.astype(bf16)
    for e in range(out_ref.shape[0]):
        out_ref[e] = half


def values(parts, w_uv, n_exp):
    return pl.pallas_call(
        values_kernel,
        in_specs=[VMEM] * 2,
        out_specs=VMEM,
        out_shape=jax.ShapeDtypeStruct((n_exp, 16, 512), bf16),
        compiler_params=params(),
        name="values",
    )(parts, w_uv)


def project_kernel(values_ref, w_ref, out_ref, acc_ref):
    x = values_ref[...].astype(f32)
    n = x.shape[0]
    low = x[:, :8].reshape(n * 8, 512).astype(bf16)
    high = x[:, 8:].reshape(n * 8, 512).astype(bf16)
    acc = dot(low, w_ref[:512, :]) + dot(high, w_ref[512:, :])
    for e in range(n):
        acc_ref[6 * e : 6 * e + 6, :] = acc[8 * e : 8 * e + 6, :]
    out_ref[...] = acc_ref[...].astype(bf16)


def project(vals, w_o):
    shape = (vals.shape[0] * 6, w_o.shape[1])
    return pl.pallas_call(
        project_kernel,
        in_specs=[VMEM] * 2,
        out_specs=VMEM,
        out_shape=jax.ShapeDtypeStruct(shape, bf16),
        scratch_shapes=[pltpu.VMEM(shape, f32)],
        compiler_params=params(),
        name="project",
    )(vals, w_o)


def expert_in_kernel(
    ctx_ref, own_ref, up_ref, down_ref, far_up_ref, far_down_ref, hidden_ref, gain_ref, pick_ref,
    gate_w_ref, up_w_ref, out_ref, keep_ref, rows_ref, squares_ref,
):
    @pl.when(pl.program_id(0) == 0)
    def _():
        attn = own_ref[...].astype(f32) + up_ref[...].astype(f32) + down_ref[...].astype(f32)
        attn = attn + far_up_ref[...].astype(f32) + far_down_ref[...].astype(f32)
        resid = (hidden_ref[...].astype(f32) + attn).astype(bf16)
        resid32 = resid.astype(f32)
        scaled = (resid32 * gain_ref[...]).astype(bf16)
        rows_ref[...] = dot(pick_ref[...], scaled).astype(bf16)
        picked = dot(pick_ref[...], resid)
        squares = dot(jnp.ones((8, picked.shape[1]), f32), picked * picked, ((1,), (1,)), HIGH)
        hi, mid, low = split3(squares)
        line = iota(squares.shape, 0)
        parts = jnp.where(line == 0, hi, jnp.where(line == 1, mid, jnp.where(line == 2, low, 0.0)))
        squares_ref[...] = jnp.concatenate([parts, jnp.zeros((8, 256 - CAP), f32)], axis=1)
        n = resid.shape[0]
        own_row = jnp.where(iota((8, n), 1) == ctx_ref[0] * 6 + iota((8, n), 0), 1.0, 0.0)
        keep_ref[...] = dot(own_row.astype(bf16), resid)

    rows = rows_ref[...]
    gate = dot(rows, gate_w_ref[...])
    up = dot(rows, up_w_ref[...])
    squares = squares_ref[...]
    for e in range(out_ref.shape[0]):
        cols = slice(128 * e, 128 * e + 128)
        both = jnp.concatenate([gate[:, cols], up[:, cols]], axis=1)
        out_ref[e] = jnp.concatenate([both, squares], axis=0).astype(bf16)


def expert_in(ctx, sums, hidden, gain, pick, w_in, n_exp):
    rows, width = hidden.shape
    steps = 4
    cols = w_in.shape[1] // 2 // steps
    whole = lambda a: pl.BlockSpec(a.shape, lambda i: (0,) * a.ndim)
    return pl.pallas_call(
        expert_in_kernel,
        grid=(steps,),
        in_specs=[SMEM]
        + [whole(a) for a in (*sums, hidden, gain, pick)]
        + [
            pl.BlockSpec((width, cols), lambda i: (0, i)),
            pl.BlockSpec((width, cols), lambda i: (0, i + steps)),
        ],
        out_specs=[
            pl.BlockSpec((n_exp // steps, CAP + 8, 256), lambda i: (i, 0, 0)),
            pl.BlockSpec((8, width), lambda i: (0, 0)),
        ],
        out_shape=[
            jax.ShapeDtypeStruct((n_exp, CAP + 8, 256), bf16),
            jax.ShapeDtypeStruct((8, width), f32),
        ],
        scratch_shapes=[pltpu.VMEM((CAP, width), bf16), pltpu.VMEM((8, 256), f32)],
        compiler_params=params(),
        name="expert_in",
    )(ctx, *sums, hidden, gain, pick, w_in, w_in)


def act_kernel(parts_ref, out_ref):
    x = jnp.sum(parts_ref[...].astype(f32), axis=0)
    line = x[CAP : CAP + 1, :CAP] + x[CAP + 1 : CAP + 2, :CAP] + x[CAP + 2 : CAP + 3, :CAP]
    diagonal = iota((CAP, CAP), 0) == iota((CAP, CAP), 1)
    squares = jnp.sum(jnp.where(diagonal, line, 0.0), axis=1, keepdims=True)
    inv = lax.rsqrt(squares / D + EPS)
    gate, up = x[:CAP, :128] * inv, x[:CAP, 128:] * inv
    act = (jax.nn.silu(gate) * up).astype(bf16)
    for e in range(out_ref.shape[0]):
        out_ref[e] = act


def activation(parts):
    return pl.pallas_call(
        act_kernel,
        in_specs=[VMEM],
        out_specs=VMEM,
        out_shape=jax.ShapeDtypeStruct((parts.shape[0], CAP, 128), bf16),
        compiler_params=params(),
        name="activation",
    )(parts)


def expert_out_kernel(act_ref, w_ref, slot_ref, back_ref, out_ref):
    act = jnp.concatenate([act_ref[e] for e in range(act_ref.shape[0])], axis=1)
    out = (dot(act, w_ref[...]) * slot_ref[:, 0:1]).astype(bf16)
    back = dot(back_ref[...], out)
    n = out_ref.shape[0]
    low = back[:, :256].reshape(n, 8, 256)
    high = jnp.concatenate([back[:, 256:], jnp.zeros((n * 8, 64), f32)], axis=1).reshape(n, 8, 256)
    out_ref[...] = jnp.concatenate([low, high], axis=1).astype(bf16)


def expert_out(act, w_down, slot, back, n_ctx):
    return pl.pallas_call(
        expert_out_kernel,
        in_specs=[VMEM] * 4,
        out_specs=VMEM,
        out_shape=jax.ShapeDtypeStruct((n_ctx, 16, 256), bf16),
        compiler_params=params(),
        name="expert_out",
    )(act, w_down, slot, back)


def last_kernel(parts_ref, keep_ref, out_ref):
    x = jnp.sum(parts_ref[...].astype(f32), axis=0)
    moe = jnp.concatenate([x[:8], x[8:, :192]], axis=1)
    out_ref[...] = (keep_ref[...] + moe)[:6].astype(bf16)


def last(parts, keep):
    return pl.pallas_call(
        last_kernel,
        in_specs=[VMEM] * 2,
        out_specs=VMEM,
        out_shape=jax.ShapeDtypeStruct((6, keep.shape[1]), bf16),
        compiler_params=params(),
        name="last",
    )(parts, keep)


def local(
    cache, idx_keys, lat_query, idx_query, idx_weight, chosen_blocks, w_uv, w_o, hidden_in, norm_gain,
    route, route_weight, w_in, w_down,
):
    n_ctx, n_exp = lax.axis_size("ctx"), lax.axis_size("exp")
    n_z = n_ctx // 2
    ctx = lax.axis_index("ctx").astype(jnp.int32).reshape(1)
    other_core = [(i, i ^ 1) for i in range(n_ctx)]
    z_groups = [[2 * z + k for z in range(n_z)] for k in range(2)]

    def along_z(shift):
        return [(i, (i + 2 * shift) % n_ctx) for i in range(n_ctx)]

    mine, other = attention(ctx, chosen_blocks, lat_query, cache)
    other = lax.ppermute(other, "ctx", other_core)
    index_scores, pick, back, slot = side(
        ctx, route.T, route_weight.T, idx_query, idx_weight, idx_keys
    )
    parts = pair(mine, other)
    parts = lax.all_to_all(parts, "ctx", 0, 0, axis_index_groups=z_groups)
    vals = values(parts, w_uv, n_exp)
    vals = lax.all_to_all(vals, "exp", 0, 0)
    part = project(vals, w_o)

    def add(*terms):
        return sum(t.astype(f32) for t in terms).astype(bf16)

    own = add(part, lax.ppermute(part, "ctx", other_core))
    above = lax.ppermute(own, "ctx", along_z(-1))
    below = lax.ppermute(own, "ctx", along_z(1))
    far_above = lax.ppermute(add(own, above, below), "ctx", along_z(-3))
    far_below = lax.ppermute(add(own, above), "ctx", along_z(3))
    sums = (own, above, below, far_above, far_below)

    terms, keep = expert_in(ctx, sums, hidden_in, norm_gain.reshape(1, -1), pick, w_in[0], n_exp)
    terms = lax.all_to_all(terms, "exp", 0, 0)
    act = lax.all_to_all(activation(terms), "exp", 0, 0)
    outs = expert_out(act, w_down[0], slot, back, n_ctx)
    outs = lax.all_to_all(outs, "ctx", 0, 0)
    return index_scores, last(outs, keep)


def solution(mesh):
    return jax.shard_map(
        local,
        mesh=mesh,
        in_specs=(
            P("exp", "ctx", None),
            P("exp", "ctx", None),
            P("exp", None, None),
            P("exp", None, None),
            P("exp", None),
            P("exp", None),
            P("ctx", None, None),
            P("ctx", "exp"),
            P(None, "exp"),
            P("exp"),
            P(),
            P(),
            P("ctx", "exp", None),
            P("ctx", None, "exp"),
        ),
        out_specs=(P("exp", "ctx"), P("ctx", "exp")),
        check_vma=False,
    )
```

time: 471 us -> 123 us (0.26)
  waiting for transfers between devices: 265 us -> 21.2 us
  blocking collectives: 115 us -> 53.9 us
  other arithmetic: 42.5 us -> 0.07 us
  matrix products: 14.3 us -> 0 us
  between operations: 14.7 us -> 0.81 us
  Pallas kernels: 0 us -> 11.7 us
  starting transfers between devices: 13.4 us -> 22 us
  local copies, waits for them, and re-layouts: 4.7 us -> 12.9 us
    psum x2 -> x0, waiting for transfers between devices: 165 us -> none  [the longest x1 105 us: local(): lax.psum(head_part.astype(jnp.bfloat16), 'ctx').astype(jnp.float32)]
    all_gather x1 -> x0, waiting for transfers between devices: 100 us -> none  [merged(): gathered = jax.tree.map(lambda a: lax.all_gather(a, axis), part)]
    all_gather x3 -> x0, blocking collectives: 54.9 us -> none  [the longest x2 36.4 us: merged(): gathered = jax.tree.map(lambda a: lax.all_gather(a, axis), part)]
    all_to_all x0 -> x3, blocking collectives: none -> 53.9 us  [the longest x1 22.2 us: local(): parts = lax.all_to_all(parts, 'ctx', 0, 0, axis_index_groups=z_groups)]
    add x30 -> x0, other arithmetic: 38 us -> none  [the longest x15 27.6 us: combine(): summed_one * factor_one[..., None] + summed_two * factor_two[..., None]]
    psum x1 -> x0, blocking collectives: 33.2 us -> none  [local(): lax.psum(slot_stats[:, 0].astype(jnp.bfloat16), 'exp').astype(jnp.float32)]
    unnamed x1 -> x0, blocking collectives: 26.7 us -> none
    dot_general x10 -> x0, matrix products: 14.3 us -> none  [the longest x1 3.7 us: local(): part_in = jnp.dot(rows_in, in_weight, preferred_element_type=jnp.float32)]
  transfers between devices with their start and end apart: 7 -> 8, of which waited for: 3 -> 8; matrix products, arithmetic and copies ran while one was open for 1% -> 3% of each run, Pallas kernels for 0% -> 2%
where the time goes in v1:
time: 123 us
  blocking collectives  53.9 us (44%)
  starting transfers between devices  22 us (18%)
  waiting for transfers between devices  21.2 us (17%)
  local copies, waits for them, and re-layouts  12.9 us (10%)
  Pallas kernels  11.7 us (10%)
    all_to_all x1, blocking collectives, local(): parts = lax.all_to_all(parts, 'ctx', 0, 0, axis_index_groups=z_groups)  22.2 us
    all_to_all x1, blocking collectives, local(): outs = lax.all_to_all(outs, 'ctx', 0, 0)  20.5 us
    unnamed x28, local copies, waits for them, and re-layouts  12.9 us
    all_to_all x1, blocking collectives, local(): terms = lax.all_to_all(terms, 'exp', 0, 0)  11.2 us
    all_to_all x1, waiting for transfers between devices, local(): vals = lax.all_to_all(vals, 'exp', 0, 0)  7 us
    all_to_all x1, starting transfers between devices, local(): vals = lax.all_to_all(vals, 'exp', 0, 0)  6.9 us
    all_to_all x1, waiting for transfers between devices, local(): act = lax.all_to_all(activation(terms), 'exp', 0, 0)  4.34 us
    all_to_all x1, starting transfers between devices, local(): act = lax.all_to_all(activation(terms), 'exp', 0, 0)  3.52 us
  transfers between devices with their start and end apart: 8, of which 8 were waited for; matrix products, arithmetic and copies ran while one was open for 3% of the time, Pallas kernels for 2%

profile of v1, /device:TPU:1, one launch (start us, length us, event | category | flops | bytes accessed | tf_op | source)
XLA Modules:
  0.0 122.6 jit_solution(4119588319213304160)
XLA Ops:
  0.6 4.0 %copy.17.cache_ref = bf16[6,384,576]{2,1,0:T(8,128)(2,1)S(1)} copy(bf16[6,384,576]{1,2,0:T(8,128)(2,1)} %param.14) | data formatting | bytes 5308416 | tf_op args[0]
  4.7 2.2 %copy.16.query_ref = bf16[6,128,576]{2,1,0:T(8,128)(2,1)} copy(bf16[6,128,576]{1,2,0:T(8,128)(2,1)} %param.16) | data formatting | bytes 1769472 | tf_op args[2]
  6.9 1.2 copy-done.1
  8.1 3.3 %attention.1 = (f32[8,48,640]{2,1,0:T(8,128)S(1)}, bf16[8,48,640]{2,1,0:T(8,128)(2,1)S(1)}) custom-call(s32[1]{0:T(128)} %bitcast.ctx_ref, s32[6,32]{1,0:T(8,128)S(1)} %copy-done.6, bf16[6,128,576]{2,1,0:T(8,128)(2,1)S(1)} %copy-done.1, bf16[6,384,576]{2,1,0:T(8,128)(2,1)S(1)} %copy.17.cache_ref), custom_call_target="tpu_custom_call" | custom-call | tf_op jit(solution)/shard_map/attention/pallas_call | solution.py:101
  11.5 3.3 %collective-permute-start = (bf16[8,48,640]{2,1,0:T(8,128)(2,1)S(1)}, bf16[8,48,640]{2,1,0:T(8,128)(2,1)S(1)}, u32[]{:S(2)}, u32[]{:S(2)}) collective-permute-start(bf16[8,48,640]{2,1,0:T(8,128)(2,1)S(1)} %get-tuple-element.12), channel_id=1, source_target_pairs={{0,16},{16,0},{32,48},{48,32},{64,80},{80,64},{96,112},{112,96},{1... | collective-permute-start | bytes 1474568 | tf_op jit(solution)/shard_map/ppermute | solution.py:376
  14.8 1.5 %collective-permute-done.other_ref = bf16[8,48,640]{2,1,0:T(8,128)(2,1)S(1)} collective-permute-done((bf16[8,48,640]{2,1,0:T(8,128)(2,1)S(1)}, bf16[8,48,640]{2,1,0:T(8,128)(2,1)S(1)}, u32[]{:S(2)}, u32[]{:S(2)}) %collective-permute-start) | collective-permute-done | bytes 491552 | tf_op jit(solution)/shard_map/ppermute | solution.py:376
  17.0 22.2 %all_to_all.25.parts_ref = bf16[8,48,640]{2,1,0:T(8,128)(2,1)S(1)} all-to-all(bf16[8,48,640]{2,1,0:T(8,128)(2,1)S(1)} %pair.1), channel_id=1, replica_groups={{0,32,64,96,128,160,192,224},{16,48,80,112,144,176,208,240},{1,33,65,97..., dimensions={0} | all-to-all | bytes 983040 | tf_op jit(solution)/shard_map/all_to_all | solution.py:381
  39.2 1.3 %values.1 = bf16[16,16,512]{2,1,0:T(8,128)(2,1)} custom-call(bf16[8,48,640]{2,1,0:T(8,128)(2,1)S(1)} %all_to_all.25.parts_ref, bf16[8,512,128]{2,1,0:T(8,128)(2,1)S(1)} %copy-done.2), custom_call_target="tpu_custom_call" | custom-call | tf_op jit(solution)/shard_map/values/pallas_call | solution.py:207
  40.5 6.9 %all-to-all-start.1 = ((bf16[16,16,512]{2,1,0:T(8,128)(2,1)}), bf16[16,16,512]{2,1,0:T(8,128)(2,1)S(1)}, u32[]{:S(2)}, u32[]{:S(2)}) async-start(bf16[16,16,512]{2,1,0:T(8,128)(2,1)} %values.1), calls=%async_computation.1 | async-start | bytes 524288 | tf_op jit(solution)/shard_map/all_to_all | solution.py:383
  48.0 7.0 %all-to-all-done.1.values_ref = bf16[16,16,512]{2,1,0:T(8,128)(2,1)S(1)} async-done(((bf16[16,16,512]{2,1,0:T(8,128)(2,1)}), bf16[16,16,512]{2,1,0:T(8,128)(2,1)S(1)}, u32[]{:S(2)}, u32[]{:S(2)}) %all-to-all-start.1) | async-done | bytes 262176 | tf_op jit(solution)/shard_map/all_to_all | solution.py:383
  55.3 3.4 %collective-permute-start.1 = (bf16[96,448]{1,0:T(8,128)(2,1)S(1)}, bf16[96,448]{1,0:T(8,128)(2,1)S(1)}, u32[]{:S(2)}, u32[]{:S(2)}) collective-permute-start(bf16[96,448]{1,0:T(8,128)(2,1)S(1)} %project.1), channel_id=1, source_target_pairs={{0,16},{16,0},{32,48},{48,32},{64,80},{80,64},{96,112},{112,96},{1... | collective-permute-start | bytes 258056 | tf_op jit(solution)/shard_map/ppermute | solution.py:389
  59.7 1.5 %collective-permute-start.3 = (bf16[96,448]{1,0:T(8,128)(2,1)S(1)}, bf16[96,448]{1,0:T(8,128)(2,1)S(1)}, u32[]{:S(2)}, u32[]{:S(2)}) collective-permute-start(bf16[96,448]{1,0:T(8,128)(2,1)S(1)} %add_convert_fusion.1.own_ref), channel_id=1, source_target_pairs={{0,32},{16,48},{32,64},{48,80},{64,96},{80,112},{96,128},{112,144}... | collective-permute-start | bytes 258056 | tf_op jit(solution)/shard_map/ppermute | solution.py:391
  61.2 2.6 %collective-permute-done.2.up_ref = bf16[96,448]{1,0:T(8,128)(2,1)S(1)} collective-permute-done((bf16[96,448]{1,0:T(8,128)(2,1)S(1)}, bf16[96,448]{1,0:T(8,128)(2,1)S(1)}, u32[]{:S(2)}, u32[]{:S(2)}) %collective-permute-start.2) | collective-permute-done | bytes 86048 | tf_op jit(solution)/shard_map/ppermute | solution.py:390
  63.7 1.3 %collective-permute-done.3.down_ref = bf16[96,448]{1,0:T(8,128)(2,1)S(1)} collective-permute-done((bf16[96,448]{1,0:T(8,128)(2,1)S(1)}, bf16[96,448]{1,0:T(8,128)(2,1)S(1)}, u32[]{:S(2)}, u32[]{:S(2)}) %collective-permute-start.3) | collective-permute-done | bytes 86048 | tf_op jit(solution)/shard_map/ppermute | solution.py:391
  65.2 3.3 %collective-permute-start.5 = (bf16[96,448]{1,0:T(8,128)(2,1)S(1)}, bf16[96,448]{1,0:T(8,128)(2,1)S(1)}, u32[]{:S(2)}, u32[]{:S(2)}) collective-permute-start(bf16[96,448]{1,0:T(8,128)(2,1)S(1)} %get-tuple-element.18), channel_id=1, source_target_pairs={{0,96},{16,112},{32,128},{48,144},{64,160},{80,176},{96,192},{112,... | collective-permute-start | bytes 258056 | tf_op jit(solution)/shard_map/ppermute | solution.py:393
  68.4 2.1 %side.1 = (f32[6,384]{1,0:T(8,128)}, bf16[48,96]{1,0:T(8,128)(2,1)S(1)}, bf16[128,48]{1,0:T(8,128)(2,1)S(1)}, f32[48,128]{1,0:T(8,128)S(1)}) custom-call(s32[1]{0:T(128)} %bitcast.ctx_ref, s32[4,96]{1,0:T(4,128)S(1)} %bitcast.9, f32[4,96]{1,0:T(4,128)S(1)} %bitcast.10, bf16[6,64,128]{2,1,0:T(8,128)(2,1)S(1)} %copy-done.5, f32[6,64]{1,0:T(8,128)S(1)} %copy-done.7, ...), custom_call_target="tpu_custom_call" | custom-call | tf_op jit(solution)/shard_map/side/pallas_call | solution.py:142
  70.9 3.2 %collective-permute-done.5.far_down_ref = bf16[96,448]{1,0:T(8,128)(2,1)S(1)} collective-permute-done((bf16[96,448]{1,0:T(8,128)(2,1)S(1)}, bf16[96,448]{1,0:T(8,128)(2,1)S(1)}, u32[]{:S(2)}, u32[]{:S(2)}) %collective-permute-start.5) | collective-permute-done | bytes 86048 | tf_op jit(solution)/shard_map/ppermute | solution.py:393
  74.1 2.0 %copy-done = bf16[1,448,4096]{2,1,0:T(8,128)(2,1)S(1)} copy-done((bf16[1,448,4096]{2,1,0:T(8,128)(2,1)S(1)}, bf16[1,448,4096]{2,1,0:T(8,128)(2,1)}, u32[]{:S(2)}) %copy-start) | copy-done | bytes 3670040
  76.2 1.9 %expert_in.1 = (bf16[16,56,256]{2,1,0:T(8,128)(2,1)S(1)}, f32[8,448]{1,0:T(8,128)S(1)}) custom-call(s32[1]{0:T(128)} %bitcast.ctx_ref, bf16[96,448]{1,0:T(8,128)(2,1)S(1)} %add_convert_fusion.1.own_ref, bf16[96,448]{1,0:T(8,128)(2,1)S(1)} %collective-permute-done.2.up_ref, bf16[96,448]{1,0:T(8,128)(2,1)S(1)} %collective-permute-done.3.down_ref, ...), custom_call_target="tpu_custom_call" | custom-call | tf_op jit(solution)/shard_map/expert_in/pallas_call | solution.py:278
  78.1 11.2 %all_to_all.26.parts_ref = bf16[16,56,256]{2,1,0:T(8,128)(2,1)S(1)} all-to-all(bf16[16,56,256]{2,1,0:T(8,128)(2,1)S(1)} %get-tuple-element.14), channel_id=1, replica_groups=mesh['ctx'=16,'exp'=16] {'exp'}, dimensions={0} | all-to-all | bytes 917504 | tf_op jit(solution)/shard_map/all_to_all | solution.py:397
  90.1 3.5 %all-to-all-start.3 = ((bf16[16,48,128]{2,1,0:T(8,128)(2,1)}), bf16[16,48,128]{2,1,0:T(8,128)(2,1)S(1)}, u32[]{:S(2)}, u32[]{:S(2)}) async-start(bf16[16,48,128]{2,1,0:T(8,128)(2,1)} %activation.1), calls=%async_computation.3 | async-start | bytes 393216 | tf_op jit(solution)/shard_map/all_to_all | solution.py:398
  93.7 2.8 %copy.19 = bf16[1,2048,448]{2,1,0:T(8,128)(2,1)S(1)} copy(bf16[1,2048,448]{1,2,0:T(8,128)(2,1)} %param.27) | data formatting | bytes 3670016 | tf_op args[13]
  96.5 4.3 %all-to-all-done.3.act_ref = bf16[16,48,128]{2,1,0:T(8,128)(2,1)S(1)} async-done(((bf16[16,48,128]{2,1,0:T(8,128)(2,1)}), bf16[16,48,128]{2,1,0:T(8,128)(2,1)S(1)}, u32[]{:S(2)}, u32[]{:S(2)}) %all-to-all-start.3) | async-done | bytes 196640 | tf_op jit(solution)/shard_map/all_to_all | solution.py:398
  101.4 20.5 %all_to_all.27.parts_ref = bf16[16,16,256]{2,1,0:T(8,128)(2,1)S(1)} all-to-all(bf16[16,16,256]{2,1,0:T(8,128)(2,1)S(1)} %expert_out.1), channel_id=1, replica_groups=mesh['ctx'=16,'exp'=16] {'ctx'}, dimensions={0} | all-to-all | bytes 262144 | tf_op jit(solution)/shard_map/all_to_all | solution.py:400
  (34 shorter events, 5.2 us)
Async XLA Ops:
  0.6 6.3 %copy-start.6 = (s32[6,32]{1,0:T(8,128)S(1)}, s32[6,32]{1,0:T(8,128)}, u32[]{:S(2)}) copy-start(s32[6,32]{1,0:T(8,128)} %blocks_ref.1) | copy-start | bytes 2308
  6.9 1.2 copy-start.1
  8.1 31.0 %copy-start.2 = (bf16[8,512,128]{2,1,0:T(8,128)(2,1)S(1)}, bf16[8,512,128]{2,1,0:T(8,128)(2,1)}, u32[]{:S(2)}) copy-start(bf16[8,512,128]{2,1,0:T(8,128)(2,1)} %w_ref.2) | copy-start | bytes 3145732
  11.5 35.9 %copy-start.11 = (bf16[1024,448]{0,1:T(8,128)(2,1)S(1)}, bf16[1024,448]{0,1:T(8,128)(2,1)}, u32[]{:S(2)}) copy-start(bf16[1024,448]{0,1:T(8,128)(2,1)} %param.21) | copy-start | bytes 2752516
  11.5 4.8 %collective-permute-start = (bf16[8,48,640]{2,1,0:T(8,128)(2,1)S(1)}, bf16[8,48,640]{2,1,0:T(8,128)(2,1)S(1)}, u32[]{:S(2)}, u32[]{:S(2)}) collective-permute-start(bf16[8,48,640]{2,1,0:T(8,128)(2,1)S(1)} %get-tuple-element.12), channel_id=1, source_target_pairs={{0,16},{16,0},{32,48},{48,32},{64,80},{80,64},{96,112},{112,96},{1... | collective-permute-start | bytes 1474568 | tf_op jit(solution)/shard_map/ppermute | solution.py:376
  40.5 28.0 %copy-start.3 = (bf16[6,384,128]{2,1,0:T(8,128)(2,1)S(1)}, bf16[6,384,128]{2,1,0:T(8,128)(2,1)}, u32[]{:S(2)}) copy-start(bf16[6,384,128]{2,1,0:T(8,128)(2,1)} %keys_ref.1) | copy-start | bytes 1769476
  40.5 28.0 %copy-start.5 = (bf16[6,64,128]{2,1,0:T(8,128)(2,1)S(1)}, bf16[6,64,128]{2,1,0:T(8,128)(2,1)}, u32[]{:S(2)}) copy-start(bf16[6,64,128]{2,1,0:T(8,128)(2,1)} %iq_ref.1) | copy-start | bytes 294916
  40.5 28.0 %copy-start.7 = (f32[6,64]{1,0:T(8,128)S(1)}, f32[6,64]{1,0:T(8,128)}, u32[]{:S(2)}) copy-start(f32[6,64]{1,0:T(8,128)} %iw_ref.1) | copy-start | bytes 4612
  40.5 28.0 %copy-start.8 = (s32[96,4]{0,1:T(4,128)S(1)}, s32[96,4]{0,1:T(4,128)}, u32[]{:S(2)}) copy-start(s32[96,4]{0,1:T(4,128)} %param.24) | copy-start | bytes 4612
  40.5 28.0 %copy-start.9 = (f32[96,4]{0,1:T(4,128)S(1)}, f32[96,4]{0,1:T(4,128)}, u32[]{:S(2)}) copy-start(f32[96,4]{0,1:T(4,128)} %param.25) | copy-start | bytes 4612
  40.5 33.6 %copy-start.4 = (bf16[96,448]{1,0:T(8,128)(2,1)S(1)}, bf16[96,448]{1,0:T(8,128)(2,1)}, u32[]{:S(2)}) copy-start(bf16[96,448]{1,0:T(8,128)(2,1)} %hidden_ref.1) | copy-start | bytes 258052
  40.5 33.6 %copy-start.10 = (f32[448]{0:T(512)S(1)}, f32[448]{0:T(512)}, u32[]{:S(2)}) copy-start(f32[448]{0:T(512)} %param.23) | copy-start | bytes 5380
  40.5 14.4 %all-to-all-start.1 = ((bf16[16,16,512]{2,1,0:T(8,128)(2,1)}), bf16[16,16,512]{2,1,0:T(8,128)(2,1)S(1)}, u32[]{:S(2)}, u32[]{:S(2)}) async-start(bf16[16,16,512]{2,1,0:T(8,128)(2,1)} %values.1), calls=%async_computation.1 | async-start | bytes 524288 | tf_op jit(solution)/shard_map/all_to_all | solution.py:383
  55.3 4.3 %collective-permute-start.1 = (bf16[96,448]{1,0:T(8,128)(2,1)S(1)}, bf16[96,448]{1,0:T(8,128)(2,1)S(1)}, u32[]{:S(2)}, u32[]{:S(2)}) collective-permute-start(bf16[96,448]{1,0:T(8,128)(2,1)S(1)} %project.1), channel_id=1, source_target_pairs={{0,16},{16,0},{32,48},{48,32},{64,80},{80,64},{96,112},{112,96},{1... | collective-permute-start | bytes 258056 | tf_op jit(solution)/shard_map/ppermute | solution.py:389
  59.6 4.1 %collective-permute-start.2 = (bf16[96,448]{1,0:T(8,128)(2,1)S(1)}, bf16[96,448]{1,0:T(8,128)(2,1)S(1)}, u32[]{:S(2)}, u32[]{:S(2)}) collective-permute-start(bf16[96,448]{1,0:T(8,128)(2,1)S(1)} %add_convert_fusion.1.own_ref), channel_id=1, source_target_pairs={{0,224},{16,240},{32,0},{48,16},{64,32},{80,48},{96,64},{112,80},{... | collective-permute-start | bytes 258056 | tf_op jit(solution)/shard_map/ppermute | solution.py:390
  59.7 5.3 %collective-permute-start.3 = (bf16[96,448]{1,0:T(8,128)(2,1)S(1)}, bf16[96,448]{1,0:T(8,128)(2,1)S(1)}, u32[]{:S(2)}, u32[]{:S(2)}) collective-permute-start(bf16[96,448]{1,0:T(8,128)(2,1)S(1)} %add_convert_fusion.1.own_ref), channel_id=1, source_target_pairs={{0,32},{16,48},{32,64},{48,80},{64,96},{80,112},{96,128},{112,144}... | collective-permute-start | bytes 258056 | tf_op jit(solution)/shard_map/ppermute | solution.py:391
  65.1 5.8 %collective-permute-start.4 = (bf16[96,448]{1,0:T(8,128)(2,1)S(1)}, bf16[96,448]{1,0:T(8,128)(2,1)S(1)}, u32[]{:S(2)}, u32[]{:S(2)}) collective-permute-start(bf16[96,448]{1,0:T(8,128)(2,1)S(1)} %get-tuple-element.19), channel_id=1, source_target_pairs={{0,160},{16,176},{32,192},{48,208},{64,224},{80,240},{96,0},{112,1... | collective-permute-start | bytes 258056 | tf_op jit(solution)/shard_map/ppermute | solution.py:392
  65.2 8.9 %collective-permute-start.5 = (bf16[96,448]{1,0:T(8,128)(2,1)S(1)}, bf16[96,448]{1,0:T(8,128)(2,1)S(1)}, u32[]{:S(2)}, u32[]{:S(2)}) collective-permute-start(bf16[96,448]{1,0:T(8,128)(2,1)S(1)} %get-tuple-element.18), channel_id=1, source_target_pairs={{0,96},{16,112},{32,128},{48,144},{64,160},{80,176},{96,192},{112,... | collective-permute-start | bytes 258056 | tf_op jit(solution)/shard_map/ppermute | solution.py:393
  74.1 2.0 %copy-start = (bf16[1,448,4096]{2,1,0:T(8,128)(2,1)S(1)}, bf16[1,448,4096]{2,1,0:T(8,128)(2,1)}, u32[]{:S(2)}) copy-start(bf16[1,448,4096]{2,1,0:T(8,128)(2,1)} %param.26) | copy-start | bytes 11010052
  90.1 10.7 %all-to-all-start.3 = ((bf16[16,48,128]{2,1,0:T(8,128)(2,1)}), bf16[16,48,128]{2,1,0:T(8,128)(2,1)S(1)}, u32[]{:S(2)}, u32[]{:S(2)}) async-start(bf16[16,48,128]{2,1,0:T(8,128)(2,1)} %activation.1), calls=%async_computation.3 | async-start | bytes 393216 | tf_op jit(solution)/shard_map/all_to_all | solution.py:398

commit v2 on v1

--- a/solution.py
+++ b/solution.py
@@ -14,6 +14,7 @@
 LAT = 512
 WIDE = 640
 CAP = 48
+FAR = 6
 NEG = -1e30
 SCORE_SCALE = 192.0 ** (-0.5)
 EPS = 1e-06
@@ -22,9 +23,15 @@
 
 VMEM = pl.BlockSpec(memory_space=pltpu.VMEM)
 SMEM = pl.BlockSpec(memory_space=pltpu.SMEM)
-
-
-def params(mb=32):
+HBM = pl.BlockSpec(memory_space=pltpu.HBM)
+ANY = pl.BlockSpec(memory_space=pl.ANY)
+
+
+def in_hbm(x):
+    return pltpu.with_memory_space_constraint(x, pltpu.HBM)
+
+
+def params(mb=8):
     return pltpu.CompilerParams(vmem_limit_bytes=mb * MB)
 
 
@@ -63,7 +70,7 @@
     step = pl.program_id(0)
     ctx = ctx_ref[0]
     core = lax.rem(ctx, 2)
-    tokens = cache_ref.shape[1]
+    tokens = cache_ref.shape[2]
     per = tokens // BLOCK
 
     @pl.when(step == 0)
@@ -81,12 +88,12 @@
     for i in range(2):
         chosen = mask_ref[pl.ds(step * 2 + i, 1), :] > 0.0
         keys = cache_ref[i]
-        scores = dot(query_ref[i], keys, ((1,), (1,))) * SCORE_SCALE
+        scores = dot(query_ref[i], keys, ((0,), (0,))) * SCORE_SCALE
         masked = jnp.where(chosen, scores, NEG)
         peak = jnp.max(masked, axis=1, keepdims=True)
         expo = jnp.where(chosen, jnp.exp(masked - peak), 0.0)
         total = jnp.sum(expo, axis=1, keepdims=True)
-        weighted = dot(expo.astype(bf16), keys[:, :LAT])
+        weighted = dot(expo.astype(bf16), keys[:LAT], ((1,), (1,)))
         wide = jnp.concatenate([weighted, stats_tile(peak, total)], axis=1)
         wide = wide.reshape(8, 2, 8, WIDE)
         mine.append(jnp.where(core == 0, wide[:, 0], wide[:, 1]))
@@ -96,16 +103,16 @@
 
 
 def attention(ctx, blocks, query, cache):
-    rows, heads, width = query.shape
-    tokens = cache.shape[1]
+    rows, width, heads = query.shape
+    tokens = cache.shape[2]
     return pl.pallas_call(
         attention_kernel,
         grid=(rows // 2,),
         in_specs=[
             SMEM,
             pl.BlockSpec((rows, blocks.shape[1]), lambda i: (0, 0)),
-            pl.BlockSpec((2, heads, width), lambda i: (i, 0, 0)),
-            pl.BlockSpec((2, tokens, width), lambda i: (i, 0, 0)),
+            pl.BlockSpec((2, width, heads), lambda i: (i, 0, 0)),
+            pl.BlockSpec((2, width, tokens), lambda i: (i, 0, 0)),
         ],
         out_specs=[pl.BlockSpec((8, 16, WIDE), lambda i: (0, i, 0))] * 2,
         out_shape=[
@@ -113,45 +120,62 @@
             jax.ShapeDtypeStruct((8, rows * 8, WIDE), bf16),
         ],
         scratch_shapes=[pltpu.VMEM((rows, tokens), f32)],
-        compiler_params=params(),
+        compiler_params=params(16),
         name="attention",
-    )(ctx, blocks, query, cache)
-
-
-def side_kernel(ctx_ref, route_ref, gate_ref, iq_ref, iw_ref, keys_ref, score_ref, pick_ref, back_ref, slot_ref):
+    )(ctx, in_hbm(blocks), in_hbm(query), in_hbm(cache))
+
+
+def side_kernel(
+    ctx_ref, route_ref, gate_ref, iq_ref, iw_ref, keys_ref, _,
+    score_ref, send_ref, pick_ref, back_ref, slot_ref,
+):
     rows = iq_ref.shape[0]
     for r in range(rows):
         raw = dot(iq_ref[r], keys_ref[r], ((1,), (1,))) * (iq_ref.shape[2] ** (-0.5))
         score_ref[r : r + 1, :] = dot(iw_ref[r : r + 1, :], jnp.maximum(raw, 0.0), precision=HIGH)
     n = route_ref.shape[1]
-    is_mine = route_ref[...] == ctx_ref[0]
-    hit = jnp.max(jnp.where(is_mine, 1.0, 0.0), axis=0, keepdims=True)
-    gate = jnp.sum(jnp.where(is_mine, gate_ref[...], 0.0), axis=0, keepdims=True)
+    ctx = ctx_ref[0]
+    n_ctx = n // 6
+    names = route_ref[...]
+    experts = [ctx, lax.rem(ctx + n_ctx - FAR, n_ctx), lax.rem(ctx + FAR, n_ctx)]
+    hit = [jnp.max(jnp.where(names == g, 1.0, 0.0), axis=0, keepdims=True) for g in experts]
     upto = jnp.where(iota((n, n), 0) <= iota((n, n), 1), 1.0, 0.0).astype(bf16)
-    slot = dot(jnp.broadcast_to(hit, (8, n)).astype(bf16), upto)[0:1].astype(jnp.int32) - 1
-    pick = jnp.where((iota((CAP, n), 0) == slot) & (hit > 0.0), 1.0, 0.0)
-    pick_ref[...] = pick.astype(bf16)
+    hits = jnp.concatenate(hit + [jnp.zeros((8 - len(hit), n), f32)], axis=0)
+    slots = dot(hits.astype(bf16), upto).astype(jnp.int32) - 1
+    line, col = iota((8, n), 0), iota((8, n), 1)
+    picks = []
+    for j, g in enumerate(experts):
+        picks.append(jnp.where((iota((CAP, n), 0) == slots[j : j + 1]) & (hit[j] > 0.0), 1.0, 0.0))
+        own = jnp.where((col == 6 * g + line) & (line < 6), 1.0, 0.0)
+        both = jnp.concatenate([picks[j], own], axis=0).astype(bf16)
+        if j == 0:
+            pick_ref[...] = both
+        else:
+            send_ref[j - 1] = both
+    gate = jnp.sum(jnp.where(names == ctx, gate_ref[...], 0.0), axis=0, keepdims=True)
     row, col = iota((128, n), 0), iota((128, n), 1)
     spread = (row // 8 * 6 + row % 8 == col) & (row % 8 < 6)
     spread = jnp.where(spread, 1.0, 0.0).astype(bf16)
-    back_ref[...] = dot(spread, pick.astype(bf16), ((1,), (1,))).astype(bf16)
-    slot_ref[...] = jnp.broadcast_to(jnp.sum(pick * gate, axis=1, keepdims=True), (CAP, 128))
-
-
-def side(ctx, route, gate, iq, iw, keys):
+    back_ref[...] = dot(spread, picks[0].astype(bf16), ((1,), (1,))).astype(bf16)
+    slot_ref[...] = jnp.broadcast_to(jnp.sum(picks[0] * gate, axis=1, keepdims=True), (CAP, 128))
+
+
+def side(ctx, route, gate, iq, iw, keys, after):
+    n = route.shape[1]
     return pl.pallas_call(
         side_kernel,
-        in_specs=[SMEM] + [VMEM] * 5,
-        out_specs=[VMEM] * 4,
+        in_specs=[SMEM] + [VMEM] * 5 + [ANY],
+        out_specs=[VMEM] * 5,
         out_shape=[
             jax.ShapeDtypeStruct((iq.shape[0], keys.shape[1]), f32),
-            jax.ShapeDtypeStruct((CAP, route.shape[1]), bf16),
+            jax.ShapeDtypeStruct((2, CAP + 8, n), bf16),
+            jax.ShapeDtypeStruct((CAP + 8, n), bf16),
             jax.ShapeDtypeStruct((128, CAP), bf16),
             jax.ShapeDtypeStruct((CAP, 128), f32),
         ],
         compiler_params=params(),
         name="side",
-    )(ctx, route, gate, iq, iw, keys)
+    )(ctx, route, gate, iq, iw, keys, after)
 
 
 def pair_kernel(mine_ref, other_ref, out_ref):
@@ -214,88 +238,108 @@
     )(parts, w_uv)
 
 
-def project_kernel(values_ref, w_ref, out_ref, acc_ref):
+def project_kernel(values_ref, w_ref, _, out_ref, acc_ref):
     x = values_ref[...].astype(f32)
     n = x.shape[0]
     low = x[:, :8].reshape(n * 8, 512).astype(bf16)
     high = x[:, 8:].reshape(n * 8, 512).astype(bf16)
-    acc = dot(low, w_ref[:512, :]) + dot(high, w_ref[512:, :])
+    acc = dot(low, w_ref[:, :512], ((1,), (1,))) + dot(high, w_ref[:, 512:], ((1,), (1,)))
     for e in range(n):
         acc_ref[6 * e : 6 * e + 6, :] = acc[8 * e : 8 * e + 6, :]
     out_ref[...] = acc_ref[...].astype(bf16)
 
 
-def project(vals, w_o):
-    shape = (vals.shape[0] * 6, w_o.shape[1])
+def project(vals, w_o, after):
+    shape = (vals.shape[0] * 6, w_o.shape[0])
     return pl.pallas_call(
         project_kernel,
-        in_specs=[VMEM] * 2,
+        in_specs=[VMEM] * 2 + [ANY],
         out_specs=VMEM,
         out_shape=jax.ShapeDtypeStruct(shape, bf16),
         scratch_shapes=[pltpu.VMEM(shape, f32)],
         compiler_params=params(),
         name="project",
-    )(vals, w_o)
-
-
-def expert_in_kernel(
-    ctx_ref, own_ref, up_ref, down_ref, far_up_ref, far_down_ref, hidden_ref, gain_ref, pick_ref,
-    gate_w_ref, up_w_ref, out_ref, keep_ref, rows_ref, squares_ref,
-):
-    @pl.when(pl.program_id(0) == 0)
-    def _():
-        attn = own_ref[...].astype(f32) + up_ref[...].astype(f32) + down_ref[...].astype(f32)
-        attn = attn + far_up_ref[...].astype(f32) + far_down_ref[...].astype(f32)
-        resid = (hidden_ref[...].astype(f32) + attn).astype(bf16)
-        resid32 = resid.astype(f32)
-        scaled = (resid32 * gain_ref[...]).astype(bf16)
-        rows_ref[...] = dot(pick_ref[...], scaled).astype(bf16)
-        picked = dot(pick_ref[...], resid)
-        squares = dot(jnp.ones((8, picked.shape[1]), f32), picked * picked, ((1,), (1,)), HIGH)
-        hi, mid, low = split3(squares)
-        line = iota(squares.shape, 0)
-        parts = jnp.where(line == 0, hi, jnp.where(line == 1, mid, jnp.where(line == 2, low, 0.0)))
-        squares_ref[...] = jnp.concatenate([parts, jnp.zeros((8, 256 - CAP), f32)], axis=1)
-        n = resid.shape[0]
-        own_row = jnp.where(iota((8, n), 1) == ctx_ref[0] * 6 + iota((8, n), 0), 1.0, 0.0)
-        keep_ref[...] = dot(own_row.astype(bf16), resid)
-
-    rows = rows_ref[...]
-    gate = dot(rows, gate_w_ref[...])
-    up = dot(rows, up_w_ref[...])
-    squares = squares_ref[...]
-    for e in range(out_ref.shape[0]):
-        cols = slice(128 * e, 128 * e + 128)
-        both = jnp.concatenate([gate[:, cols], up[:, cols]], axis=1)
-        out_ref[e] = jnp.concatenate([both, squares], axis=0).astype(bf16)
-
-
-def expert_in(ctx, sums, hidden, gain, pick, w_in, n_exp):
-    rows, width = hidden.shape
-    steps = 4
-    cols = w_in.shape[1] // 2 // steps
-    whole = lambda a: pl.BlockSpec(a.shape, lambda i: (0,) * a.ndim)
+    )(vals, w_o, after)
+
+
+def fold_kernel(own_ref, above_ref, below_ref, send_ref, up_ref, down_ref):
+    two = own_ref[...].astype(f32) + above_ref[...].astype(f32)
+    three = (two + below_ref[...].astype(f32)).astype(bf16)
+    up_ref[...] = dot(send_ref[0], three).astype(bf16)
+    down_ref[...] = dot(send_ref[1], two.astype(bf16)).astype(bf16)
+
+
+def fold(own, above, below, send):
+    shape = jax.ShapeDtypeStruct((send.shape[1], own.shape[1]), bf16)
+    return pl.pallas_call(
+        fold_kernel,
+        in_specs=[VMEM] * 4,
+        out_specs=[VMEM] * 2,
+        out_shape=[shape, shape],
+        compiler_params=params(),
+        name="fold",
+    )(own, above, below, send)
+
+
+def base_kernel(own_ref, above_ref, below_ref, hidden_ref, pick_ref, w_hbm, out_ref, w_ref, sem):
+    load = pltpu.make_async_copy(w_hbm, w_ref, sem)
+    load.start()
+    pick = pick_ref[...]
+    near = dot(pick, own_ref[...]) + dot(pick, above_ref[...]) + dot(pick, below_ref[...])
+    out_ref[...] = dot(pick, hidden_ref[...]) + near
+    load.wait()
+
+
+def base(own, above, below, hidden, pick, w_in):
+    return pl.pallas_call(
+        base_kernel,
+        in_specs=[VMEM] * 5 + [HBM],
+        out_specs=[VMEM] * 2,
+        out_shape=[
+            jax.ShapeDtypeStruct((pick.shape[0], own.shape[1]), f32),
+            jax.ShapeDtypeStruct(w_in.shape, bf16),
+        ],
+        scratch_shapes=[pltpu.SemaphoreType.DMA],
+        compiler_params=params(),
+        name="base",
+    )(own, above, below, hidden, pick, in_hbm(w_in))
+
+
+def expert_in_kernel(near_ref, far_up_ref, far_down_ref, gain_ref, w_ref, out_ref, keep_ref):
+    n = out_ref.shape[0]
+    half = w_ref.shape[1] // 2
+    attn = near_ref[...] + far_up_ref[...].astype(f32) + far_down_ref[...].astype(f32)
+    resid32 = attn.astype(bf16).astype(f32)
+    keep_ref[...] = resid32[CAP:]
+    picked = resid32[:CAP]
+    rows = (picked * gain_ref[...]).astype(bf16)
+    squares = dot(jnp.ones((8, picked.shape[1]), f32), picked * picked, ((1,), (1,)), HIGH)
+    hi, mid, low = split3(squares)
+    line = iota(squares.shape, 0)
+    parts = jnp.where(line == 0, hi, jnp.where(line == 1, mid, jnp.where(line == 2, low, 0.0)))
+    parts = jnp.concatenate([parts, jnp.zeros((8, 256 - CAP), f32)], axis=1)
+    for e in range(0, n, 2):
+        gate = dot(rows, w_ref[:, 128 * e : 128 * e + 256])
+        up = dot(rows, w_ref[:, half + 128 * e : half + 128 * e + 256])
+        for i in range(2):
+            here = slice(128 * i, 128 * i + 128)
+            both = jnp.concatenate([gate[:, here], up[:, here]], axis=1)
+            out_ref[e + i] = jnp.concatenate([both, parts], axis=0).astype(bf16)
+
+
+def expert_in(near, far_up, far_down, gain, w_in, n_exp):
+    width = near.shape[1]
     return pl.pallas_call(
         expert_in_kernel,
-        grid=(steps,),
-        in_specs=[SMEM]
-        + [whole(a) for a in (*sums, hidden, gain, pick)]
-        + [
-            pl.BlockSpec((width, cols), lambda i: (0, i)),
-            pl.BlockSpec((width, cols), lambda i: (0, i + steps)),
-        ],
-        out_specs=[
-            pl.BlockSpec((n_exp // steps, CAP + 8, 256), lambda i: (i, 0, 0)),
-            pl.BlockSpec((8, width), lambda i: (0, 0)),
-        ],
+        in_specs=[VMEM] * 5,
+        out_specs=[VMEM] * 2,
         out_shape=[
             jax.ShapeDtypeStruct((n_exp, CAP + 8, 256), bf16),
             jax.ShapeDtypeStruct((8, width), f32),
         ],
-        scratch_shapes=[pltpu.VMEM((CAP, width), bf16), pltpu.VMEM((8, 256), f32)],
         compiler_params=params(),
         name="expert_in",
-    )(ctx, *sums, hidden, gain, pick, w_in, w_in)
+    )(near, far_up, far_down, gain, w_in)
 
 
 def act_kernel(parts_ref, out_ref):
@@ -323,7 +367,7 @@
 
 def expert_out_kernel(act_ref, w_ref, slot_ref, back_ref, out_ref):
     act = jnp.concatenate([act_ref[e] for e in range(act_ref.shape[0])], axis=1)
-    out = (dot(act, w_ref[...]) * slot_ref[:, 0:1]).astype(bf16)
+    out = (dot(act, w_ref[...], ((1,), (1,))) * slot_ref[:, 0:1]).astype(bf16)
     back = dot(back_ref[...], out)
     n = out_ref.shape[0]
     low = back[:, :256].reshape(n, 8, 256)
@@ -367,36 +411,35 @@
     n_z = n_ctx // 2
     ctx = lax.axis_index("ctx").astype(jnp.int32).reshape(1)
     other_core = [(i, i ^ 1) for i in range(n_ctx)]
+    def along_z(shift):
+        return [(i, (i + shift) % n_ctx) for i in range(n_ctx)]
+
     z_groups = [[2 * z + k for z in range(n_z)] for k in range(2)]
 
-    def along_z(shift):
-        return [(i, (i + 2 * shift) % n_ctx) for i in range(n_ctx)]
-
-    mine, other = attention(ctx, chosen_blocks, lat_query, cache)
+    mine, other = attention(
+        ctx, chosen_blocks, jnp.swapaxes(lat_query, 1, 2), jnp.swapaxes(cache, 1, 2)
+    )
     other = lax.ppermute(other, "ctx", other_core)
-    index_scores, pick, back, slot = side(
-        ctx, route.T, route_weight.T, idx_query, idx_weight, idx_keys
-    )
     parts = pair(mine, other)
     parts = lax.all_to_all(parts, "ctx", 0, 0, axis_index_groups=z_groups)
     vals = values(parts, w_uv, n_exp)
+    index_scores, send, pick, back, slot = side(
+        ctx, route.T, route_weight.T, idx_query, idx_weight, idx_keys, vals
+    )
     vals = lax.all_to_all(vals, "exp", 0, 0)
-    part = project(vals, w_o)
-
-    def add(*terms):
-        return sum(t.astype(f32) for t in terms).astype(bf16)
-
-    own = add(part, lax.ppermute(part, "ctx", other_core))
-    above = lax.ppermute(own, "ctx", along_z(-1))
-    below = lax.ppermute(own, "ctx", along_z(1))
-    far_above = lax.ppermute(add(own, above, below), "ctx", along_z(-3))
-    far_below = lax.ppermute(add(own, above), "ctx", along_z(3))
-    sums = (own, above, below, far_above, far_below)
-
-    terms, keep = expert_in(ctx, sums, hidden_in, norm_gain.reshape(1, -1), pick, w_in[0], n_exp)
+    part = project(vals, w_o.T, send)
+    own = part.astype(f32) + lax.ppermute(part, "ctx", other_core).astype(f32)
+    own = own.astype(bf16)
+    above = lax.ppermute(own, "ctx", along_z(-2))
+    below = lax.ppermute(own, "ctx", along_z(2))
+    up, down = fold(own, above, below, send)
+    far_up = lax.ppermute(up, "ctx", along_z(-FAR))
+    far_down = lax.ppermute(down, "ctx", along_z(FAR))
+    near, w_gate_up = base(own, above, below, hidden_in, pick, w_in[0])
+    terms, keep = expert_in(near, far_up, far_down, norm_gain.reshape(1, -1), w_gate_up, n_exp)
     terms = lax.all_to_all(terms, "exp", 0, 0)
     act = lax.all_to_all(activation(terms), "exp", 0, 0)
-    outs = expert_out(act, w_down[0], slot, back, n_ctx)
+    outs = expert_out(act, w_down[0].T, slot, back, n_ctx)
     outs = lax.all_to_all(outs, "ctx", 0, 0)
     return index_scores, last(outs, keep)
 

time: 123 us -> 110 us (0.89)
  local copies, waits for them, and re-layouts: 12.9 us -> 0.05 us
  blocking collectives: 53.9 us -> 64 us
  waiting for transfers between devices: 21.2 us -> 11.2 us
  starting transfers between devices: 22 us -> 19.6 us
  Pallas kernels: 11.7 us -> 13.8 us
    unnamed x28 -> x20, local copies, waits for them, and re-layouts: 12.9 us -> 0.05 us
    all_to_all x0 -> x1, blocking collectives: none -> 9.84 us  [local(): act = lax.all_to_all(activation(terms), 'exp', 0, 0)]
    all_to_all x1 -> x0, waiting for transfers between devices: 4.34 us -> none  [local(): act = lax.all_to_all(activation(terms), 'exp', 0, 0)]
    ppermute x5, waiting for transfers between devices: 8.42 us -> 4.28 us  [the longest x1 2.56 us: local(): below = lax.ppermute(own, 'ctx', along_z(2))]
    all_to_all x1 -> x0, starting transfers between devices: 3.52 us -> none  [local(): act = lax.all_to_all(activation(terms), 'exp', 0, 0)]
    all_to_all x1, waiting for transfers between devices: 7 us -> 5.44 us  [local(): vals = lax.all_to_all(vals, 'exp', 0, 0)]
    pallas_call x1, Pallas kernels: 3.35 us -> 4.73 us  [attention(): pl.pallas_call(attention_kernel, grid=(rows // 2,), in_specs=[SMEM, pl.Bl...]
    pallas_call x3 -> x5, Pallas kernels: 4.31 us -> 5.46 us  [the longest x1 2.06 us: base(): pl.pallas_call(base_kernel, in_specs=[VMEM] * 5 + [HBM], out_specs=[VMEM]...]
  transfers between devices with their start and end apart: 8 -> 7, of which waited for: 8 -> 6; matrix products, arithmetic and copies ran while one was open for 3% -> 0% of each run, Pallas kernels for 2% -> 4%
where the time goes in v2:
time: 110 us
  blocking collectives  64 us (58%)
  starting transfers between devices  19.6 us (18%)
  Pallas kernels  13.8 us (13%)
  waiting for transfers between devices  11.2 us (10%)
    all_to_all x1, blocking collectives, local(): parts = lax.all_to_all(parts, 'ctx', 0, 0, axis_index_groups=z_groups)  22.2 us
    all_to_all x1, blocking collectives, local(): outs = lax.all_to_all(outs, 'ctx', 0, 0)  20.7 us
    all_to_all x1, blocking collectives, local(): terms = lax.all_to_all(terms, 'exp', 0, 0)  11.2 us
    all_to_all x1, blocking collectives, local(): act = lax.all_to_all(activation(terms), 'exp', 0, 0)  9.84 us
    all_to_all x1, starting transfers between devices, local(): vals = lax.all_to_all(vals, 'exp', 0, 0)  6.88 us
    all_to_all x1, waiting for transfers between devices, local(): vals = lax.all_to_all(vals, 'exp', 0, 0)  5.44 us
    pallas_call x1, Pallas kernels, attention(): pl.pallas_call(attention_kernel, grid=(rows // 2,), in_specs=[SMEM, pl.Bl...  4.73 us
    ppermute x1, starting transfers between devices, local(): own = part.astype(f32) + lax.ppermute(part, 'ctx', other_core).astype(f32)  3.35 us
  transfers between devices with their start and end apart: 7, of which 6 were waited for; matrix products, arithmetic and copies ran while one was open for 0% of the time, Pallas kernels for 4%

profile of v2, /device:TPU:1, one launch (start us, length us, event | category | flops | bytes accessed | tf_op | source)
XLA Modules:
  0.0 109.5 jit_solution(10584586675823854127)
XLA Ops:
  0.7 4.7 %attention.1 = (f32[8,48,640]{2,1,0:T(8,128)S(1)}, bf16[8,48,640]{2,1,0:T(8,128)(2,1)S(1)}) custom-call(s32[1]{0:T(128)} %bitcast.ctx_ref, s32[6,32]{1,0:T(8,128)} %blocks_ref.1, bf16[6,576,128]{2,1,0:T(8,128)(2,1)} %bitcast.18, bf16[6,576,384]{2,1,0:T(8,128)(2,1)} %bitcast.17), custom_call_target="tpu_custom_call" | custom-call | tf_op jit(solution)/shard_map/attention/pallas_call | solution.py:108
  5.4 3.3 %collective-permute-start = (bf16[8,48,640]{2,1,0:T(8,128)(2,1)S(1)}, bf16[8,48,640]{2,1,0:T(8,128)(2,1)S(1)}, u32[]{:S(2)}, u32[]{:S(2)}) collective-permute-start(bf16[8,48,640]{2,1,0:T(8,128)(2,1)S(1)} %get-tuple-element.16), channel_id=1, source_target_pairs={{0,16},{16,0},{32,48},{48,32},{64,80},{80,64},{96,112},{112,96},{1... | collective-permute-start | bytes 1474568 | tf_op jit(solution)/shard_map/ppermute | solution.py:422
  8.8 1.5 %collective-permute-done.other_ref = bf16[8,48,640]{2,1,0:T(8,128)(2,1)S(1)} collective-permute-done((bf16[8,48,640]{2,1,0:T(8,128)(2,1)S(1)}, bf16[8,48,640]{2,1,0:T(8,128)(2,1)S(1)}, u32[]{:S(2)}, u32[]{:S(2)}) %collective-permute-start) | collective-permute-done | bytes 491552 | tf_op jit(solution)/shard_map/ppermute | solution.py:422
  10.3 0.7 pair.1
  11.0 22.2 %all_to_all.25.parts_ref = bf16[8,48,640]{2,1,0:T(8,128)(2,1)S(1)} all-to-all(bf16[8,48,640]{2,1,0:T(8,128)(2,1)S(1)} %pair.1), channel_id=1, replica_groups={{0,32,64,96,128,160,192,224},{16,48,80,112,144,176,208,240},{1,33,65,97..., dimensions={0} | all-to-all | bytes 983040 | tf_op jit(solution)/shard_map/all_to_all | solution.py:424
  33.1 1.3 %values.1._ = bf16[16,16,512]{2,1,0:T(8,128)(2,1)} custom-call(bf16[8,48,640]{2,1,0:T(8,128)(2,1)S(1)} %all_to_all.25.parts_ref, bf16[8,512,128]{2,1,0:T(8,128)(2,1)S(1)} %copy-done.1), custom_call_target="tpu_custom_call" | custom-call | tf_op jit(solution)/shard_map/values/pallas_call | solution.py:231
  34.4 6.9 %all-to-all-start.1 = ((bf16[16,16,512]{2,1,0:T(8,128)(2,1)}), bf16[16,16,512]{2,1,0:T(8,128)(2,1)S(1)}, u32[]{:S(2)}, u32[]{:S(2)}) async-start(bf16[16,16,512]{2,1,0:T(8,128)(2,1)} %values.1._), calls=%async_computation.1 | async-start | bytes 524288 | tf_op jit(solution)/shard_map/all_to_all | solution.py:429
  41.4 2.0 %side.1 = (f32[6,384]{1,0:T(8,128)}, bf16[2,56,96]{2,1,0:T(8,128)(2,1)S(1)}, bf16[56,96]{1,0:T(8,128)(2,1)S(1)}, bf16[128,48]{1,0:T(8,128)(2,1)S(1)}, f32[48,128]{1,0:T(8,128)S(1)}) custom-call(s32[1]{0:T(128)} %bitcast.ctx_ref, s32[4,96]{1,0:T(4,128)S(1)} %bitcast.14, f32[4,96]{1,0:T(4,128)S(1)} %bitcast.15, bf16[6,64,128]{2,1,0:T(8,128)(2,1)S(1)} %copy-done.4, ...), custom_call_target="tpu_custom_call" | custom-call | tf_op jit(solution)/shard_map/side/pallas_call | solution.py:165
  43.4 5.4 %all-to-all-done.1.values_ref = bf16[16,16,512]{2,1,0:T(8,128)(2,1)S(1)} async-done(((bf16[16,16,512]{2,1,0:T(8,128)(2,1)}), bf16[16,16,512]{2,1,0:T(8,128)(2,1)S(1)}, u32[]{:S(2)}, u32[]{:S(2)}) %all-to-all-start.1) | async-done | bytes 262176 | tf_op jit(solution)/shard_map/all_to_all | solution.py:429
  48.9 0.4 project.1
  49.3 3.4 %collective-permute-start.1 = (bf16[96,448]{1,0:T(8,128)(2,1)S(1)}, bf16[96,448]{1,0:T(8,128)(2,1)S(1)}, u32[]{:S(2)}, u32[]{:S(2)}) collective-permute-start(bf16[96,448]{1,0:T(8,128)(2,1)S(1)} %project.1), channel_id=1, source_target_pairs={{0,16},{16,0},{32,48},{48,32},{64,80},{80,64},{96,112},{112,96},{1... | collective-permute-start | bytes 258056 | tf_op jit(solution)/shard_map/ppermute | solution.py:431
  52.7 0.9 collective-permute-done.1
  53.6 0.4 collective-permute-start.3
  54.0 2.4 %collective-permute-start.2 = (bf16[96,448]{1,0:T(8,128)(2,1)S(1)}, bf16[96,448]{1,0:T(8,128)(2,1)S(1)}, u32[]{:S(2)}, u32[]{:S(2)}) collective-permute-start(bf16[96,448]{1,0:T(8,128)(2,1)S(1)} %add_convert_fusion.own_ref), channel_id=1, source_target_pairs={{0,224},{16,240},{32,0},{48,16},{64,32},{80,48},{96,64},{112,80},{... | collective-permute-start | bytes 258056 | tf_op jit(solution)/shard_map/ppermute | solution.py:433
  56.4 2.6 %collective-permute-done.3.below_ref = bf16[96,448]{1,0:T(8,128)(2,1)S(1)} collective-permute-done((bf16[96,448]{1,0:T(8,128)(2,1)S(1)}, bf16[96,448]{1,0:T(8,128)(2,1)S(1)}, u32[]{:S(2)}, u32[]{:S(2)}) %collective-permute-start.3) | collective-permute-done | bytes 86048 | tf_op jit(solution)/shard_map/ppermute | solution.py:434
  59.3 3.3 %collective-permute-start.5 = (bf16[56,448]{1,0:T(8,128)(2,1)S(1)}, bf16[56,448]{1,0:T(8,128)(2,1)S(1)}, u32[]{:S(2)}, u32[]{:S(2)}) collective-permute-start(bf16[56,448]{1,0:T(8,128)(2,1)S(1)} %get-tuple-element.22), channel_id=1, source_target_pairs={{0,96},{16,112},{32,128},{48,144},{64,160},{80,176},{96,192},{112,... | collective-permute-start | bytes 150536 | tf_op jit(solution)/shard_map/ppermute | solution.py:437
  62.5 2.1 %base.1 = (f32[56,448]{1,0:T(8,128)S(1)}, bf16[448,4096]{1,0:T(8,128)(2,1)S(1)}) custom-call(bf16[96,448]{1,0:T(8,128)(2,1)S(1)} %add_convert_fusion.own_ref, bf16[96,448]{1,0:T(8,128)(2,1)S(1)} %collective-permute-done.2.above_ref, bf16[96,448]{1,0:T(8,128)(2,1)S(1)} %collective-permute-done.3.below_ref, bf16[96,448]{1,0:T(8,128)(2,1)S(1)} %copy-done.5, ...), custom_call_target="tpu_custom_call" | custom-call | tf_op jit(solution)/shard_map/base/pallas_call | solution.py:294
  64.6 0.5 collective-permute-done.4.far_up_ref
  65.4 0.7 expert_in.1
  66.1 11.2 %all_to_all.26.parts_ref = bf16[16,56,256]{2,1,0:T(8,128)(2,1)S(1)} all-to-all(bf16[16,56,256]{2,1,0:T(8,128)(2,1)S(1)} %get-tuple-element.24), channel_id=1, replica_groups=mesh['ctx'=16,'exp'=16] {'exp'}, dimensions={0} | all-to-all | bytes 917504 | tf_op jit(solution)/shard_map/all_to_all | solution.py:440
  77.5 9.8 %all_to_all.27.act_ref = bf16[16,48,128]{2,1,0:T(8,128)(2,1)S(1)} all-to-all(bf16[16,48,128]{2,1,0:T(8,128)(2,1)S(1)} %activation.1), channel_id=1, replica_groups=mesh['ctx'=16,'exp'=16] {'exp'}, dimensions={0} | all-to-all | bytes 393216 | tf_op jit(solution)/shard_map/all_to_all | solution.py:441
  87.3 0.9 expert_out.1
  88.2 20.7 %all_to_all.28.parts_ref = bf16[16,16,256]{2,1,0:T(8,128)(2,1)S(1)} all-to-all(bf16[16,16,256]{2,1,0:T(8,128)(2,1)S(1)} %expert_out.1), channel_id=1, replica_groups=mesh['ctx'=16,'exp'=16] {'ctx'}, dimensions={0} | all-to-all | bytes 262144 | tf_op jit(solution)/shard_map/all_to_all | solution.py:443
  108.9 0.6 last.1
  (26 shorter events, 0.7 us)
Async XLA Ops:
  0.6 32.5 %copy-start.1 = (bf16[8,512,128]{2,1,0:T(8,128)(2,1)S(1)}, bf16[8,512,128]{2,1,0:T(8,128)(2,1)}, u32[]{:S(2)}) copy-start(bf16[8,512,128]{2,1,0:T(8,128)(2,1)} %w_ref.1) | copy-start | bytes 3145732
  0.6 40.7 %copy-start.3 = (bf16[6,384,128]{2,1,0:T(8,128)(2,1)S(1)}, bf16[6,384,128]{2,1,0:T(8,128)(2,1)}, u32[]{:S(2)}) copy-start(bf16[6,384,128]{2,1,0:T(8,128)(2,1)} %keys_ref.1) | copy-start | bytes 1769476
  0.7 40.7 %copy-start.4 = (bf16[6,64,128]{2,1,0:T(8,128)(2,1)S(1)}, bf16[6,64,128]{2,1,0:T(8,128)(2,1)}, u32[]{:S(2)}) copy-start(bf16[6,64,128]{2,1,0:T(8,128)(2,1)} %iq_ref.1) | copy-start | bytes 294916
  0.7 40.7 %copy-start.6 = (f32[6,64]{1,0:T(8,128)S(1)}, f32[6,64]{1,0:T(8,128)}, u32[]{:S(2)}) copy-start(f32[6,64]{1,0:T(8,128)} %iw_ref.1) | copy-start | bytes 4612
  0.7 40.7 %copy-start.8 = (s32[96,4]{0,1:T(4,128)S(1)}, s32[96,4]{0,1:T(4,128)}, u32[]{:S(2)}) copy-start(s32[96,4]{0,1:T(4,128)} %param.24) | copy-start | bytes 4612
  0.7 40.7 %copy-start.9 = (f32[96,4]{0,1:T(4,128)S(1)}, f32[96,4]{0,1:T(4,128)}, u32[]{:S(2)}) copy-start(f32[96,4]{0,1:T(4,128)} %param.25) | copy-start | bytes 4612
  5.4 43.4 %copy-start.2 = (bf16[1024,448]{0,1:T(8,128)(2,1)S(1)}, bf16[1024,448]{0,1:T(8,128)(2,1)}, u32[]{:S(2)}) copy-start(bf16[1024,448]{0,1:T(8,128)(2,1)} %param.21) | copy-start | bytes 2752516
  5.4 4.8 %collective-permute-start = (bf16[8,48,640]{2,1,0:T(8,128)(2,1)S(1)}, bf16[8,48,640]{2,1,0:T(8,128)(2,1)S(1)}, u32[]{:S(2)}, u32[]{:S(2)}) collective-permute-start(bf16[8,48,640]{2,1,0:T(8,128)(2,1)S(1)} %get-tuple-element.16), channel_id=1, source_target_pairs={{0,16},{16,0},{32,48},{48,32},{64,80},{80,64},{96,112},{112,96},{1... | collective-permute-start | bytes 1474568 | tf_op jit(solution)/shard_map/ppermute | solution.py:422
  10.3 52.3 %copy-start.5 = (bf16[96,448]{1,0:T(8,128)(2,1)S(1)}, bf16[96,448]{1,0:T(8,128)(2,1)}, u32[]{:S(2)}) copy-start(bf16[96,448]{1,0:T(8,128)(2,1)} %hidden_ref.1) | copy-start | bytes 258052
  34.4 30.9 %copy-start.7 = (f32[448]{0:T(512)S(1)}, f32[448]{0:T(512)}, u32[]{:S(2)}) copy-start(f32[448]{0:T(512)} %param.23) | copy-start | bytes 5380
  34.4 14.4 %all-to-all-start.1 = ((bf16[16,16,512]{2,1,0:T(8,128)(2,1)}), bf16[16,16,512]{2,1,0:T(8,128)(2,1)S(1)}, u32[]{:S(2)}, u32[]{:S(2)}) async-start(bf16[16,16,512]{2,1,0:T(8,128)(2,1)} %values.1._), calls=%async_computation.1 | async-start | bytes 524288 | tf_op jit(solution)/shard_map/all_to_all | solution.py:429
  49.3 4.3 %collective-permute-start.1 = (bf16[96,448]{1,0:T(8,128)(2,1)S(1)}, bf16[96,448]{1,0:T(8,128)(2,1)S(1)}, u32[]{:S(2)}, u32[]{:S(2)}) collective-permute-start(bf16[96,448]{1,0:T(8,128)(2,1)S(1)} %project.1), channel_id=1, source_target_pairs={{0,16},{16,0},{32,48},{48,32},{64,80},{80,64},{96,112},{112,96},{1... | collective-permute-start | bytes 258056 | tf_op jit(solution)/shard_map/ppermute | solution.py:431
  53.6 5.3 %collective-permute-start.3 = (bf16[96,448]{1,0:T(8,128)(2,1)S(1)}, bf16[96,448]{1,0:T(8,128)(2,1)S(1)}, u32[]{:S(2)}, u32[]{:S(2)}) collective-permute-start(bf16[96,448]{1,0:T(8,128)(2,1)S(1)} %add_convert_fusion.own_ref), channel_id=1, source_target_pairs={{0,32},{16,48},{32,64},{48,80},{64,96},{80,112},{96,128},{112,144}... | collective-permute-start | bytes 258056 | tf_op jit(solution)/shard_map/ppermute | solution.py:434
  54.0 5.0 %collective-permute-start.2 = (bf16[96,448]{1,0:T(8,128)(2,1)S(1)}, bf16[96,448]{1,0:T(8,128)(2,1)S(1)}, u32[]{:S(2)}, u32[]{:S(2)}) collective-permute-start(bf16[96,448]{1,0:T(8,128)(2,1)S(1)} %add_convert_fusion.own_ref), channel_id=1, source_target_pairs={{0,224},{16,240},{32,0},{48,16},{64,32},{80,48},{96,64},{112,80},{... | collective-permute-start | bytes 258056 | tf_op jit(solution)/shard_map/ppermute | solution.py:433
  59.2 6.0 %collective-permute-start.4 = (bf16[56,448]{1,0:T(8,128)(2,1)S(1)}, bf16[56,448]{1,0:T(8,128)(2,1)S(1)}, u32[]{:S(2)}, u32[]{:S(2)}) collective-permute-start(bf16[56,448]{1,0:T(8,128)(2,1)S(1)} %get-tuple-element.21), channel_id=1, source_target_pairs={{0,160},{16,176},{32,192},{48,208},{64,224},{80,240},{96,0},{112,1... | collective-permute-start | bytes 150536 | tf_op jit(solution)/shard_map/ppermute | solution.py:436
  59.3 6.1 %collective-permute-start.5 = (bf16[56,448]{1,0:T(8,128)(2,1)S(1)}, bf16[56,448]{1,0:T(8,128)(2,1)S(1)}, u32[]{:S(2)}, u32[]{:S(2)}) collective-permute-start(bf16[56,448]{1,0:T(8,128)(2,1)S(1)} %get-tuple-element.22), channel_id=1, source_target_pairs={{0,96},{16,112},{32,128},{48,144},{64,160},{80,176},{96,192},{112,... | collective-permute-start | bytes 150536 | tf_op jit(solution)/shard_map/ppermute | solution.py:437
  64.6 22.7 %copy-start = (bf16[1,2048,448]{1,2,0:T(8,128)(2,1)S(1)}, bf16[1,2048,448]{1,2,0:T(8,128)(2,1)}, u32[]{:S(2)}) copy-start(bf16[1,2048,448]{1,2,0:T(8,128)(2,1)} %param.27) | copy-start | bytes 5505028

commit v3 on v2

--- a/solution.py
+++ b/solution.py
@@ -14,7 +14,7 @@
 LAT = 512
 WIDE = 640
 CAP = 48
-FAR = 6
+UP, DOWN = 6, 4
 NEG = -1e30
 SCORE_SCALE = 192.0 ** (-0.5)
 EPS = 1e-06
@@ -137,7 +137,7 @@
     ctx = ctx_ref[0]
     n_ctx = n // 6
     names = route_ref[...]
-    experts = [ctx, lax.rem(ctx + n_ctx - FAR, n_ctx), lax.rem(ctx + FAR, n_ctx)]
+    experts = [ctx, lax.rem(ctx + n_ctx - UP, n_ctx), lax.rem(ctx + DOWN, n_ctx)]
     hit = [jnp.max(jnp.where(names == g, 1.0, 0.0), axis=0, keepdims=True) for g in experts]
     upto = jnp.where(iota((n, n), 0) <= iota((n, n), 1), 1.0, 0.0).astype(bf16)
     hits = jnp.concatenate(hit + [jnp.zeros((8 - len(hit), n), f32)], axis=0)
@@ -178,45 +178,66 @@
     )(ctx, route, gate, iq, iw, keys, after)
 
 
-def pair_kernel(mine_ref, other_ref, out_ref):
-    one = mine_ref[...]
-    two = other_ref[...].astype(f32)
-    peak_one, total_one = read_stats(one)
-    peak_two, total_two = read_stats(two)
-    peak = jnp.maximum(peak_one, peak_two)
-    f_one, f_two = jnp.exp(peak_one - peak), jnp.exp(peak_two - peak)
-    out_ref[..., :LAT] = (one[..., :LAT] * f_one + two[..., :LAT] * f_two).astype(bf16)
-    out_ref[..., LAT:] = stats_tile(peak, total_one * f_one + total_two * f_two).astype(bf16)
-
-
-def pair(mine, other):
-    spec = pl.BlockSpec((2,) + mine.shape[1:], lambda i: (i, 0, 0))
+def merge(parts):
+    stats = [read_stats(x) for x in parts]
+    peak = functools.reduce(jnp.maximum, [p for p, _ in stats])
+    factors = [jnp.exp(p - peak) for p, _ in stats]
+    total = sum(t * f for (_, t), f in zip(stats, factors))
+    return peak, total, sum(x[:, :LAT] * f for x, f in zip(parts, factors))
+
+
+def widen(peak, total, summed):
+    return jnp.concatenate([summed, stats_tile(peak, total)], axis=1)
+
+
+def pair_kernel(ctx_ref, mine_ref, other_ref, keep_ref, up_ref, down_ref):
+    n = mine_ref.shape[0]
+    z = ctx_ref[0] // 2
+    for ref, offsets in ((up_ref, (1, 6, 3)), (down_ref, (7, 4)), (keep_ref, (0, 5, 2))):
+        for i, offset in enumerate(offsets):
+            there = lax.rem(z + offset, n)
+            both = merge([mine_ref[there], other_ref[there].astype(f32)])
+            ref[i] = widen(*both).astype(ref.dtype)
+
+
+def pair(ctx, mine, other):
+    rest = mine.shape[1:]
     return pl.pallas_call(
         pair_kernel,
-        grid=(mine.shape[0] // 2,),
-        in_specs=[spec, spec],
-        out_specs=spec,
-        out_shape=jax.ShapeDtypeStruct(mine.shape, bf16),
+        in_specs=[SMEM, VMEM, VMEM],
+        out_specs=[VMEM] * 3,
+        out_shape=[
+            jax.ShapeDtypeStruct((3,) + rest, f32),
+            jax.ShapeDtypeStruct((3,) + rest, bf16),
+            jax.ShapeDtypeStruct((2,) + rest, bf16),
+        ],
         compiler_params=params(),
         name="pair",
-    )(mine, other)
-
-
-def values_kernel(parts_ref, w_ref, out_ref):
-    n, rows, _ = parts_ref.shape
-    peaks, totals = [], []
-    for i in range(n):
-        p, t = read_stats(parts_ref[i].astype(f32))
-        peaks.append(p)
-        totals.append(t)
-    peak = functools.reduce(jnp.maximum, peaks)
-    summed = jnp.zeros((rows, LAT), f32)
-    total = jnp.zeros((rows, 1), f32)
-    for i in range(n):
-        factor = jnp.exp(peaks[i] - peak)
-        summed = summed + parts_ref[i, :, :LAT].astype(f32) * factor
-        total = total + totals[i] * factor
+    )(ctx, mine, other)
+
+
+def relay_kernel(keep_ref, below_ref, above_ref, up_ref, down_ref):
+    down = merge([keep_ref[1], below_ref[1].astype(f32), above_ref[1].astype(f32)])
+    down_ref[...] = widen(*down).astype(bf16)
+    up_ref[...] = widen(*merge([keep_ref[2], below_ref[2].astype(f32)])).astype(bf16)
+
+
+def relay(keep, below, above):
+    return pl.pallas_call(
+        relay_kernel,
+        in_specs=[VMEM] * 3,
+        out_specs=[VMEM] * 2,
+        out_shape=[jax.ShapeDtypeStruct(keep.shape[1:], bf16)] * 2,
+        compiler_params=params(),
+        name="relay",
+    )(keep, below, above)
+
+
+def values_kernel(keep_ref, below_ref, above_ref, far_below_ref, far_above_ref, w_ref, _, out_ref):
+    parts = [keep_ref[0], below_ref[0], above_ref[0], far_below_ref[...], far_above_ref[...]]
+    _, total, summed = merge([x.astype(f32) for x in parts])
     lat = (summed / total).astype(bf16)
+    rows = lat.shape[0]
     row, col = iota((64, rows), 0), iota((64, rows), 1)
     by_head = jnp.where((row % 8) * 8 + row // 8 == col, 1.0, 0.0).astype(bf16)
     lat = dot(by_head, lat)
@@ -227,18 +248,18 @@
         out_ref[e] = half
 
 
-def values(parts, w_uv, n_exp):
+def values(parts, w_uv, after, n_exp):
     return pl.pallas_call(
         values_kernel,
-        in_specs=[VMEM] * 2,
+        in_specs=[VMEM] * (len(parts) + 1) + [ANY],
         out_specs=VMEM,
         out_shape=jax.ShapeDtypeStruct((n_exp, 16, 512), bf16),
         compiler_params=params(),
         name="values",
-    )(parts, w_uv)
-
-
-def project_kernel(values_ref, w_ref, _, out_ref, acc_ref):
+    )(*parts, w_uv, after)
+
+
+def project_kernel(values_ref, w_ref, out_ref, acc_ref):
     x = values_ref[...].astype(f32)
     n = x.shape[0]
     low = x[:, :8].reshape(n * 8, 512).astype(bf16)
@@ -249,22 +270,22 @@
     out_ref[...] = acc_ref[...].astype(bf16)
 
 
-def project(vals, w_o, after):
+def project(vals, w_o):
     shape = (vals.shape[0] * 6, w_o.shape[0])
     return pl.pallas_call(
         project_kernel,
-        in_specs=[VMEM] * 2 + [ANY],
+        in_specs=[VMEM] * 2,
         out_specs=VMEM,
         out_shape=jax.ShapeDtypeStruct(shape, bf16),
         scratch_shapes=[pltpu.VMEM(shape, f32)],
         compiler_params=params(),
         name="project",
-    )(vals, w_o, after)
+    )(vals, w_o)
 
 
 def fold_kernel(own_ref, above_ref, below_ref, send_ref, up_ref, down_ref):
-    two = own_ref[...].astype(f32) + above_ref[...].astype(f32)
-    three = (two + below_ref[...].astype(f32)).astype(bf16)
+    two = own_ref[...].astype(f32) + below_ref[...].astype(f32)
+    three = (two + above_ref[...].astype(f32)).astype(bf16)
     up_ref[...] = dot(send_ref[0], three).astype(bf16)
     down_ref[...] = dot(send_ref[1], two.astype(bf16)).astype(bf16)
 
@@ -408,33 +429,34 @@
     route, route_weight, w_in, w_down,
 ):
     n_ctx, n_exp = lax.axis_size("ctx"), lax.axis_size("exp")
-    n_z = n_ctx // 2
     ctx = lax.axis_index("ctx").astype(jnp.int32).reshape(1)
     other_core = [(i, i ^ 1) for i in range(n_ctx)]
     def along_z(shift):
         return [(i, (i + shift) % n_ctx) for i in range(n_ctx)]
 
-    z_groups = [[2 * z + k for z in range(n_z)] for k in range(2)]
-
     mine, other = attention(
         ctx, chosen_blocks, jnp.swapaxes(lat_query, 1, 2), jnp.swapaxes(cache, 1, 2)
     )
     other = lax.ppermute(other, "ctx", other_core)
-    parts = pair(mine, other)
-    parts = lax.all_to_all(parts, "ctx", 0, 0, axis_index_groups=z_groups)
-    vals = values(parts, w_uv, n_exp)
+    keep, up, down = pair(ctx, mine, other)
+    below = lax.ppermute(up, "ctx", along_z(2))
+    above = lax.ppermute(down, "ctx", along_z(-2))
+    up, down = relay(keep, below, above)
+    far_below = lax.ppermute(up, "ctx", along_z(DOWN))
+    far_above = lax.ppermute(down, "ctx", along_z(-UP))
     index_scores, send, pick, back, slot = side(
-        ctx, route.T, route_weight.T, idx_query, idx_weight, idx_keys, vals
+        ctx, route.T, route_weight.T, idx_query, idx_weight, idx_keys, up
     )
+    vals = values((keep, below, above, far_below, far_above), w_uv, send, n_exp)
     vals = lax.all_to_all(vals, "exp", 0, 0)
-    part = project(vals, w_o.T, send)
+    part = project(vals, w_o.T)
     own = part.astype(f32) + lax.ppermute(part, "ctx", other_core).astype(f32)
     own = own.astype(bf16)
     above = lax.ppermute(own, "ctx", along_z(-2))
     below = lax.ppermute(own, "ctx", along_z(2))
     up, down = fold(own, above, below, send)
-    far_up = lax.ppermute(up, "ctx", along_z(-FAR))
-    far_down = lax.ppermute(down, "ctx", along_z(FAR))
+    far_up = lax.ppermute(up, "ctx", along_z(-UP))
+    far_down = lax.ppermute(down, "ctx", along_z(DOWN))
     near, w_gate_up = base(own, above, below, hidden_in, pick, w_in[0])
     terms, keep = expert_in(near, far_up, far_down, norm_gain.reshape(1, -1), w_gate_up, n_exp)
     terms = lax.all_to_all(terms, "exp", 0, 0)

time: 110 us -> 103 us (0.936)
  blocking collectives: 64 us -> 54.8 us
  starting transfers between devices: 19.6 us -> 21.6 us
  waiting for transfers between devices: 11.2 us -> 12.7 us
    ppermute x2 -> x6, starting transfers between devices: 3.33 us -> 11.6 us  [the longest x1 3.9 us: local(): above = lax.ppermute(down, 'ctx', along_z(-2))]
    all_to_all x1, blocking collectives: 22.2 us -> 14.3 us  [local(): vals = lax.all_to_all(vals, 'exp', 0, 0)]
    all_to_all x1 -> x0, starting transfers between devices: 6.88 us -> none  [local(): vals = lax.all_to_all(vals, 'exp', 0, 0)]
    ppermute x2 -> x6, waiting for transfers between devices: 0.78 us -> 7.66 us  [the longest x1 2.34 us: local(): above = lax.ppermute(down, 'ctx', along_z(-2))]
    all_to_all x1 -> x0, waiting for transfers between devices: 5.44 us -> none  [local(): vals = lax.all_to_all(vals, 'exp', 0, 0)]
    all_to_all x1, blocking collectives: 20.7 us -> 19.4 us  [local(): outs = lax.all_to_all(outs, 'ctx', 0, 0)]
    pallas_call x3 -> x4, Pallas kernels: 2.44 us -> 1.58 us  [the longest x1 0.53 us: values(): pl.pallas_call(values_kernel, in_specs=[VMEM] * (len(parts) + 1) + [ANY],...]
  transfers between devices with their start and end apart: 7 -> 10, of which waited for: 6 -> 8; matrix products, arithmetic and copies ran while one was open for 0% -> 0% of each run, Pallas kernels for 4% -> 4%
where the time goes in v3:
time: 103 us
  blocking collectives  54.8 us (53%)
  starting transfers between devices  21.6 us (21%)
  Pallas kernels  12.9 us (13%)
  waiting for transfers between devices  12.7 us (12%)
    all_to_all x1, blocking collectives, local(): outs = lax.all_to_all(outs, 'ctx', 0, 0)  19.4 us
    all_to_all x1, blocking collectives, local(): vals = lax.all_to_all(vals, 'exp', 0, 0)  14.3 us
    all_to_all x1, blocking collectives, local(): terms = lax.all_to_all(terms, 'exp', 0, 0)  11.3 us
    all_to_all x1, blocking collectives, local(): act = lax.all_to_all(activation(terms), 'exp', 0, 0)  9.8 us
    pallas_call x1, Pallas kernels, attention(): pl.pallas_call(attention_kernel, grid=(rows // 2,), in_specs=[SMEM, pl.Bl...  4.73 us
    ppermute x1, starting transfers between devices, local(): above = lax.ppermute(down, 'ctx', along_z(-2))  3.9 us
    ppermute x1, starting transfers between devices, local(): own = part.astype(f32) + lax.ppermute(part, 'ctx', other_core).astype(f32)  3.9 us
    ppermute x1, starting transfers between devices, local(): other = lax.ppermute(other, 'ctx', other_core)  3.34 us
  transfers between devices with their start and end apart: 10, of which 8 were waited for; matrix products, arithmetic and copies ran while one was open for 0% of the time, Pallas kernels for 4%

profile of v3, /device:TPU:1, one launch (start us, length us, event | category | flops | bytes accessed | tf_op | source)
XLA Modules:
  0.0 102.8 jit_solution(17600045938376096510)
XLA Ops:
  0.7 4.7 %attention.1 = (f32[8,48,640]{2,1,0:T(8,128)S(1)}, bf16[8,48,640]{2,1,0:T(8,128)(2,1)S(1)}) custom-call(s32[1]{0:T(128)} %bitcast.ctx_ref, s32[6,32]{1,0:T(8,128)} %blocks_ref.1, bf16[6,576,128]{2,1,0:T(8,128)(2,1)} %bitcast.18, bf16[6,576,384]{2,1,0:T(8,128)(2,1)} %bitcast.17), custom_call_target="tpu_custom_call" | custom-call | tf_op jit(solution)/shard_map/attention/pallas_call | solution.py:108
  5.5 3.3 %collective-permute-start = (bf16[8,48,640]{2,1,0:T(8,128)(2,1)S(1)}, bf16[8,48,640]{2,1,0:T(8,128)(2,1)S(1)}, u32[]{:S(2)}, u32[]{:S(2)}) collective-permute-start(bf16[8,48,640]{2,1,0:T(8,128)(2,1)S(1)} %get-tuple-element.21), channel_id=1, source_target_pairs={{0,16},{16,0},{32,48},{48,32},{64,80},{80,64},{96,112},{112,96},{1... | collective-permute-start | bytes 1474568 | tf_op jit(solution)/shard_map/ppermute | solution.py:440
  8.8 1.5 %collective-permute-done.other_ref = bf16[8,48,640]{2,1,0:T(8,128)(2,1)S(1)} collective-permute-done((bf16[8,48,640]{2,1,0:T(8,128)(2,1)S(1)}, bf16[8,48,640]{2,1,0:T(8,128)(2,1)S(1)}, u32[]{:S(2)}, u32[]{:S(2)}) %collective-permute-start) | collective-permute-done | bytes 491552 | tf_op jit(solution)/shard_map/ppermute | solution.py:440
  10.8 3.9 %collective-permute-start.2 = (bf16[2,48,640]{2,1,0:T(8,128)(2,1)S(1)}, bf16[2,48,640]{2,1,0:T(8,128)(2,1)S(1)}, u32[]{:S(2)}, u32[]{:S(2)}) collective-permute-start(bf16[2,48,640]{2,1,0:T(8,128)(2,1)S(1)} %get-tuple-element.24), channel_id=1, source_target_pairs={{0,224},{16,240},{32,0},{48,16},{64,32},{80,48},{96,64},{112,80},{... | collective-permute-start | bytes 368648 | tf_op jit(solution)/shard_map/ppermute | solution.py:443
  14.7 2.3 %collective-permute-done.2.above_ref = bf16[2,48,640]{2,1,0:T(8,128)(2,1)S(1)} collective-permute-done((bf16[2,48,640]{2,1,0:T(8,128)(2,1)S(1)}, bf16[2,48,640]{2,1,0:T(8,128)(2,1)S(1)}, u32[]{:S(2)}, u32[]{:S(2)}) %collective-permute-start.2) | collective-permute-done | bytes 122912 | tf_op jit(solution)/shard_map/ppermute | solution.py:443
  17.0 2.3 %collective-permute-done.1.below_ref = bf16[3,48,640]{2,1,0:T(8,128)(2,1)S(1)} collective-permute-done((bf16[3,48,640]{2,1,0:T(8,128)(2,1)S(1)}, bf16[3,48,640]{2,1,0:T(8,128)(2,1)S(1)}, u32[]{:S(2)}, u32[]{:S(2)}) %collective-permute-start.1) | collective-permute-done | bytes 184352 | tf_op jit(solution)/shard_map/ppermute | solution.py:442
  19.5 2.1 %collective-permute-start.4 = (bf16[48,640]{1,0:T(8,128)(2,1)S(1)}, bf16[48,640]{1,0:T(8,128)(2,1)S(1)}, u32[]{:S(2)}, u32[]{:S(2)}) collective-permute-start(bf16[48,640]{1,0:T(8,128)(2,1)S(1)} %get-tuple-element.27), channel_id=1, source_target_pairs={{0,160},{16,176},{32,192},{48,208},{64,224},{80,240},{96,0},{112,1... | collective-permute-start | bytes 184328 | tf_op jit(solution)/shard_map/ppermute | solution.py:446
  21.6 1.2 %collective-permute-start.3 = (bf16[48,640]{1,0:T(8,128)(2,1)S(1)}, bf16[48,640]{1,0:T(8,128)(2,1)S(1)}, u32[]{:S(2)}, u32[]{:S(2)}) collective-permute-start(bf16[48,640]{1,0:T(8,128)(2,1)S(1)} %get-tuple-element.25._), channel_id=1, source_target_pairs={{0,64},{16,80},{32,96},{48,112},{64,128},{80,144},{96,160},{112,17... | collective-permute-start | bytes 184328 | tf_op jit(solution)/shard_map/ppermute | solution.py:445
  22.8 2.0 %side.1 = (f32[6,384]{1,0:T(8,128)}, bf16[2,56,96]{2,1,0:T(8,128)(2,1)S(1)}, bf16[56,96]{1,0:T(8,128)(2,1)S(1)}, bf16[128,48]{1,0:T(8,128)(2,1)S(1)}, f32[48,128]{1,0:T(8,128)S(1)}) custom-call(s32[1]{0:T(128)} %bitcast.ctx_ref, s32[4,96]{1,0:T(4,128)S(1)} %bitcast.14, f32[4,96]{1,0:T(4,128)S(1)} %bitcast.15, bf16[6,64,128]{2,1,0:T(8,128)(2,1)S(1)} %copy-done.4, ...), custom_call_target="tpu_custom_call" | custom-call | tf_op jit(solution)/shard_map/side/pallas_call | solution.py:165
  24.9 2.0 %collective-permute-done.4.far_above_ref = bf16[48,640]{1,0:T(8,128)(2,1)S(1)} collective-permute-done((bf16[48,640]{1,0:T(8,128)(2,1)S(1)}, bf16[48,640]{1,0:T(8,128)(2,1)S(1)}, u32[]{:S(2)}, u32[]{:S(2)}) %collective-permute-start.4) | collective-permute-done | bytes 61472 | tf_op jit(solution)/shard_map/ppermute | solution.py:446
  26.9 0.7 collective-permute-done.3.far_below_ref
  28.2 14.3 %all_to_all.20.values_ref = bf16[16,16,512]{2,1,0:T(8,128)(2,1)S(1)} all-to-all(bf16[16,16,512]{2,1,0:T(8,128)(2,1)S(1)} %values.1), channel_id=1, replica_groups=mesh['ctx'=16,'exp'=16] {'exp'}, dimensions={0} | all-to-all | bytes 524288 | tf_op jit(solution)/shard_map/all_to_all | solution.py:451
  42.9 3.9 %collective-permute-start.5 = (bf16[96,448]{1,0:T(8,128)(2,1)S(1)}, bf16[96,448]{1,0:T(8,128)(2,1)S(1)}, u32[]{:S(2)}, u32[]{:S(2)}) collective-permute-start(bf16[96,448]{1,0:T(8,128)(2,1)S(1)} %project.1), channel_id=1, source_target_pairs={{0,16},{16,0},{32,48},{48,32},{64,80},{80,64},{96,112},{112,96},{1... | collective-permute-start | bytes 258056 | tf_op jit(solution)/shard_map/ppermute | solution.py:453
  46.8 0.9 collective-permute-done.5
  47.8 0.7 collective-permute-start.7
  48.6 2.0 %collective-permute-start.6 = (bf16[96,448]{1,0:T(8,128)(2,1)S(1)}, bf16[96,448]{1,0:T(8,128)(2,1)S(1)}, u32[]{:S(2)}, u32[]{:S(2)}) collective-permute-start(bf16[96,448]{1,0:T(8,128)(2,1)S(1)} %add_convert_fusion.own_ref), channel_id=1, source_target_pairs={{0,224},{16,240},{32,0},{48,16},{64,32},{80,48},{96,64},{112,80},{... | collective-permute-start | bytes 258056 | tf_op jit(solution)/shard_map/ppermute | solution.py:455
  50.6 2.6 %collective-permute-done.7.below_ref = bf16[96,448]{1,0:T(8,128)(2,1)S(1)} collective-permute-done((bf16[96,448]{1,0:T(8,128)(2,1)S(1)}, bf16[96,448]{1,0:T(8,128)(2,1)S(1)}, u32[]{:S(2)}, u32[]{:S(2)}) %collective-permute-start.7) | collective-permute-done | bytes 86048 | tf_op jit(solution)/shard_map/ppermute | solution.py:456
  53.3 1.3 %collective-permute-start.8 = (bf16[56,448]{1,0:T(8,128)(2,1)S(1)}, bf16[56,448]{1,0:T(8,128)(2,1)S(1)}, u32[]{:S(2)}, u32[]{:S(2)}) collective-permute-start(bf16[56,448]{1,0:T(8,128)(2,1)S(1)} %get-tuple-element.31), channel_id=1, source_target_pairs={{0,160},{16,176},{32,192},{48,208},{64,224},{80,240},{96,0},{112,1... | collective-permute-start | bytes 150536 | tf_op jit(solution)/shard_map/ppermute | solution.py:458
  54.6 3.0 %collective-permute-start.9 = (bf16[56,448]{1,0:T(8,128)(2,1)S(1)}, bf16[56,448]{1,0:T(8,128)(2,1)S(1)}, u32[]{:S(2)}, u32[]{:S(2)}) collective-permute-start(bf16[56,448]{1,0:T(8,128)(2,1)S(1)} %get-tuple-element.32), channel_id=1, source_target_pairs={{0,64},{16,80},{32,96},{48,112},{64,128},{80,144},{96,160},{112,17... | collective-permute-start | bytes 150536 | tf_op jit(solution)/shard_map/ppermute | solution.py:459
  57.6 2.1 %base.1 = (f32[56,448]{1,0:T(8,128)S(1)}, bf16[448,4096]{1,0:T(8,128)(2,1)S(1)}) custom-call(bf16[96,448]{1,0:T(8,128)(2,1)S(1)} %add_convert_fusion.own_ref, bf16[96,448]{1,0:T(8,128)(2,1)S(1)} %collective-permute-done.6.above_ref, bf16[96,448]{1,0:T(8,128)(2,1)S(1)} %collective-permute-done.7.below_ref, bf16[96,448]{1,0:T(8,128)(2,1)S(1)} %copy-done.5, ...), custom_call_target="tpu_custom_call" | custom-call | tf_op jit(solution)/shard_map/base/pallas_call | solution.py:315
  60.7 11.3 %all_to_all.21.parts_ref = bf16[16,56,256]{2,1,0:T(8,128)(2,1)S(1)} all-to-all(bf16[16,56,256]{2,1,0:T(8,128)(2,1)S(1)} %get-tuple-element.34), channel_id=1, replica_groups=mesh['ctx'=16,'exp'=16] {'exp'}, dimensions={0} | all-to-all | bytes 917504 | tf_op jit(solution)/shard_map/all_to_all | solution.py:462
  72.1 9.8 %all_to_all.22.act_ref = bf16[16,48,128]{2,1,0:T(8,128)(2,1)S(1)} all-to-all(bf16[16,48,128]{2,1,0:T(8,128)(2,1)S(1)} %activation.1), channel_id=1, replica_groups=mesh['ctx'=16,'exp'=16] {'exp'}, dimensions={0} | all-to-all | bytes 393216 | tf_op jit(solution)/shard_map/all_to_all | solution.py:463
  81.9 0.9 expert_out.1
  82.8 19.4 %all_to_all.23.parts_ref = bf16[16,16,256]{2,1,0:T(8,128)(2,1)S(1)} all-to-all(bf16[16,16,256]{2,1,0:T(8,128)(2,1)S(1)} %expert_out.1), channel_id=1, replica_groups=mesh['ctx'=16,'exp'=16] {'ctx'}, dimensions={0} | all-to-all | bytes 262144 | tf_op jit(solution)/shard_map/all_to_all | solution.py:465
  (33 shorter events, 3.7 us)
Async XLA Ops:
  0.6 22.2 %copy-start.9 = (f32[96,4]{0,1:T(4,128)S(1)}, f32[96,4]{0,1:T(4,128)}, u32[]{:S(2)}) copy-start(f32[96,4]{0,1:T(4,128)} %param.25) | copy-start | bytes 4612
  0.6 22.2 %copy-start.8 = (s32[96,4]{0,1:T(4,128)S(1)}, s32[96,4]{0,1:T(4,128)}, u32[]{:S(2)}) copy-start(s32[96,4]{0,1:T(4,128)} %param.24) | copy-start | bytes 4612
  0.7 22.2 %copy-start.6 = (f32[6,64]{1,0:T(8,128)S(1)}, f32[6,64]{1,0:T(8,128)}, u32[]{:S(2)}) copy-start(f32[6,64]{1,0:T(8,128)} %iw_ref.1) | copy-start | bytes 4612
  0.7 22.2 %copy-start.4 = (bf16[6,64,128]{2,1,0:T(8,128)(2,1)S(1)}, bf16[6,64,128]{2,1,0:T(8,128)(2,1)}, u32[]{:S(2)}) copy-start(bf16[6,64,128]{2,1,0:T(8,128)(2,1)} %iq_ref.1) | copy-start | bytes 294916
  0.7 22.2 %copy-start.3 = (bf16[6,384,128]{2,1,0:T(8,128)(2,1)S(1)}, bf16[6,384,128]{2,1,0:T(8,128)(2,1)}, u32[]{:S(2)}) copy-start(bf16[6,384,128]{2,1,0:T(8,128)(2,1)} %keys_ref.1) | copy-start | bytes 1769476
  0.7 26.9 %copy-start.1 = (bf16[8,512,128]{2,1,0:T(8,128)(2,1)S(1)}, bf16[8,512,128]{2,1,0:T(8,128)(2,1)}, u32[]{:S(2)}) copy-start(bf16[8,512,128]{2,1,0:T(8,128)(2,1)} %w_ref.1) | copy-start | bytes 3145732
  5.4 37.0 %copy-start.2 = (bf16[1024,448]{0,1:T(8,128)(2,1)S(1)}, bf16[1024,448]{0,1:T(8,128)(2,1)}, u32[]{:S(2)}) copy-start(bf16[1024,448]{0,1:T(8,128)(2,1)} %param.21) | copy-start | bytes 2752516
  5.5 4.8 %collective-permute-start = (bf16[8,48,640]{2,1,0:T(8,128)(2,1)S(1)}, bf16[8,48,640]{2,1,0:T(8,128)(2,1)S(1)}, u32[]{:S(2)}, u32[]{:S(2)}) collective-permute-start(bf16[8,48,640]{2,1,0:T(8,128)(2,1)S(1)} %get-tuple-element.21), channel_id=1, source_target_pairs={{0,16},{16,0},{32,48},{48,32},{64,80},{80,64},{96,112},{112,96},{1... | collective-permute-start | bytes 1474568 | tf_op jit(solution)/shard_map/ppermute | solution.py:440
  10.3 47.3 %copy-start.5 = (bf16[96,448]{1,0:T(8,128)(2,1)S(1)}, bf16[96,448]{1,0:T(8,128)(2,1)}, u32[]{:S(2)}) copy-start(bf16[96,448]{1,0:T(8,128)(2,1)} %hidden_ref.1) | copy-start | bytes 258052
  10.7 8.6 %collective-permute-start.1 = (bf16[3,48,640]{2,1,0:T(8,128)(2,1)S(1)}, bf16[3,48,640]{2,1,0:T(8,128)(2,1)S(1)}, u32[]{:S(2)}, u32[]{:S(2)}) collective-permute-start(bf16[3,48,640]{2,1,0:T(8,128)(2,1)S(1)} %get-tuple-element.23), channel_id=1, source_target_pairs={{0,32},{16,48},{32,64},{48,80},{64,96},{80,112},{96,128},{112,144}... | collective-permute-start | bytes 552968 | tf_op jit(solution)/shard_map/ppermute | solution.py:442
  10.8 6.2 %collective-permute-start.2 = (bf16[2,48,640]{2,1,0:T(8,128)(2,1)S(1)}, bf16[2,48,640]{2,1,0:T(8,128)(2,1)S(1)}, u32[]{:S(2)}, u32[]{:S(2)}) collective-permute-start(bf16[2,48,640]{2,1,0:T(8,128)(2,1)S(1)} %get-tuple-element.24), channel_id=1, source_target_pairs={{0,224},{16,240},{32,0},{48,16},{64,32},{80,48},{96,64},{112,80},{... | collective-permute-start | bytes 368648 | tf_op jit(solution)/shard_map/ppermute | solution.py:443
  19.5 7.4 %collective-permute-start.4 = (bf16[48,640]{1,0:T(8,128)(2,1)S(1)}, bf16[48,640]{1,0:T(8,128)(2,1)S(1)}, u32[]{:S(2)}, u32[]{:S(2)}) collective-permute-start(bf16[48,640]{1,0:T(8,128)(2,1)S(1)} %get-tuple-element.27), channel_id=1, source_target_pairs={{0,160},{16,176},{32,192},{48,208},{64,224},{80,240},{96,0},{112,1... | collective-permute-start | bytes 184328 | tf_op jit(solution)/shard_map/ppermute | solution.py:446
  21.6 6.0 %collective-permute-start.3 = (bf16[48,640]{1,0:T(8,128)(2,1)S(1)}, bf16[48,640]{1,0:T(8,128)(2,1)S(1)}, u32[]{:S(2)}, u32[]{:S(2)}) collective-permute-start(bf16[48,640]{1,0:T(8,128)(2,1)S(1)} %get-tuple-element.25._), channel_id=1, source_target_pairs={{0,64},{16,80},{32,96},{48,112},{64,128},{80,144},{96,160},{112,17... | collective-permute-start | bytes 184328 | tf_op jit(solution)/shard_map/ppermute | solution.py:445
  28.1 31.9 %copy-start.7 = (f32[448]{0:T(512)S(1)}, f32[448]{0:T(512)}, u32[]{:S(2)}) copy-start(f32[448]{0:T(512)} %param.23) | copy-start | bytes 5380
  42.9 4.8 %collective-permute-start.5 = (bf16[96,448]{1,0:T(8,128)(2,1)S(1)}, bf16[96,448]{1,0:T(8,128)(2,1)S(1)}, u32[]{:S(2)}, u32[]{:S(2)}) collective-permute-start(bf16[96,448]{1,0:T(8,128)(2,1)S(1)} %project.1), channel_id=1, source_target_pairs={{0,16},{16,0},{32,48},{48,32},{64,80},{80,64},{96,112},{112,96},{1... | collective-permute-start | bytes 258056 | tf_op jit(solution)/shard_map/ppermute | solution.py:453
  47.8 5.3 %collective-permute-start.7 = (bf16[96,448]{1,0:T(8,128)(2,1)S(1)}, bf16[96,448]{1,0:T(8,128)(2,1)S(1)}, u32[]{:S(2)}, u32[]{:S(2)}) collective-permute-start(bf16[96,448]{1,0:T(8,128)(2,1)S(1)} %add_convert_fusion.own_ref), channel_id=1, source_target_pairs={{0,32},{16,48},{32,64},{48,80},{64,96},{80,112},{96,128},{112,144}... | collective-permute-start | bytes 258056 | tf_op jit(solution)/shard_map/ppermute | solution.py:456
  48.6 4.6 %collective-permute-start.6 = (bf16[96,448]{1,0:T(8,128)(2,1)S(1)}, bf16[96,448]{1,0:T(8,128)(2,1)S(1)}, u32[]{:S(2)}, u32[]{:S(2)}) collective-permute-start(bf16[96,448]{1,0:T(8,128)(2,1)S(1)} %add_convert_fusion.own_ref), channel_id=1, source_target_pairs={{0,224},{16,240},{32,0},{48,16},{64,32},{80,48},{96,64},{112,80},{... | collective-permute-start | bytes 258056 | tf_op jit(solution)/shard_map/ppermute | solution.py:455
  53.3 6.4 %collective-permute-start.8 = (bf16[56,448]{1,0:T(8,128)(2,1)S(1)}, bf16[56,448]{1,0:T(8,128)(2,1)S(1)}, u32[]{:S(2)}, u32[]{:S(2)}) collective-permute-start(bf16[56,448]{1,0:T(8,128)(2,1)S(1)} %get-tuple-element.31), channel_id=1, source_target_pairs={{0,160},{16,176},{32,192},{48,208},{64,224},{80,240},{96,0},{112,1... | collective-permute-start | bytes 150536 | tf_op jit(solution)/shard_map/ppermute | solution.py:458
  54.6 5.4 %collective-permute-start.9 = (bf16[56,448]{1,0:T(8,128)(2,1)S(1)}, bf16[56,448]{1,0:T(8,128)(2,1)S(1)}, u32[]{:S(2)}, u32[]{:S(2)}) collective-permute-start(bf16[56,448]{1,0:T(8,128)(2,1)S(1)} %get-tuple-element.32), channel_id=1, source_target_pairs={{0,64},{16,80},{32,96},{48,112},{64,128},{80,144},{96,160},{112,17... | collective-permute-start | bytes 150536 | tf_op jit(solution)/shard_map/ppermute | solution.py:459
  59.7 22.3 %copy-start = (bf16[1,2048,448]{1,2,0:T(8,128)(2,1)S(1)}, bf16[1,2048,448]{1,2,0:T(8,128)(2,1)}, u32[]{:S(2)}) copy-start(bf16[1,2048,448]{1,2,0:T(8,128)(2,1)} %param.27) | copy-start | bytes 5505028

commit v4 on v3

--- a/solution.py
+++ b/solution.py
@@ -66,60 +66,97 @@
     return peak, total
 
 
-def attention_kernel(ctx_ref, blocks_ref, query_ref, cache_ref, mine_ref, other_ref, mask_ref):
-    step = pl.program_id(0)
+def pack(x):
+    n = x.shape[0]
+    half = (n // 2 + 7) // 8 * 8
+    ends = jnp.concatenate([x[:half, 384:], x[n - half :, 384:]], axis=1)
+    return jnp.concatenate([x[:, :128], x[:, 128:256], x[:, 256:384], ends], axis=0)
+
+
+def unpack(x, n):
+    half = x.shape[0] - 3 * n
+    ends = jnp.concatenate([x[3 * n :, :64], x[3 * n + 2 * half - n :, 64:]], axis=0)
+    return jnp.concatenate([x[:n], x[n : 2 * n], x[2 * n : 3 * n], ends], axis=1)
+
+
+def packed_lines(n):
+    return 3 * n + (n // 2 + 7) // 8 * 8
+
+
+def attention_kernel(
+    ctx_ref, blocks_hbm, query_hbm, cache_hbm, mine_ref, other_ref, blocks_ref, query_ref, cache_ref, sems, sem
+):
+    rows, _, tokens = cache_ref.shape
+    load_blocks = pltpu.make_async_copy(blocks_hbm, blocks_ref, sem)
+    copies = [
+        (
+            pltpu.make_async_copy(query_hbm.at[r], query_ref.at[r], sems.at[0, r]),
+            pltpu.make_async_copy(cache_hbm.at[r], cache_ref.at[r], sems.at[1, r]),
+        )
+        for r in range(rows)
+    ]
+
+    def start(r):
+        for copy in copies[r]:
+            copy.start()
+
+    start(0)
+    load_blocks.start()
+    for r in range(1, 4):
+        start(r)
     ctx = ctx_ref[0]
     core = lax.rem(ctx, 2)
-    tokens = cache_ref.shape[2]
     per = tokens // BLOCK
-
-    @pl.when(step == 0)
-    def _():
-        rows = blocks_ref.shape[0]
-        block_of = iota((rows, tokens), 1) // BLOCK
-        mask = jnp.zeros((rows, tokens), f32)
-        picked = blocks_ref[...]
-        for b in range(per):
-            hit = jnp.max(jnp.where(picked == ctx * per + b, 1.0, 0.0), axis=1, keepdims=True)
-            mask = jnp.where(block_of == b, hit, mask)
-        mask_ref[...] = mask
-
-    mine, other = [], []
-    for i in range(2):
-        chosen = mask_ref[pl.ds(step * 2 + i, 1), :] > 0.0
-        keys = cache_ref[i]
-        scores = dot(query_ref[i], keys, ((0,), (0,))) * SCORE_SCALE
-        masked = jnp.where(chosen, scores, NEG)
-        peak = jnp.max(masked, axis=1, keepdims=True)
-        expo = jnp.where(chosen, jnp.exp(masked - peak), 0.0)
-        total = jnp.sum(expo, axis=1, keepdims=True)
-        weighted = dot(expo.astype(bf16), keys[:LAT], ((1,), (1,)))
-        wide = jnp.concatenate([weighted, stats_tile(peak, total)], axis=1)
-        wide = wide.reshape(8, 2, 8, WIDE)
-        mine.append(jnp.where(core == 0, wide[:, 0], wide[:, 1]))
-        other.append(jnp.where(core == 0, wide[:, 1], wide[:, 0]))
-    mine_ref[...] = jnp.concatenate(mine, axis=1)
-    other_ref[...] = jnp.concatenate(other, axis=1).astype(bf16)
+    mask = None
+    for r in range(0, rows, 2):
+        for i in range(r, r + 2):
+            for copy in copies[i]:
+                copy.wait()
+            if i + 4 < rows:
+                start(i + 4)
+        if mask is None:
+            load_blocks.wait()
+            block_of = iota((rows, tokens), 1) // BLOCK
+            mask = jnp.zeros((rows, tokens), f32)
+            picked = blocks_ref[...]
+            for b in range(per):
+                hit = jnp.max(jnp.where(picked == ctx * per + b, 1.0, 0.0), axis=1, keepdims=True)
+                mask = jnp.where(block_of == b, hit, mask)
+        mine, other = [], []
+        for i in range(r, r + 2):
+            chosen = mask[i : i + 1, :] > 0.0
+            keys = cache_ref[i]
+            scores = dot(query_ref[i], keys, ((0,), (0,))) * SCORE_SCALE
+            masked = jnp.where(chosen, scores, NEG)
+            peak = jnp.max(masked, axis=1, keepdims=True)
+            expo = jnp.where(chosen, jnp.exp(masked - peak), 0.0)
+            total = jnp.sum(expo, axis=1, keepdims=True)
+            weighted = dot(expo.astype(bf16), keys[:LAT], ((1,), (1,)))
+            wide = jnp.concatenate([weighted, stats_tile(peak, total)], axis=1)
+            wide = wide.reshape(8, 2, 8, WIDE)
+            mine.append(jnp.where(core == 0, wide[:, 0], wide[:, 1]))
+            other.append(jnp.where(core == 0, wide[:, 1], wide[:, 0]))
+        mine_ref[:, 8 * r : 8 * r + 16, :] = jnp.concatenate(mine, axis=1)
+        other_ref[:, 8 * r : 8 * r + 16, :] = jnp.concatenate(other, axis=1).astype(bf16)
 
 
 def attention(ctx, blocks, query, cache):
-    rows, width, heads = query.shape
-    tokens = cache.shape[2]
+    rows = query.shape[0]
     return pl.pallas_call(
         attention_kernel,
-        grid=(rows // 2,),
-        in_specs=[
-            SMEM,
-            pl.BlockSpec((rows, blocks.shape[1]), lambda i: (0, 0)),
-            pl.BlockSpec((2, width, heads), lambda i: (i, 0, 0)),
-            pl.BlockSpec((2, width, tokens), lambda i: (i, 0, 0)),
-        ],
-        out_specs=[pl.BlockSpec((8, 16, WIDE), lambda i: (0, i, 0))] * 2,
+        in_specs=[SMEM, HBM, HBM, HBM],
+        out_specs=[VMEM] * 2,
         out_shape=[
             jax.ShapeDtypeStruct((8, rows * 8, WIDE), f32),
             jax.ShapeDtypeStruct((8, rows * 8, WIDE), bf16),
         ],
-        scratch_shapes=[pltpu.VMEM((rows, tokens), f32)],
+        scratch_shapes=[
+            pltpu.VMEM(blocks.shape, jnp.int32),
+            pltpu.VMEM(query.shape, bf16),
+            pltpu.VMEM(cache.shape, bf16),
+            pltpu.SemaphoreType.DMA((2, rows)),
+            pltpu.SemaphoreType.DMA,
+        ],
         compiler_params=params(16),
         name="attention",
     )(ctx, in_hbm(blocks), in_hbm(query), in_hbm(cache))
@@ -267,7 +304,7 @@
     acc = dot(low, w_ref[:, :512], ((1,), (1,))) + dot(high, w_ref[:, 512:], ((1,), (1,)))
     for e in range(n):
         acc_ref[6 * e : 6 * e + 6, :] = acc[8 * e : 8 * e + 6, :]
-    out_ref[...] = acc_ref[...].astype(bf16)
+    out_ref[...] = pack(acc_ref[...]).astype(bf16)
 
 
 def project(vals, w_o):
@@ -276,7 +313,7 @@
         project_kernel,
         in_specs=[VMEM] * 2,
         out_specs=VMEM,
-        out_shape=jax.ShapeDtypeStruct(shape, bf16),
+        out_shape=jax.ShapeDtypeStruct((packed_lines(shape[0]), 128), bf16),
         scratch_shapes=[pltpu.VMEM(shape, f32)],
         compiler_params=params(),
         name="project",
@@ -284,14 +321,15 @@
 
 
 def fold_kernel(own_ref, above_ref, below_ref, send_ref, up_ref, down_ref):
+    n = send_ref.shape[2]
     two = own_ref[...].astype(f32) + below_ref[...].astype(f32)
-    three = (two + above_ref[...].astype(f32)).astype(bf16)
-    up_ref[...] = dot(send_ref[0], three).astype(bf16)
-    down_ref[...] = dot(send_ref[1], two.astype(bf16)).astype(bf16)
+    three = two + above_ref[...].astype(f32)
+    up_ref[...] = pack(dot(send_ref[0], unpack(three, n).astype(bf16))).astype(bf16)
+    down_ref[...] = pack(dot(send_ref[1], unpack(two, n).astype(bf16))).astype(bf16)
 
 
 def fold(own, above, below, send):
-    shape = jax.ShapeDtypeStruct((send.shape[1], own.shape[1]), bf16)
+    shape = jax.ShapeDtypeStruct((packed_lines(send.shape[1]), 128), bf16)
     return pl.pallas_call(
         fold_kernel,
         in_specs=[VMEM] * 4,
@@ -306,7 +344,10 @@
     load = pltpu.make_async_copy(w_hbm, w_ref, sem)
     load.start()
     pick = pick_ref[...]
-    near = dot(pick, own_ref[...]) + dot(pick, above_ref[...]) + dot(pick, below_ref[...])
+    n = pick.shape[1]
+    near = sum(
+        dot(pick, unpack(ref[...].astype(f32), n).astype(bf16)) for ref in (own_ref, above_ref, below_ref)
+    )
     out_ref[...] = dot(pick, hidden_ref[...]) + near
     load.wait()
 
@@ -317,7 +358,7 @@
         in_specs=[VMEM] * 5 + [HBM],
         out_specs=[VMEM] * 2,
         out_shape=[
-            jax.ShapeDtypeStruct((pick.shape[0], own.shape[1]), f32),
+            jax.ShapeDtypeStruct((pick.shape[0], hidden.shape[1]), f32),
             jax.ShapeDtypeStruct(w_in.shape, bf16),
         ],
         scratch_shapes=[pltpu.SemaphoreType.DMA],
@@ -329,7 +370,8 @@
 def expert_in_kernel(near_ref, far_up_ref, far_down_ref, gain_ref, w_ref, out_ref, keep_ref):
     n = out_ref.shape[0]
     half = w_ref.shape[1] // 2
-    attn = near_ref[...] + far_up_ref[...].astype(f32) + far_down_ref[...].astype(f32)
+    far = far_up_ref[...].astype(f32) + far_down_ref[...].astype(f32)
+    attn = near_ref[...] + unpack(far, near_ref.shape[0])
     resid32 = attn.astype(bf16).astype(f32)
     keep_ref[...] = resid32[CAP:]
     picked = resid32[:CAP]

time: 103 us -> 102 us (level)
  no operation moved by 1% of the time
where the time goes in v4:
time: 102 us
  blocking collectives  54.7 us (54%)
  starting transfers between devices  21.7 us (21%)
  Pallas kernels  12.7 us (12%)
  waiting for transfers between devices  12.2 us (12%)
    all_to_all x1, blocking collectives, local(): outs = lax.all_to_all(outs, 'ctx', 0, 0)  19.2 us
    all_to_all x1, blocking collectives, local(): vals = lax.all_to_all(vals, 'exp', 0, 0)  14.3 us
    all_to_all x1, blocking collectives, local(): terms = lax.all_to_all(terms, 'exp', 0, 0)  11.3 us
    all_to_all x1, blocking collectives, local(): act = lax.all_to_all(activation(terms), 'exp', 0, 0)  9.78 us
    pallas_call x1, Pallas kernels, attention(): pl.pallas_call(attention_kernel, in_specs=[SMEM, HBM, HBM, HBM], out_spec...  4.36 us
    ppermute x1, starting transfers between devices, local(): above = lax.ppermute(down, 'ctx', along_z(-2))  3.92 us
    ppermute x1, starting transfers between devices, local(): own = part.astype(f32) + lax.ppermute(part, 'ctx', other_core).astype(f32)  3.9 us
    ppermute x1, starting transfers between devices, local(): other = lax.ppermute(other, 'ctx', other_core)  3.33 us
  transfers between devices with their start and end apart: 10, of which 8 were waited for; matrix products, arithmetic and copies ran while one was open for 0% of the time, Pallas kernels for 4%

profile of v4, /device:TPU:1, one launch (start us, length us, event | category | flops | bytes accessed | tf_op | source)
XLA Modules:
  0.0 102.1 jit_solution(3758753181642087550)
XLA Ops:
  0.7 4.4 %attention.1 = (f32[8,48,640]{2,1,0:T(8,128)S(1)}, bf16[8,48,640]{2,1,0:T(8,128)(2,1)S(1)}) custom-call(s32[1]{0:T(128)} %bitcast.ctx_ref, s32[6,32]{1,0:T(8,128)} %blocks_hbm.1, bf16[6,576,128]{2,1,0:T(8,128)(2,1)} %bitcast.18, bf16[6,576,384]{2,1,0:T(8,128)(2,1)} %bitcast.17), custom_call_target="tpu_custom_call" | custom-call | tf_op jit(solution)/shard_map/attention/pallas_call | solution.py:145
  5.1 3.3 %collective-permute-start = (bf16[8,48,640]{2,1,0:T(8,128)(2,1)S(1)}, bf16[8,48,640]{2,1,0:T(8,128)(2,1)S(1)}, u32[]{:S(2)}, u32[]{:S(2)}) collective-permute-start(bf16[8,48,640]{2,1,0:T(8,128)(2,1)S(1)} %get-tuple-element.21), channel_id=1, source_target_pairs={{0,16},{16,0},{32,48},{48,32},{64,80},{80,64},{96,112},{112,96},{1... | collective-permute-start | bytes 1474568 | tf_op jit(solution)/shard_map/ppermute | solution.py:482
  8.4 1.5 %collective-permute-done.other_ref = bf16[8,48,640]{2,1,0:T(8,128)(2,1)S(1)} collective-permute-done((bf16[8,48,640]{2,1,0:T(8,128)(2,1)S(1)}, bf16[8,48,640]{2,1,0:T(8,128)(2,1)S(1)}, u32[]{:S(2)}, u32[]{:S(2)}) %collective-permute-start) | collective-permute-done | bytes 491552 | tf_op jit(solution)/shard_map/ppermute | solution.py:482
  10.4 3.9 %collective-permute-start.2 = (bf16[2,48,640]{2,1,0:T(8,128)(2,1)S(1)}, bf16[2,48,640]{2,1,0:T(8,128)(2,1)S(1)}, u32[]{:S(2)}, u32[]{:S(2)}) collective-permute-start(bf16[2,48,640]{2,1,0:T(8,128)(2,1)S(1)} %get-tuple-element.24), channel_id=1, source_target_pairs={{0,224},{16,240},{32,0},{48,16},{64,32},{80,48},{96,64},{112,80},{... | collective-permute-start | bytes 368648 | tf_op jit(solution)/shard_map/ppermute | solution.py:485
  14.3 2.3 %collective-permute-done.2.above_ref = bf16[2,48,640]{2,1,0:T(8,128)(2,1)S(1)} collective-permute-done((bf16[2,48,640]{2,1,0:T(8,128)(2,1)S(1)}, bf16[2,48,640]{2,1,0:T(8,128)(2,1)S(1)}, u32[]{:S(2)}, u32[]{:S(2)}) %collective-permute-start.2) | collective-permute-done | bytes 122912 | tf_op jit(solution)/shard_map/ppermute | solution.py:485
  16.7 2.3 %collective-permute-done.1.below_ref = bf16[3,48,640]{2,1,0:T(8,128)(2,1)S(1)} collective-permute-done((bf16[3,48,640]{2,1,0:T(8,128)(2,1)S(1)}, bf16[3,48,640]{2,1,0:T(8,128)(2,1)S(1)}, u32[]{:S(2)}, u32[]{:S(2)}) %collective-permute-start.1) | collective-permute-done | bytes 184352 | tf_op jit(solution)/shard_map/ppermute | solution.py:484
  19.1 2.1 %collective-permute-start.4 = (bf16[48,640]{1,0:T(8,128)(2,1)S(1)}, bf16[48,640]{1,0:T(8,128)(2,1)S(1)}, u32[]{:S(2)}, u32[]{:S(2)}) collective-permute-start(bf16[48,640]{1,0:T(8,128)(2,1)S(1)} %get-tuple-element.27), channel_id=1, source_target_pairs={{0,160},{16,176},{32,192},{48,208},{64,224},{80,240},{96,0},{112,1... | collective-permute-start | bytes 184328 | tf_op jit(solution)/shard_map/ppermute | solution.py:488
  21.3 1.2 %collective-permute-start.3 = (bf16[48,640]{1,0:T(8,128)(2,1)S(1)}, bf16[48,640]{1,0:T(8,128)(2,1)S(1)}, u32[]{:S(2)}, u32[]{:S(2)}) collective-permute-start(bf16[48,640]{1,0:T(8,128)(2,1)S(1)} %get-tuple-element.25._), channel_id=1, source_target_pairs={{0,64},{16,80},{32,96},{48,112},{64,128},{80,144},{96,160},{112,17... | collective-permute-start | bytes 184328 | tf_op jit(solution)/shard_map/ppermute | solution.py:487
  22.5 2.1 %side.1 = (f32[6,384]{1,0:T(8,128)}, bf16[2,56,96]{2,1,0:T(8,128)(2,1)S(1)}, bf16[56,96]{1,0:T(8,128)(2,1)S(1)}, bf16[128,48]{1,0:T(8,128)(2,1)S(1)}, f32[48,128]{1,0:T(8,128)S(1)}) custom-call(s32[1]{0:T(128)} %bitcast.ctx_ref, s32[4,96]{1,0:T(4,128)S(1)} %bitcast.14, f32[4,96]{1,0:T(4,128)S(1)} %bitcast.15, bf16[6,64,128]{2,1,0:T(8,128)(2,1)S(1)} %copy-done.4, ...), custom_call_target="tpu_custom_call" | custom-call | tf_op jit(solution)/shard_map/side/pallas_call | solution.py:202
  24.5 2.0 %collective-permute-done.4.far_above_ref = bf16[48,640]{1,0:T(8,128)(2,1)S(1)} collective-permute-done((bf16[48,640]{1,0:T(8,128)(2,1)S(1)}, bf16[48,640]{1,0:T(8,128)(2,1)S(1)}, u32[]{:S(2)}, u32[]{:S(2)}) %collective-permute-start.4) | collective-permute-done | bytes 61472 | tf_op jit(solution)/shard_map/ppermute | solution.py:488
  26.5 0.7 collective-permute-done.3.far_below_ref
  27.8 14.3 %all_to_all.20.values_ref = bf16[16,16,512]{2,1,0:T(8,128)(2,1)S(1)} all-to-all(bf16[16,16,512]{2,1,0:T(8,128)(2,1)S(1)} %values.1), channel_id=1, replica_groups=mesh['ctx'=16,'exp'=16] {'exp'}, dimensions={0} | all-to-all | bytes 524288 | tf_op jit(solution)/shard_map/all_to_all | solution.py:493
  42.6 3.9 %collective-permute-start.5 = (bf16[336,128]{1,0:T(8,128)(2,1)S(1)}, bf16[336,128]{1,0:T(8,128)(2,1)S(1)}, u32[]{:S(2)}, u32[]{:S(2)}) collective-permute-start(bf16[336,128]{1,0:T(8,128)(2,1)S(1)} %project.1), channel_id=1, source_target_pairs={{0,16},{16,0},{32,48},{48,32},{64,80},{80,64},{96,112},{112,96},{1... | collective-permute-start | bytes 258056 | tf_op jit(solution)/shard_map/ppermute | solution.py:495
  46.5 0.9 collective-permute-done.5
  47.4 0.7 collective-permute-start.7
  48.2 2.0 %collective-permute-start.6 = (bf16[336,128]{1,0:T(8,128)(2,1)S(1)}, bf16[336,128]{1,0:T(8,128)(2,1)S(1)}, u32[]{:S(2)}, u32[]{:S(2)}) collective-permute-start(bf16[336,128]{1,0:T(8,128)(2,1)S(1)} %add_convert_fusion.own_ref), channel_id=1, source_target_pairs={{0,224},{16,240},{32,0},{48,16},{64,32},{80,48},{96,64},{112,80},{... | collective-permute-start | bytes 258056 | tf_op jit(solution)/shard_map/ppermute | solution.py:497
  50.2 2.3 %collective-permute-done.7.below_ref = bf16[336,128]{1,0:T(8,128)(2,1)S(1)} collective-permute-done((bf16[336,128]{1,0:T(8,128)(2,1)S(1)}, bf16[336,128]{1,0:T(8,128)(2,1)S(1)}, u32[]{:S(2)}, u32[]{:S(2)}) %collective-permute-start.7) | collective-permute-done | bytes 86048 | tf_op jit(solution)/shard_map/ppermute | solution.py:498
  52.8 1.4 %collective-permute-start.8 = (bf16[200,128]{1,0:T(8,128)(2,1)S(1)}, bf16[200,128]{1,0:T(8,128)(2,1)S(1)}, u32[]{:S(2)}, u32[]{:S(2)}) collective-permute-start(bf16[200,128]{1,0:T(8,128)(2,1)S(1)} %get-tuple-element.31), channel_id=1, source_target_pairs={{0,160},{16,176},{32,192},{48,208},{64,224},{80,240},{96,0},{112,1... | collective-permute-start | bytes 153608 | tf_op jit(solution)/shard_map/ppermute | solution.py:500
  54.2 3.0 %collective-permute-start.9 = (bf16[200,128]{1,0:T(8,128)(2,1)S(1)}, bf16[200,128]{1,0:T(8,128)(2,1)S(1)}, u32[]{:S(2)}, u32[]{:S(2)}) collective-permute-start(bf16[200,128]{1,0:T(8,128)(2,1)S(1)} %get-tuple-element.32), channel_id=1, source_target_pairs={{0,64},{16,80},{32,96},{48,112},{64,128},{80,144},{96,160},{112,17... | collective-permute-start | bytes 153608 | tf_op jit(solution)/shard_map/ppermute | solution.py:501
  57.2 2.0 %base.1 = (f32[56,448]{1,0:T(8,128)S(1)}, bf16[448,4096]{1,0:T(8,128)(2,1)S(1)}) custom-call(bf16[336,128]{1,0:T(8,128)(2,1)S(1)} %add_convert_fusion.own_ref, bf16[336,128]{1,0:T(8,128)(2,1)S(1)} %collective-permute-done.6.above_ref, bf16[336,128]{1,0:T(8,128)(2,1)S(1)} %collective-permute-done.7.below_ref, bf16[96,448]{1,0:T(8,128)(2,1)S(1)} %copy-done.5, ...), custom_call_target="tpu_custom_call" | custom-call | tf_op jit(solution)/shard_map/base/pallas_call | solution.py:356
  60.2 11.3 %all_to_all.21.parts_ref = bf16[16,56,256]{2,1,0:T(8,128)(2,1)S(1)} all-to-all(bf16[16,56,256]{2,1,0:T(8,128)(2,1)S(1)} %get-tuple-element.34), channel_id=1, replica_groups=mesh['ctx'=16,'exp'=16] {'exp'}, dimensions={0} | all-to-all | bytes 917504 | tf_op jit(solution)/shard_map/all_to_all | solution.py:504
  71.7 9.8 %all_to_all.22.act_ref = bf16[16,48,128]{2,1,0:T(8,128)(2,1)S(1)} all-to-all(bf16[16,48,128]{2,1,0:T(8,128)(2,1)S(1)} %activation.1), channel_id=1, replica_groups=mesh['ctx'=16,'exp'=16] {'exp'}, dimensions={0} | all-to-all | bytes 393216 | tf_op jit(solution)/shard_map/all_to_all | solution.py:505
  81.4 0.9 expert_out.1
  82.3 19.2 %all_to_all.23.parts_ref = bf16[16,16,256]{2,1,0:T(8,128)(2,1)S(1)} all-to-all(bf16[16,16,256]{2,1,0:T(8,128)(2,1)S(1)} %expert_out.1), channel_id=1, replica_groups=mesh['ctx'=16,'exp'=16] {'ctx'}, dimensions={0} | all-to-all | bytes 262144 | tf_op jit(solution)/shard_map/all_to_all | solution.py:507
  (33 shorter events, 3.7 us)
Async XLA Ops:
  0.6 21.8 %copy-start.9 = (f32[96,4]{0,1:T(4,128)S(1)}, f32[96,4]{0,1:T(4,128)}, u32[]{:S(2)}) copy-start(f32[96,4]{0,1:T(4,128)} %param.25) | copy-start | bytes 4612
  0.6 21.8 %copy-start.8 = (s32[96,4]{0,1:T(4,128)S(1)}, s32[96,4]{0,1:T(4,128)}, u32[]{:S(2)}) copy-start(s32[96,4]{0,1:T(4,128)} %param.24) | copy-start | bytes 4612
  0.7 21.8 %copy-start.6 = (f32[6,64]{1,0:T(8,128)S(1)}, f32[6,64]{1,0:T(8,128)}, u32[]{:S(2)}) copy-start(f32[6,64]{1,0:T(8,128)} %iw_ref.1) | copy-start | bytes 4612
  0.7 21.8 %copy-start.4 = (bf16[6,64,128]{2,1,0:T(8,128)(2,1)S(1)}, bf16[6,64,128]{2,1,0:T(8,128)(2,1)}, u32[]{:S(2)}) copy-start(bf16[6,64,128]{2,1,0:T(8,128)(2,1)} %iq_ref.1) | copy-start | bytes 294916
  0.7 21.8 %copy-start.3 = (bf16[6,384,128]{2,1,0:T(8,128)(2,1)S(1)}, bf16[6,384,128]{2,1,0:T(8,128)(2,1)}, u32[]{:S(2)}) copy-start(bf16[6,384,128]{2,1,0:T(8,128)(2,1)} %keys_ref.1) | copy-start | bytes 1769476
  0.7 26.6 %copy-start.1 = (bf16[8,512,128]{2,1,0:T(8,128)(2,1)S(1)}, bf16[8,512,128]{2,1,0:T(8,128)(2,1)}, u32[]{:S(2)}) copy-start(bf16[8,512,128]{2,1,0:T(8,128)(2,1)} %w_ref.1) | copy-start | bytes 3145732
  5.1 37.0 %copy-start.2 = (bf16[1024,448]{0,1:T(8,128)(2,1)S(1)}, bf16[1024,448]{0,1:T(8,128)(2,1)}, u32[]{:S(2)}) copy-start(bf16[1024,448]{0,1:T(8,128)(2,1)} %param.21) | copy-start | bytes 2752516
  5.1 4.8 %collective-permute-start = (bf16[8,48,640]{2,1,0:T(8,128)(2,1)S(1)}, bf16[8,48,640]{2,1,0:T(8,128)(2,1)S(1)}, u32[]{:S(2)}, u32[]{:S(2)}) collective-permute-start(bf16[8,48,640]{2,1,0:T(8,128)(2,1)S(1)} %get-tuple-element.21), channel_id=1, source_target_pairs={{0,16},{16,0},{32,48},{48,32},{64,80},{80,64},{96,112},{112,96},{1... | collective-permute-start | bytes 1474568 | tf_op jit(solution)/shard_map/ppermute | solution.py:482
  9.9 47.3 %copy-start.5 = (bf16[96,448]{1,0:T(8,128)(2,1)S(1)}, bf16[96,448]{1,0:T(8,128)(2,1)}, u32[]{:S(2)}) copy-start(bf16[96,448]{1,0:T(8,128)(2,1)} %hidden_ref.1) | copy-start | bytes 258052
  10.3 8.6 %collective-permute-start.1 = (bf16[3,48,640]{2,1,0:T(8,128)(2,1)S(1)}, bf16[3,48,640]{2,1,0:T(8,128)(2,1)S(1)}, u32[]{:S(2)}, u32[]{:S(2)}) collective-permute-start(bf16[3,48,640]{2,1,0:T(8,128)(2,1)S(1)} %get-tuple-element.23), channel_id=1, source_target_pairs={{0,32},{16,48},{32,64},{48,80},{64,96},{80,112},{96,128},{112,144}... | collective-permute-start | bytes 552968 | tf_op jit(solution)/shard_map/ppermute | solution.py:484
  10.4 6.3 %collective-permute-start.2 = (bf16[2,48,640]{2,1,0:T(8,128)(2,1)S(1)}, bf16[2,48,640]{2,1,0:T(8,128)(2,1)S(1)}, u32[]{:S(2)}, u32[]{:S(2)}) collective-permute-start(bf16[2,48,640]{2,1,0:T(8,128)(2,1)S(1)} %get-tuple-element.24), channel_id=1, source_target_pairs={{0,224},{16,240},{32,0},{48,16},{64,32},{80,48},{96,64},{112,80},{... | collective-permute-start | bytes 368648 | tf_op jit(solution)/shard_map/ppermute | solution.py:485
  19.1 7.4 %collective-permute-start.4 = (bf16[48,640]{1,0:T(8,128)(2,1)S(1)}, bf16[48,640]{1,0:T(8,128)(2,1)S(1)}, u32[]{:S(2)}, u32[]{:S(2)}) collective-permute-start(bf16[48,640]{1,0:T(8,128)(2,1)S(1)} %get-tuple-element.27), channel_id=1, source_target_pairs={{0,160},{16,176},{32,192},{48,208},{64,224},{80,240},{96,0},{112,1... | collective-permute-start | bytes 184328 | tf_op jit(solution)/shard_map/ppermute | solution.py:488
  21.3 6.0 %collective-permute-start.3 = (bf16[48,640]{1,0:T(8,128)(2,1)S(1)}, bf16[48,640]{1,0:T(8,128)(2,1)S(1)}, u32[]{:S(2)}, u32[]{:S(2)}) collective-permute-start(bf16[48,640]{1,0:T(8,128)(2,1)S(1)} %get-tuple-element.25._), channel_id=1, source_target_pairs={{0,64},{16,80},{32,96},{48,112},{64,128},{80,144},{96,160},{112,17... | collective-permute-start | bytes 184328 | tf_op jit(solution)/shard_map/ppermute | solution.py:487
  27.8 31.7 %copy-start.7 = (f32[448]{0:T(512)S(1)}, f32[448]{0:T(512)}, u32[]{:S(2)}) copy-start(f32[448]{0:T(512)} %param.23) | copy-start | bytes 5380
  42.6 4.8 %collective-permute-start.5 = (bf16[336,128]{1,0:T(8,128)(2,1)S(1)}, bf16[336,128]{1,0:T(8,128)(2,1)S(1)}, u32[]{:S(2)}, u32[]{:S(2)}) collective-permute-start(bf16[336,128]{1,0:T(8,128)(2,1)S(1)} %project.1), channel_id=1, source_target_pairs={{0,16},{16,0},{32,48},{48,32},{64,80},{80,64},{96,112},{112,96},{1... | collective-permute-start | bytes 258056 | tf_op jit(solution)/shard_map/ppermute | solution.py:495
  47.4 5.1 %collective-permute-start.7 = (bf16[336,128]{1,0:T(8,128)(2,1)S(1)}, bf16[336,128]{1,0:T(8,128)(2,1)S(1)}, u32[]{:S(2)}, u32[]{:S(2)}) collective-permute-start(bf16[336,128]{1,0:T(8,128)(2,1)S(1)} %add_convert_fusion.own_ref), channel_id=1, source_target_pairs={{0,32},{16,48},{32,64},{48,80},{64,96},{80,112},{96,128},{112,144}... | collective-permute-start | bytes 258056 | tf_op jit(solution)/shard_map/ppermute | solution.py:498
  48.2 4.3 %collective-permute-start.6 = (bf16[336,128]{1,0:T(8,128)(2,1)S(1)}, bf16[336,128]{1,0:T(8,128)(2,1)S(1)}, u32[]{:S(2)}, u32[]{:S(2)}) collective-permute-start(bf16[336,128]{1,0:T(8,128)(2,1)S(1)} %add_convert_fusion.own_ref), channel_id=1, source_target_pairs={{0,224},{16,240},{32,0},{48,16},{64,32},{80,48},{96,64},{112,80},{... | collective-permute-start | bytes 258056 | tf_op jit(solution)/shard_map/ppermute | solution.py:497
  52.8 6.5 %collective-permute-start.8 = (bf16[200,128]{1,0:T(8,128)(2,1)S(1)}, bf16[200,128]{1,0:T(8,128)(2,1)S(1)}, u32[]{:S(2)}, u32[]{:S(2)}) collective-permute-start(bf16[200,128]{1,0:T(8,128)(2,1)S(1)} %get-tuple-element.31), channel_id=1, source_target_pairs={{0,160},{16,176},{32,192},{48,208},{64,224},{80,240},{96,0},{112,1... | collective-permute-start | bytes 153608 | tf_op jit(solution)/shard_map/ppermute | solution.py:500
  54.2 5.3 %collective-permute-start.9 = (bf16[200,128]{1,0:T(8,128)(2,1)S(1)}, bf16[200,128]{1,0:T(8,128)(2,1)S(1)}, u32[]{:S(2)}, u32[]{:S(2)}) collective-permute-start(bf16[200,128]{1,0:T(8,128)(2,1)S(1)} %get-tuple-element.32), channel_id=1, source_target_pairs={{0,64},{16,80},{32,96},{48,112},{64,128},{80,144},{96,160},{112,17... | collective-permute-start | bytes 153608 | tf_op jit(solution)/shard_map/ppermute | solution.py:501
  59.2 22.2 %copy-start = (bf16[1,2048,448]{1,2,0:T(8,128)(2,1)S(1)}, bf16[1,2048,448]{1,2,0:T(8,128)(2,1)}, u32[]{:S(2)}) copy-start(bf16[1,2048,448]{1,2,0:T(8,128)(2,1)} %param.27) | copy-start | bytes 5505028

commit v5 on v4

--- a/solution.py
+++ b/solution.py
@@ -102,42 +102,47 @@
 
     start(0)
     load_blocks.start()
-    for r in range(1, 4):
+    for r in range(1, 3):
         start(r)
     ctx = ctx_ref[0]
     core = lax.rem(ctx, 2)
     per = tokens // BLOCK
-    mask = None
-    for r in range(0, rows, 2):
-        for i in range(r, r + 2):
-            for copy in copies[i]:
-                copy.wait()
-            if i + 4 < rows:
-                start(i + 4)
-        if mask is None:
-            load_blocks.wait()
-            block_of = iota((rows, tokens), 1) // BLOCK
-            mask = jnp.zeros((rows, tokens), f32)
-            picked = blocks_ref[...]
-            for b in range(per):
-                hit = jnp.max(jnp.where(picked == ctx * per + b, 1.0, 0.0), axis=1, keepdims=True)
-                mask = jnp.where(block_of == b, hit, mask)
-        mine, other = [], []
-        for i in range(r, r + 2):
-            chosen = mask[i : i + 1, :] > 0.0
-            keys = cache_ref[i]
-            scores = dot(query_ref[i], keys, ((0,), (0,))) * SCORE_SCALE
-            masked = jnp.where(chosen, scores, NEG)
-            peak = jnp.max(masked, axis=1, keepdims=True)
-            expo = jnp.where(chosen, jnp.exp(masked - peak), 0.0)
-            total = jnp.sum(expo, axis=1, keepdims=True)
-            weighted = dot(expo.astype(bf16), keys[:LAT], ((1,), (1,)))
-            wide = jnp.concatenate([weighted, stats_tile(peak, total)], axis=1)
-            wide = wide.reshape(8, 2, 8, WIDE)
-            mine.append(jnp.where(core == 0, wide[:, 0], wide[:, 1]))
-            other.append(jnp.where(core == 0, wide[:, 1], wide[:, 0]))
-        mine_ref[:, 8 * r : 8 * r + 16, :] = jnp.concatenate(mine, axis=1)
-        other_ref[:, 8 * r : 8 * r + 16, :] = jnp.concatenate(other, axis=1).astype(bf16)
+
+    def scores_of(i):
+        for copy in copies[i]:
+            copy.wait()
+        if i + 3 < rows:
+            start(i + 3)
+        return dot(query_ref[i], cache_ref[i], ((0,), (0,))) * SCORE_SCALE
+
+    def partial(i, scores, mask):
+        chosen = mask[i : i + 1, :] > 0.0
+        masked = jnp.where(chosen, scores, NEG)
+        peak = jnp.max(masked, axis=1, keepdims=True)
+        expo = jnp.where(chosen, jnp.exp(masked - peak), 0.0)
+        total = jnp.sum(expo, axis=1, keepdims=True)
+        weighted = dot(expo.astype(bf16), cache_ref[i, :LAT], ((1,), (1,)))
+        wide = jnp.concatenate([weighted, stats_tile(peak, total)], axis=1).reshape(8, 2, 8, WIDE)
+        return jnp.where(core == 0, wide[:, 0], wide[:, 1]), jnp.where(core == 0, wide[:, 1], wide[:, 0])
+
+    scores = scores_of(0)
+    load_blocks.wait()
+    block_of = iota((rows, tokens), 1) // BLOCK
+    mask = jnp.zeros((rows, tokens), f32)
+    picked = blocks_ref[...]
+    for b in range(per):
+        hit = jnp.max(jnp.where(picked == ctx * per + b, 1.0, 0.0), axis=1, keepdims=True)
+        mask = jnp.where(block_of == b, hit, mask)
+    for i in range(rows):
+        later = scores_of(i + 1) if i + 1 < rows else None
+        mine, other = partial(i, scores, mask)
+        if i % 2 == 0:
+            mine_even, other_even = mine, other
+        else:
+            lines = slice(8 * i - 8, 8 * i + 8)
+            mine_ref[:, lines, :] = jnp.concatenate([mine_even, mine], axis=1)
+            other_ref[:, lines, :] = jnp.concatenate([other_even, other], axis=1).astype(bf16)
+        scores = later
 
 
 def attention(ctx, blocks, query, cache):

time: 102 us -> 102 us (level)
  no operation moved by 1% of the time
where the time goes in v5:
time: 102 us
  blocking collectives  54.7 us (54%)
  starting transfers between devices  21.7 us (21%)
  Pallas kernels  12.3 us (12%)
  waiting for transfers between devices  12.3 us (12%)
    all_to_all x1, blocking collectives, local(): outs = lax.all_to_all(outs, 'ctx', 0, 0)  19.2 us
    all_to_all x1, blocking collectives, local(): vals = lax.all_to_all(vals, 'exp', 0, 0)  14.3 us
    all_to_all x1, blocking collectives, local(): terms = lax.all_to_all(terms, 'exp', 0, 0)  11.3 us
    all_to_all x1, blocking collectives, local(): act = lax.all_to_all(activation(terms), 'exp', 0, 0)  9.78 us
    pallas_call x1, Pallas kernels, attention(): pl.pallas_call(attention_kernel, in_specs=[SMEM, HBM, HBM, HBM], out_spec...  4.05 us
    ppermute x1, starting transfers between devices, local(): above = lax.ppermute(down, 'ctx', along_z(-2))  3.92 us
    ppermute x1, starting transfers between devices, local(): own = part.astype(f32) + lax.ppermute(part, 'ctx', other_core).astype(f32)  3.9 us
    ppermute x1, starting transfers between devices, local(): other = lax.ppermute(other, 'ctx', other_core)  3.32 us
  transfers between devices with their start and end apart: 10, of which 8 were waited for; matrix products, arithmetic and copies ran while one was open for 0% of the time, Pallas kernels for 4%

profile of v5, /device:TPU:1, one launch (start us, length us, event | category | flops | bytes accessed | tf_op | source)
XLA Modules:
  0.0 101.8 jit_solution(16215095773299951886)
XLA Ops:
  0.7 4.0 %attention.1 = (f32[8,48,640]{2,1,0:T(8,128)S(1)}, bf16[8,48,640]{2,1,0:T(8,128)(2,1)S(1)}) custom-call(s32[1]{0:T(128)} %bitcast.ctx_ref, s32[6,32]{1,0:T(8,128)} %blocks_hbm.1, bf16[6,576,128]{2,1,0:T(8,128)(2,1)} %bitcast.18, bf16[6,576,384]{2,1,0:T(8,128)(2,1)} %bitcast.17), custom_call_target="tpu_custom_call" | custom-call | tf_op jit(solution)/shard_map/attention/pallas_call | solution.py:150
  4.8 3.3 %collective-permute-start = (bf16[8,48,640]{2,1,0:T(8,128)(2,1)S(1)}, bf16[8,48,640]{2,1,0:T(8,128)(2,1)S(1)}, u32[]{:S(2)}, u32[]{:S(2)}) collective-permute-start(bf16[8,48,640]{2,1,0:T(8,128)(2,1)S(1)} %get-tuple-element.21), channel_id=1, source_target_pairs={{0,16},{16,0},{32,48},{48,32},{64,80},{80,64},{96,112},{112,96},{1... | collective-permute-start | bytes 1474568 | tf_op jit(solution)/shard_map/ppermute | solution.py:487
  8.1 1.5 %collective-permute-done.other_ref = bf16[8,48,640]{2,1,0:T(8,128)(2,1)S(1)} collective-permute-done((bf16[8,48,640]{2,1,0:T(8,128)(2,1)S(1)}, bf16[8,48,640]{2,1,0:T(8,128)(2,1)S(1)}, u32[]{:S(2)}, u32[]{:S(2)}) %collective-permute-start) | collective-permute-done | bytes 491552 | tf_op jit(solution)/shard_map/ppermute | solution.py:487
  10.1 3.9 %collective-permute-start.2 = (bf16[2,48,640]{2,1,0:T(8,128)(2,1)S(1)}, bf16[2,48,640]{2,1,0:T(8,128)(2,1)S(1)}, u32[]{:S(2)}, u32[]{:S(2)}) collective-permute-start(bf16[2,48,640]{2,1,0:T(8,128)(2,1)S(1)} %get-tuple-element.24), channel_id=1, source_target_pairs={{0,224},{16,240},{32,0},{48,16},{64,32},{80,48},{96,64},{112,80},{... | collective-permute-start | bytes 368648 | tf_op jit(solution)/shard_map/ppermute | solution.py:490
  14.0 2.3 %collective-permute-done.2.above_ref = bf16[2,48,640]{2,1,0:T(8,128)(2,1)S(1)} collective-permute-done((bf16[2,48,640]{2,1,0:T(8,128)(2,1)S(1)}, bf16[2,48,640]{2,1,0:T(8,128)(2,1)S(1)}, u32[]{:S(2)}, u32[]{:S(2)}) %collective-permute-start.2) | collective-permute-done | bytes 122912 | tf_op jit(solution)/shard_map/ppermute | solution.py:490
  16.3 2.3 %collective-permute-done.1.below_ref = bf16[3,48,640]{2,1,0:T(8,128)(2,1)S(1)} collective-permute-done((bf16[3,48,640]{2,1,0:T(8,128)(2,1)S(1)}, bf16[3,48,640]{2,1,0:T(8,128)(2,1)S(1)}, u32[]{:S(2)}, u32[]{:S(2)}) %collective-permute-start.1) | collective-permute-done | bytes 184352 | tf_op jit(solution)/shard_map/ppermute | solution.py:489
  18.8 2.1 %collective-permute-start.4 = (bf16[48,640]{1,0:T(8,128)(2,1)S(1)}, bf16[48,640]{1,0:T(8,128)(2,1)S(1)}, u32[]{:S(2)}, u32[]{:S(2)}) collective-permute-start(bf16[48,640]{1,0:T(8,128)(2,1)S(1)} %get-tuple-element.27), channel_id=1, source_target_pairs={{0,160},{16,176},{32,192},{48,208},{64,224},{80,240},{96,0},{112,1... | collective-permute-start | bytes 184328 | tf_op jit(solution)/shard_map/ppermute | solution.py:493
  20.9 1.2 %collective-permute-start.3 = (bf16[48,640]{1,0:T(8,128)(2,1)S(1)}, bf16[48,640]{1,0:T(8,128)(2,1)S(1)}, u32[]{:S(2)}, u32[]{:S(2)}) collective-permute-start(bf16[48,640]{1,0:T(8,128)(2,1)S(1)} %get-tuple-element.25._), channel_id=1, source_target_pairs={{0,64},{16,80},{32,96},{48,112},{64,128},{80,144},{96,160},{112,17... | collective-permute-start | bytes 184328 | tf_op jit(solution)/shard_map/ppermute | solution.py:492
  22.1 2.0 %side.1 = (f32[6,384]{1,0:T(8,128)}, bf16[2,56,96]{2,1,0:T(8,128)(2,1)S(1)}, bf16[56,96]{1,0:T(8,128)(2,1)S(1)}, bf16[128,48]{1,0:T(8,128)(2,1)S(1)}, f32[48,128]{1,0:T(8,128)S(1)}) custom-call(s32[1]{0:T(128)} %bitcast.ctx_ref, s32[4,96]{1,0:T(4,128)S(1)} %bitcast.14, f32[4,96]{1,0:T(4,128)S(1)} %bitcast.15, bf16[6,64,128]{2,1,0:T(8,128)(2,1)S(1)} %copy-done.4, ...), custom_call_target="tpu_custom_call" | custom-call | tf_op jit(solution)/shard_map/side/pallas_call | solution.py:207
  24.2 2.0 %collective-permute-done.4.far_above_ref = bf16[48,640]{1,0:T(8,128)(2,1)S(1)} collective-permute-done((bf16[48,640]{1,0:T(8,128)(2,1)S(1)}, bf16[48,640]{1,0:T(8,128)(2,1)S(1)}, u32[]{:S(2)}, u32[]{:S(2)}) %collective-permute-start.4) | collective-permute-done | bytes 61472 | tf_op jit(solution)/shard_map/ppermute | solution.py:493
  26.2 0.7 collective-permute-done.3.far_below_ref
  27.5 14.3 %all_to_all.20.values_ref = bf16[16,16,512]{2,1,0:T(8,128)(2,1)S(1)} all-to-all(bf16[16,16,512]{2,1,0:T(8,128)(2,1)S(1)} %values.1), channel_id=1, replica_groups=mesh['ctx'=16,'exp'=16] {'exp'}, dimensions={0} | all-to-all | bytes 524288 | tf_op jit(solution)/shard_map/all_to_all | solution.py:498
  42.3 3.9 %collective-permute-start.5 = (bf16[336,128]{1,0:T(8,128)(2,1)S(1)}, bf16[336,128]{1,0:T(8,128)(2,1)S(1)}, u32[]{:S(2)}, u32[]{:S(2)}) collective-permute-start(bf16[336,128]{1,0:T(8,128)(2,1)S(1)} %project.1), channel_id=1, source_target_pairs={{0,16},{16,0},{32,48},{48,32},{64,80},{80,64},{96,112},{112,96},{1... | collective-permute-start | bytes 258056 | tf_op jit(solution)/shard_map/ppermute | solution.py:500
  46.2 0.9 collective-permute-done.5
  47.1 0.8 collective-permute-start.7
  47.9 2.0 %collective-permute-start.6 = (bf16[336,128]{1,0:T(8,128)(2,1)S(1)}, bf16[336,128]{1,0:T(8,128)(2,1)S(1)}, u32[]{:S(2)}, u32[]{:S(2)}) collective-permute-start(bf16[336,128]{1,0:T(8,128)(2,1)S(1)} %add_convert_fusion.own_ref), channel_id=1, source_target_pairs={{0,224},{16,240},{32,0},{48,16},{64,32},{80,48},{96,64},{112,80},{... | collective-permute-start | bytes 258056 | tf_op jit(solution)/shard_map/ppermute | solution.py:502
  49.9 2.3 %collective-permute-done.7.below_ref = bf16[336,128]{1,0:T(8,128)(2,1)S(1)} collective-permute-done((bf16[336,128]{1,0:T(8,128)(2,1)S(1)}, bf16[336,128]{1,0:T(8,128)(2,1)S(1)}, u32[]{:S(2)}, u32[]{:S(2)}) %collective-permute-start.7) | collective-permute-done | bytes 86048 | tf_op jit(solution)/shard_map/ppermute | solution.py:503
  52.5 1.4 %collective-permute-start.8 = (bf16[200,128]{1,0:T(8,128)(2,1)S(1)}, bf16[200,128]{1,0:T(8,128)(2,1)S(1)}, u32[]{:S(2)}, u32[]{:S(2)}) collective-permute-start(bf16[200,128]{1,0:T(8,128)(2,1)S(1)} %get-tuple-element.31), channel_id=1, source_target_pairs={{0,160},{16,176},{32,192},{48,208},{64,224},{80,240},{96,0},{112,1... | collective-permute-start | bytes 153608 | tf_op jit(solution)/shard_map/ppermute | solution.py:505
  53.9 3.0 %collective-permute-start.9 = (bf16[200,128]{1,0:T(8,128)(2,1)S(1)}, bf16[200,128]{1,0:T(8,128)(2,1)S(1)}, u32[]{:S(2)}, u32[]{:S(2)}) collective-permute-start(bf16[200,128]{1,0:T(8,128)(2,1)S(1)} %get-tuple-element.32), channel_id=1, source_target_pairs={{0,64},{16,80},{32,96},{48,112},{64,128},{80,144},{96,160},{112,17... | collective-permute-start | bytes 153608 | tf_op jit(solution)/shard_map/ppermute | solution.py:506
  56.9 2.0 %base.1 = (f32[56,448]{1,0:T(8,128)S(1)}, bf16[448,4096]{1,0:T(8,128)(2,1)S(1)}) custom-call(bf16[336,128]{1,0:T(8,128)(2,1)S(1)} %add_convert_fusion.own_ref, bf16[336,128]{1,0:T(8,128)(2,1)S(1)} %collective-permute-done.6.above_ref, bf16[336,128]{1,0:T(8,128)(2,1)S(1)} %collective-permute-done.7.below_ref, bf16[96,448]{1,0:T(8,128)(2,1)S(1)} %copy-done.5, ...), custom_call_target="tpu_custom_call" | custom-call | tf_op jit(solution)/shard_map/base/pallas_call | solution.py:361
  59.9 11.3 %all_to_all.21.parts_ref = bf16[16,56,256]{2,1,0:T(8,128)(2,1)S(1)} all-to-all(bf16[16,56,256]{2,1,0:T(8,128)(2,1)S(1)} %get-tuple-element.34), channel_id=1, replica_groups=mesh['ctx'=16,'exp'=16] {'exp'}, dimensions={0} | all-to-all | bytes 917504 | tf_op jit(solution)/shard_map/all_to_all | solution.py:509
  71.3 9.8 %all_to_all.22.act_ref = bf16[16,48,128]{2,1,0:T(8,128)(2,1)S(1)} all-to-all(bf16[16,48,128]{2,1,0:T(8,128)(2,1)S(1)} %activation.1), channel_id=1, replica_groups=mesh['ctx'=16,'exp'=16] {'exp'}, dimensions={0} | all-to-all | bytes 393216 | tf_op jit(solution)/shard_map/all_to_all | solution.py:510
  81.1 0.9 expert_out.1
  82.0 19.2 %all_to_all.23.parts_ref = bf16[16,16,256]{2,1,0:T(8,128)(2,1)S(1)} all-to-all(bf16[16,16,256]{2,1,0:T(8,128)(2,1)S(1)} %expert_out.1), channel_id=1, replica_groups=mesh['ctx'=16,'exp'=16] {'ctx'}, dimensions={0} | all-to-all | bytes 262144 | tf_op jit(solution)/shard_map/all_to_all | solution.py:512
  (33 shorter events, 3.7 us)
Async XLA Ops:
  0.6 21.5 %copy-start.9 = (f32[96,4]{0,1:T(4,128)S(1)}, f32[96,4]{0,1:T(4,128)}, u32[]{:S(2)}) copy-start(f32[96,4]{0,1:T(4,128)} %param.25) | copy-start | bytes 4612
  0.6 21.5 %copy-start.8 = (s32[96,4]{0,1:T(4,128)S(1)}, s32[96,4]{0,1:T(4,128)}, u32[]{:S(2)}) copy-start(s32[96,4]{0,1:T(4,128)} %param.24) | copy-start | bytes 4612
  0.7 21.5 %copy-start.6 = (f32[6,64]{1,0:T(8,128)S(1)}, f32[6,64]{1,0:T(8,128)}, u32[]{:S(2)}) copy-start(f32[6,64]{1,0:T(8,128)} %iw_ref.1) | copy-start | bytes 4612
  0.7 21.5 %copy-start.4 = (bf16[6,64,128]{2,1,0:T(8,128)(2,1)S(1)}, bf16[6,64,128]{2,1,0:T(8,128)(2,1)}, u32[]{:S(2)}) copy-start(bf16[6,64,128]{2,1,0:T(8,128)(2,1)} %iq_ref.1) | copy-start | bytes 294916
  0.7 21.5 %copy-start.3 = (bf16[6,384,128]{2,1,0:T(8,128)(2,1)S(1)}, bf16[6,384,128]{2,1,0:T(8,128)(2,1)}, u32[]{:S(2)}) copy-start(bf16[6,384,128]{2,1,0:T(8,128)(2,1)} %keys_ref.1) | copy-start | bytes 1769476
  0.7 26.2 %copy-start.1 = (bf16[8,512,128]{2,1,0:T(8,128)(2,1)S(1)}, bf16[8,512,128]{2,1,0:T(8,128)(2,1)}, u32[]{:S(2)}) copy-start(bf16[8,512,128]{2,1,0:T(8,128)(2,1)} %w_ref.1) | copy-start | bytes 3145732
  4.8 37.0 %copy-start.2 = (bf16[1024,448]{0,1:T(8,128)(2,1)S(1)}, bf16[1024,448]{0,1:T(8,128)(2,1)}, u32[]{:S(2)}) copy-start(bf16[1024,448]{0,1:T(8,128)(2,1)} %param.21) | copy-start | bytes 2752516
  4.8 4.8 %collective-permute-start = (bf16[8,48,640]{2,1,0:T(8,128)(2,1)S(1)}, bf16[8,48,640]{2,1,0:T(8,128)(2,1)S(1)}, u32[]{:S(2)}, u32[]{:S(2)}) collective-permute-start(bf16[8,48,640]{2,1,0:T(8,128)(2,1)S(1)} %get-tuple-element.21), channel_id=1, source_target_pairs={{0,16},{16,0},{32,48},{48,32},{64,80},{80,64},{96,112},{112,96},{1... | collective-permute-start | bytes 1474568 | tf_op jit(solution)/shard_map/ppermute | solution.py:487
  9.6 47.3 %copy-start.5 = (bf16[96,448]{1,0:T(8,128)(2,1)S(1)}, bf16[96,448]{1,0:T(8,128)(2,1)}, u32[]{:S(2)}) copy-start(bf16[96,448]{1,0:T(8,128)(2,1)} %hidden_ref.1) | copy-start | bytes 258052
  10.0 8.6 %collective-permute-start.1 = (bf16[3,48,640]{2,1,0:T(8,128)(2,1)S(1)}, bf16[3,48,640]{2,1,0:T(8,128)(2,1)S(1)}, u32[]{:S(2)}, u32[]{:S(2)}) collective-permute-start(bf16[3,48,640]{2,1,0:T(8,128)(2,1)S(1)} %get-tuple-element.23), channel_id=1, source_target_pairs={{0,32},{16,48},{32,64},{48,80},{64,96},{80,112},{96,128},{112,144}... | collective-permute-start | bytes 552968 | tf_op jit(solution)/shard_map/ppermute | solution.py:489
  10.1 6.3 %collective-permute-start.2 = (bf16[2,48,640]{2,1,0:T(8,128)(2,1)S(1)}, bf16[2,48,640]{2,1,0:T(8,128)(2,1)S(1)}, u32[]{:S(2)}, u32[]{:S(2)}) collective-permute-start(bf16[2,48,640]{2,1,0:T(8,128)(2,1)S(1)} %get-tuple-element.24), channel_id=1, source_target_pairs={{0,224},{16,240},{32,0},{48,16},{64,32},{80,48},{96,64},{112,80},{... | collective-permute-start | bytes 368648 | tf_op jit(solution)/shard_map/ppermute | solution.py:490
  18.8 7.4 %collective-permute-start.4 = (bf16[48,640]{1,0:T(8,128)(2,1)S(1)}, bf16[48,640]{1,0:T(8,128)(2,1)S(1)}, u32[]{:S(2)}, u32[]{:S(2)}) collective-permute-start(bf16[48,640]{1,0:T(8,128)(2,1)S(1)} %get-tuple-element.27), channel_id=1, source_target_pairs={{0,160},{16,176},{32,192},{48,208},{64,224},{80,240},{96,0},{112,1... | collective-permute-start | bytes 184328 | tf_op jit(solution)/shard_map/ppermute | solution.py:493
  20.9 6.0 %collective-permute-start.3 = (bf16[48,640]{1,0:T(8,128)(2,1)S(1)}, bf16[48,640]{1,0:T(8,128)(2,1)S(1)}, u32[]{:S(2)}, u32[]{:S(2)}) collective-permute-start(bf16[48,640]{1,0:T(8,128)(2,1)S(1)} %get-tuple-element.25._), channel_id=1, source_target_pairs={{0,64},{16,80},{32,96},{48,112},{64,128},{80,144},{96,160},{112,17... | collective-permute-start | bytes 184328 | tf_op jit(solution)/shard_map/ppermute | solution.py:492
  27.5 31.7 %copy-start.7 = (f32[448]{0:T(512)S(1)}, f32[448]{0:T(512)}, u32[]{:S(2)}) copy-start(f32[448]{0:T(512)} %param.23) | copy-start | bytes 5380
  42.3 4.8 %collective-permute-start.5 = (bf16[336,128]{1,0:T(8,128)(2,1)S(1)}, bf16[336,128]{1,0:T(8,128)(2,1)S(1)}, u32[]{:S(2)}, u32[]{:S(2)}) collective-permute-start(bf16[336,128]{1,0:T(8,128)(2,1)S(1)} %project.1), channel_id=1, source_target_pairs={{0,16},{16,0},{32,48},{48,32},{64,80},{80,64},{96,112},{112,96},{1... | collective-permute-start | bytes 258056 | tf_op jit(solution)/shard_map/ppermute | solution.py:500
  47.1 5.1 %collective-permute-start.7 = (bf16[336,128]{1,0:T(8,128)(2,1)S(1)}, bf16[336,128]{1,0:T(8,128)(2,1)S(1)}, u32[]{:S(2)}, u32[]{:S(2)}) collective-permute-start(bf16[336,128]{1,0:T(8,128)(2,1)S(1)} %add_convert_fusion.own_ref), channel_id=1, source_target_pairs={{0,32},{16,48},{32,64},{48,80},{64,96},{80,112},{96,128},{112,144}... | collective-permute-start | bytes 258056 | tf_op jit(solution)/shard_map/ppermute | solution.py:503
  47.9 4.3 %collective-permute-start.6 = (bf16[336,128]{1,0:T(8,128)(2,1)S(1)}, bf16[336,128]{1,0:T(8,128)(2,1)S(1)}, u32[]{:S(2)}, u32[]{:S(2)}) collective-permute-start(bf16[336,128]{1,0:T(8,128)(2,1)S(1)} %add_convert_fusion.own_ref), channel_id=1, source_target_pairs={{0,224},{16,240},{32,0},{48,16},{64,32},{80,48},{96,64},{112,80},{... | collective-permute-start | bytes 258056 | tf_op jit(solution)/shard_map/ppermute | solution.py:502
  52.5 6.5 %collective-permute-start.8 = (bf16[200,128]{1,0:T(8,128)(2,1)S(1)}, bf16[200,128]{1,0:T(8,128)(2,1)S(1)}, u32[]{:S(2)}, u32[]{:S(2)}) collective-permute-start(bf16[200,128]{1,0:T(8,128)(2,1)S(1)} %get-tuple-element.31), channel_id=1, source_target_pairs={{0,160},{16,176},{32,192},{48,208},{64,224},{80,240},{96,0},{112,1... | collective-permute-start | bytes 153608 | tf_op jit(solution)/shard_map/ppermute | solution.py:505
  53.9 5.2 %collective-permute-start.9 = (bf16[200,128]{1,0:T(8,128)(2,1)S(1)}, bf16[200,128]{1,0:T(8,128)(2,1)S(1)}, u32[]{:S(2)}, u32[]{:S(2)}) collective-permute-start(bf16[200,128]{1,0:T(8,128)(2,1)S(1)} %get-tuple-element.32), channel_id=1, source_target_pairs={{0,64},{16,80},{32,96},{48,112},{64,128},{80,144},{96,160},{112,17... | collective-permute-start | bytes 153608 | tf_op jit(solution)/shard_map/ppermute | solution.py:506
  58.9 22.2 %copy-start = (bf16[1,2048,448]{1,2,0:T(8,128)(2,1)S(1)}, bf16[1,2048,448]{1,2,0:T(8,128)(2,1)}, u32[]{:S(2)}) copy-start(bf16[1,2048,448]{1,2,0:T(8,128)(2,1)} %param.27) | copy-start | bytes 5505028

commit v6 on v5

--- a/solution.py
+++ b/solution.py
@@ -171,10 +171,11 @@
     ctx_ref, route_ref, gate_ref, iq_ref, iw_ref, keys_ref, _,
     score_ref, send_ref, pick_ref, back_ref, slot_ref,
 ):
-    rows = iq_ref.shape[0]
-    for r in range(rows):
+    scores = []
+    for r in range(iq_ref.shape[0]):
         raw = dot(iq_ref[r], keys_ref[r], ((1,), (1,))) * (iq_ref.shape[2] ** (-0.5))
-        score_ref[r : r + 1, :] = dot(iw_ref[r : r + 1, :], jnp.maximum(raw, 0.0), precision=HIGH)
+        scores.append(dot(iw_ref[r : r + 1, :], jnp.maximum(raw, 0.0), precision=HIGH))
+    score_ref[...] = jnp.concatenate(scores, axis=0)
     n = route_ref.shape[1]
     ctx = ctx_ref[0]
     n_ctx = n // 6
@@ -309,7 +310,7 @@
     acc = dot(low, w_ref[:, :512], ((1,), (1,))) + dot(high, w_ref[:, 512:], ((1,), (1,)))
     for e in range(n):
         acc_ref[6 * e : 6 * e + 6, :] = acc[8 * e : 8 * e + 6, :]
-    out_ref[...] = pack(acc_ref[...]).astype(bf16)
+    out_ref[...] = pack(acc_ref[: 6 * n, :]).astype(bf16)
 
 
 def project(vals, w_o):
@@ -319,7 +320,7 @@
         in_specs=[VMEM] * 2,
         out_specs=VMEM,
         out_shape=jax.ShapeDtypeStruct((packed_lines(shape[0]), 128), bf16),
-        scratch_shapes=[pltpu.VMEM(shape, f32)],
+        scratch_shapes=[pltpu.VMEM((shape[0] + 8, shape[1]), f32)],
         compiler_params=params(),
         name="project",
     )(vals, w_o)

time: 102 us -> 102 us (level)
  no operation moved by 1% of the time
where the time goes in v6:
time: 102 us
  blocking collectives  54.7 us (54%)
  starting transfers between devices  21.7 us (21%)
  Pallas kernels  12.3 us (12%)
  waiting for transfers between devices  12.3 us (12%)
    all_to_all x1, blocking collectives, local(): outs = lax.all_to_all(outs, 'ctx', 0, 0)  19.2 us
    all_to_all x1, blocking collectives, local(): vals = lax.all_to_all(vals, 'exp', 0, 0)  14.3 us
    all_to_all x1, blocking collectives, local(): terms = lax.all_to_all(terms, 'exp', 0, 0)  11.3 us
    all_to_all x1, blocking collectives, local(): act = lax.all_to_all(activation(terms), 'exp', 0, 0)  9.78 us
    pallas_call x1, Pallas kernels, attention(): pl.pallas_call(attention_kernel, in_specs=[SMEM, HBM, HBM, HBM], out_spec...  4.05 us
    ppermute x1, starting transfers between devices, local(): above = lax.ppermute(down, 'ctx', along_z(-2))  3.92 us
    ppermute x1, starting transfers between devices, local(): own = part.astype(f32) + lax.ppermute(part, 'ctx', other_core).astype(f32)  3.9 us
    ppermute x1, starting transfers between devices, local(): other = lax.ppermute(other, 'ctx', other_core)  3.32 us
  transfers between devices with their start and end apart: 10, of which 8 were waited for; matrix products, arithmetic and copies ran while one was open for 0% of the time, Pallas kernels for 4%

profile of v6, /device:TPU:1, one launch (start us, length us, event | category | flops | bytes accessed | tf_op | source)
XLA Modules:
  0.0 101.8 jit_solution(194792461925762198)
XLA Ops:
  0.7 4.0 %attention.1 = (f32[8,48,640]{2,1,0:T(8,128)S(1)}, bf16[8,48,640]{2,1,0:T(8,128)(2,1)S(1)}) custom-call(s32[1]{0:T(128)} %bitcast.ctx_ref, s32[6,32]{1,0:T(8,128)} %blocks_hbm.1, bf16[6,576,128]{2,1,0:T(8,128)(2,1)} %bitcast.18, bf16[6,576,384]{2,1,0:T(8,128)(2,1)} %bitcast.17), custom_call_target="tpu_custom_call" | custom-call | tf_op jit(solution)/shard_map/attention/pallas_call | solution.py:150
  4.8 3.3 %collective-permute-start = (bf16[8,48,640]{2,1,0:T(8,128)(2,1)S(1)}, bf16[8,48,640]{2,1,0:T(8,128)(2,1)S(1)}, u32[]{:S(2)}, u32[]{:S(2)}) collective-permute-start(bf16[8,48,640]{2,1,0:T(8,128)(2,1)S(1)} %get-tuple-element.21), channel_id=1, source_target_pairs={{0,16},{16,0},{32,48},{48,32},{64,80},{80,64},{96,112},{112,96},{1... | collective-permute-start | bytes 1474568 | tf_op jit(solution)/shard_map/ppermute | solution.py:488
  8.1 1.5 %collective-permute-done.other_ref = bf16[8,48,640]{2,1,0:T(8,128)(2,1)S(1)} collective-permute-done((bf16[8,48,640]{2,1,0:T(8,128)(2,1)S(1)}, bf16[8,48,640]{2,1,0:T(8,128)(2,1)S(1)}, u32[]{:S(2)}, u32[]{:S(2)}) %collective-permute-start) | collective-permute-done | bytes 491552 | tf_op jit(solution)/shard_map/ppermute | solution.py:488
  10.1 3.9 %collective-permute-start.2 = (bf16[2,48,640]{2,1,0:T(8,128)(2,1)S(1)}, bf16[2,48,640]{2,1,0:T(8,128)(2,1)S(1)}, u32[]{:S(2)}, u32[]{:S(2)}) collective-permute-start(bf16[2,48,640]{2,1,0:T(8,128)(2,1)S(1)} %get-tuple-element.24), channel_id=1, source_target_pairs={{0,224},{16,240},{32,0},{48,16},{64,32},{80,48},{96,64},{112,80},{... | collective-permute-start | bytes 368648 | tf_op jit(solution)/shard_map/ppermute | solution.py:491
  14.0 2.3 %collective-permute-done.2.above_ref = bf16[2,48,640]{2,1,0:T(8,128)(2,1)S(1)} collective-permute-done((bf16[2,48,640]{2,1,0:T(8,128)(2,1)S(1)}, bf16[2,48,640]{2,1,0:T(8,128)(2,1)S(1)}, u32[]{:S(2)}, u32[]{:S(2)}) %collective-permute-start.2) | collective-permute-done | bytes 122912 | tf_op jit(solution)/shard_map/ppermute | solution.py:491
  16.3 2.3 %collective-permute-done.1.below_ref = bf16[3,48,640]{2,1,0:T(8,128)(2,1)S(1)} collective-permute-done((bf16[3,48,640]{2,1,0:T(8,128)(2,1)S(1)}, bf16[3,48,640]{2,1,0:T(8,128)(2,1)S(1)}, u32[]{:S(2)}, u32[]{:S(2)}) %collective-permute-start.1) | collective-permute-done | bytes 184352 | tf_op jit(solution)/shard_map/ppermute | solution.py:490
  18.8 2.1 %collective-permute-start.4 = (bf16[48,640]{1,0:T(8,128)(2,1)S(1)}, bf16[48,640]{1,0:T(8,128)(2,1)S(1)}, u32[]{:S(2)}, u32[]{:S(2)}) collective-permute-start(bf16[48,640]{1,0:T(8,128)(2,1)S(1)} %get-tuple-element.27), channel_id=1, source_target_pairs={{0,160},{16,176},{32,192},{48,208},{64,224},{80,240},{96,0},{112,1... | collective-permute-start | bytes 184328 | tf_op jit(solution)/shard_map/ppermute | solution.py:494
  20.9 1.2 %collective-permute-start.3 = (bf16[48,640]{1,0:T(8,128)(2,1)S(1)}, bf16[48,640]{1,0:T(8,128)(2,1)S(1)}, u32[]{:S(2)}, u32[]{:S(2)}) collective-permute-start(bf16[48,640]{1,0:T(8,128)(2,1)S(1)} %get-tuple-element.25._), channel_id=1, source_target_pairs={{0,64},{16,80},{32,96},{48,112},{64,128},{80,144},{96,160},{112,17... | collective-permute-start | bytes 184328 | tf_op jit(solution)/shard_map/ppermute | solution.py:493
  22.1 2.0 %side.1 = (f32[6,384]{1,0:T(8,128)}, bf16[2,56,96]{2,1,0:T(8,128)(2,1)S(1)}, bf16[56,96]{1,0:T(8,128)(2,1)S(1)}, bf16[128,48]{1,0:T(8,128)(2,1)S(1)}, f32[48,128]{1,0:T(8,128)S(1)}) custom-call(s32[1]{0:T(128)} %bitcast.ctx_ref, s32[4,96]{1,0:T(4,128)S(1)} %bitcast.14, f32[4,96]{1,0:T(4,128)S(1)} %bitcast.15, bf16[6,64,128]{2,1,0:T(8,128)(2,1)S(1)} %copy-done.4, ...), custom_call_target="tpu_custom_call" | custom-call | tf_op jit(solution)/shard_map/side/pallas_call | solution.py:208
  24.2 2.0 %collective-permute-done.4.far_above_ref = bf16[48,640]{1,0:T(8,128)(2,1)S(1)} collective-permute-done((bf16[48,640]{1,0:T(8,128)(2,1)S(1)}, bf16[48,640]{1,0:T(8,128)(2,1)S(1)}, u32[]{:S(2)}, u32[]{:S(2)}) %collective-permute-start.4) | collective-permute-done | bytes 61472 | tf_op jit(solution)/shard_map/ppermute | solution.py:494
  26.2 0.7 collective-permute-done.3.far_below_ref
  27.5 14.3 %all_to_all.20.values_ref = bf16[16,16,512]{2,1,0:T(8,128)(2,1)S(1)} all-to-all(bf16[16,16,512]{2,1,0:T(8,128)(2,1)S(1)} %values.1), channel_id=1, replica_groups=mesh['ctx'=16,'exp'=16] {'exp'}, dimensions={0} | all-to-all | bytes 524288 | tf_op jit(solution)/shard_map/all_to_all | solution.py:499
  42.3 3.9 %collective-permute-start.5 = (bf16[336,128]{1,0:T(8,128)(2,1)S(1)}, bf16[336,128]{1,0:T(8,128)(2,1)S(1)}, u32[]{:S(2)}, u32[]{:S(2)}) collective-permute-start(bf16[336,128]{1,0:T(8,128)(2,1)S(1)} %project.1), channel_id=1, source_target_pairs={{0,16},{16,0},{32,48},{48,32},{64,80},{80,64},{96,112},{112,96},{1... | collective-permute-start | bytes 258056 | tf_op jit(solution)/shard_map/ppermute | solution.py:501
  46.2 0.9 collective-permute-done.5
  47.1 0.8 collective-permute-start.7
  47.9 2.0 %collective-permute-start.6 = (bf16[336,128]{1,0:T(8,128)(2,1)S(1)}, bf16[336,128]{1,0:T(8,128)(2,1)S(1)}, u32[]{:S(2)}, u32[]{:S(2)}) collective-permute-start(bf16[336,128]{1,0:T(8,128)(2,1)S(1)} %add_convert_fusion.own_ref), channel_id=1, source_target_pairs={{0,224},{16,240},{32,0},{48,16},{64,32},{80,48},{96,64},{112,80},{... | collective-permute-start | bytes 258056 | tf_op jit(solution)/shard_map/ppermute | solution.py:503
  49.9 2.3 %collective-permute-done.7.below_ref = bf16[336,128]{1,0:T(8,128)(2,1)S(1)} collective-permute-done((bf16[336,128]{1,0:T(8,128)(2,1)S(1)}, bf16[336,128]{1,0:T(8,128)(2,1)S(1)}, u32[]{:S(2)}, u32[]{:S(2)}) %collective-permute-start.7) | collective-permute-done | bytes 86048 | tf_op jit(solution)/shard_map/ppermute | solution.py:504
  52.5 1.4 %collective-permute-start.8 = (bf16[200,128]{1,0:T(8,128)(2,1)S(1)}, bf16[200,128]{1,0:T(8,128)(2,1)S(1)}, u32[]{:S(2)}, u32[]{:S(2)}) collective-permute-start(bf16[200,128]{1,0:T(8,128)(2,1)S(1)} %get-tuple-element.31), channel_id=1, source_target_pairs={{0,160},{16,176},{32,192},{48,208},{64,224},{80,240},{96,0},{112,1... | collective-permute-start | bytes 153608 | tf_op jit(solution)/shard_map/ppermute | solution.py:506
  53.9 3.0 %collective-permute-start.9 = (bf16[200,128]{1,0:T(8,128)(2,1)S(1)}, bf16[200,128]{1,0:T(8,128)(2,1)S(1)}, u32[]{:S(2)}, u32[]{:S(2)}) collective-permute-start(bf16[200,128]{1,0:T(8,128)(2,1)S(1)} %get-tuple-element.32), channel_id=1, source_target_pairs={{0,64},{16,80},{32,96},{48,112},{64,128},{80,144},{96,160},{112,17... | collective-permute-start | bytes 153608 | tf_op jit(solution)/shard_map/ppermute | solution.py:507
  56.9 2.0 %base.1 = (f32[56,448]{1,0:T(8,128)S(1)}, bf16[448,4096]{1,0:T(8,128)(2,1)S(1)}) custom-call(bf16[336,128]{1,0:T(8,128)(2,1)S(1)} %add_convert_fusion.own_ref, bf16[336,128]{1,0:T(8,128)(2,1)S(1)} %collective-permute-done.6.above_ref, bf16[336,128]{1,0:T(8,128)(2,1)S(1)} %collective-permute-done.7.below_ref, bf16[96,448]{1,0:T(8,128)(2,1)S(1)} %copy-done.5, ...), custom_call_target="tpu_custom_call" | custom-call | tf_op jit(solution)/shard_map/base/pallas_call | solution.py:362
  59.9 11.3 %all_to_all.21.parts_ref = bf16[16,56,256]{2,1,0:T(8,128)(2,1)S(1)} all-to-all(bf16[16,56,256]{2,1,0:T(8,128)(2,1)S(1)} %get-tuple-element.34), channel_id=1, replica_groups=mesh['ctx'=16,'exp'=16] {'exp'}, dimensions={0} | all-to-all | bytes 917504 | tf_op jit(solution)/shard_map/all_to_all | solution.py:510
  71.3 9.8 %all_to_all.22.act_ref = bf16[16,48,128]{2,1,0:T(8,128)(2,1)S(1)} all-to-all(bf16[16,48,128]{2,1,0:T(8,128)(2,1)S(1)} %activation.1), channel_id=1, replica_groups=mesh['ctx'=16,'exp'=16] {'exp'}, dimensions={0} | all-to-all | bytes 393216 | tf_op jit(solution)/shard_map/all_to_all | solution.py:511
  81.1 0.9 expert_out.1
  82.0 19.2 %all_to_all.23.parts_ref = bf16[16,16,256]{2,1,0:T(8,128)(2,1)S(1)} all-to-all(bf16[16,16,256]{2,1,0:T(8,128)(2,1)S(1)} %expert_out.1), channel_id=1, replica_groups=mesh['ctx'=16,'exp'=16] {'ctx'}, dimensions={0} | all-to-all | bytes 262144 | tf_op jit(solution)/shard_map/all_to_all | solution.py:513
  (33 shorter events, 3.7 us)
Async XLA Ops:
  0.6 21.5 %copy-start.9 = (f32[96,4]{0,1:T(4,128)S(1)}, f32[96,4]{0,1:T(4,128)}, u32[]{:S(2)}) copy-start(f32[96,4]{0,1:T(4,128)} %param.25) | copy-start | bytes 4612
  0.6 21.5 %copy-start.8 = (s32[96,4]{0,1:T(4,128)S(1)}, s32[96,4]{0,1:T(4,128)}, u32[]{:S(2)}) copy-start(s32[96,4]{0,1:T(4,128)} %param.24) | copy-start | bytes 4612
  0.7 21.5 %copy-start.6 = (f32[6,64]{1,0:T(8,128)S(1)}, f32[6,64]{1,0:T(8,128)}, u32[]{:S(2)}) copy-start(f32[6,64]{1,0:T(8,128)} %iw_ref.1) | copy-start | bytes 4612
  0.7 21.5 %copy-start.4 = (bf16[6,64,128]{2,1,0:T(8,128)(2,1)S(1)}, bf16[6,64,128]{2,1,0:T(8,128)(2,1)}, u32[]{:S(2)}) copy-start(bf16[6,64,128]{2,1,0:T(8,128)(2,1)} %iq_ref.1) | copy-start | bytes 294916
  0.7 21.5 %copy-start.3 = (bf16[6,384,128]{2,1,0:T(8,128)(2,1)S(1)}, bf16[6,384,128]{2,1,0:T(8,128)(2,1)}, u32[]{:S(2)}) copy-start(bf16[6,384,128]{2,1,0:T(8,128)(2,1)} %keys_ref.1) | copy-start | bytes 1769476
  0.7 26.2 %copy-start.1 = (bf16[8,512,128]{2,1,0:T(8,128)(2,1)S(1)}, bf16[8,512,128]{2,1,0:T(8,128)(2,1)}, u32[]{:S(2)}) copy-start(bf16[8,512,128]{2,1,0:T(8,128)(2,1)} %w_ref.1) | copy-start | bytes 3145732
  4.8 37.0 %copy-start.2 = (bf16[1024,448]{0,1:T(8,128)(2,1)S(1)}, bf16[1024,448]{0,1:T(8,128)(2,1)}, u32[]{:S(2)}) copy-start(bf16[1024,448]{0,1:T(8,128)(2,1)} %param.21) | copy-start | bytes 2752516
  4.8 4.8 %collective-permute-start = (bf16[8,48,640]{2,1,0:T(8,128)(2,1)S(1)}, bf16[8,48,640]{2,1,0:T(8,128)(2,1)S(1)}, u32[]{:S(2)}, u32[]{:S(2)}) collective-permute-start(bf16[8,48,640]{2,1,0:T(8,128)(2,1)S(1)} %get-tuple-element.21), channel_id=1, source_target_pairs={{0,16},{16,0},{32,48},{48,32},{64,80},{80,64},{96,112},{112,96},{1... | collective-permute-start | bytes 1474568 | tf_op jit(solution)/shard_map/ppermute | solution.py:488
  9.6 47.3 %copy-start.5 = (bf16[96,448]{1,0:T(8,128)(2,1)S(1)}, bf16[96,448]{1,0:T(8,128)(2,1)}, u32[]{:S(2)}) copy-start(bf16[96,448]{1,0:T(8,128)(2,1)} %hidden_ref.1) | copy-start | bytes 258052
  10.0 8.6 %collective-permute-start.1 = (bf16[3,48,640]{2,1,0:T(8,128)(2,1)S(1)}, bf16[3,48,640]{2,1,0:T(8,128)(2,1)S(1)}, u32[]{:S(2)}, u32[]{:S(2)}) collective-permute-start(bf16[3,48,640]{2,1,0:T(8,128)(2,1)S(1)} %get-tuple-element.23), channel_id=1, source_target_pairs={{0,32},{16,48},{32,64},{48,80},{64,96},{80,112},{96,128},{112,144}... | collective-permute-start | bytes 552968 | tf_op jit(solution)/shard_map/ppermute | solution.py:490
  10.1 6.3 %collective-permute-start.2 = (bf16[2,48,640]{2,1,0:T(8,128)(2,1)S(1)}, bf16[2,48,640]{2,1,0:T(8,128)(2,1)S(1)}, u32[]{:S(2)}, u32[]{:S(2)}) collective-permute-start(bf16[2,48,640]{2,1,0:T(8,128)(2,1)S(1)} %get-tuple-element.24), channel_id=1, source_target_pairs={{0,224},{16,240},{32,0},{48,16},{64,32},{80,48},{96,64},{112,80},{... | collective-permute-start | bytes 368648 | tf_op jit(solution)/shard_map/ppermute | solution.py:491
  18.8 7.4 %collective-permute-start.4 = (bf16[48,640]{1,0:T(8,128)(2,1)S(1)}, bf16[48,640]{1,0:T(8,128)(2,1)S(1)}, u32[]{:S(2)}, u32[]{:S(2)}) collective-permute-start(bf16[48,640]{1,0:T(8,128)(2,1)S(1)} %get-tuple-element.27), channel_id=1, source_target_pairs={{0,160},{16,176},{32,192},{48,208},{64,224},{80,240},{96,0},{112,1... | collective-permute-start | bytes 184328 | tf_op jit(solution)/shard_map/ppermute | solution.py:494
  20.9 6.0 %collective-permute-start.3 = (bf16[48,640]{1,0:T(8,128)(2,1)S(1)}, bf16[48,640]{1,0:T(8,128)(2,1)S(1)}, u32[]{:S(2)}, u32[]{:S(2)}) collective-permute-start(bf16[48,640]{1,0:T(8,128)(2,1)S(1)} %get-tuple-element.25._), channel_id=1, source_target_pairs={{0,64},{16,80},{32,96},{48,112},{64,128},{80,144},{96,160},{112,17... | collective-permute-start | bytes 184328 | tf_op jit(solution)/shard_map/ppermute | solution.py:493
  27.5 31.7 %copy-start.7 = (f32[448]{0:T(512)S(1)}, f32[448]{0:T(512)}, u32[]{:S(2)}) copy-start(f32[448]{0:T(512)} %param.23) | copy-start | bytes 5380
  42.3 4.8 %collective-permute-start.5 = (bf16[336,128]{1,0:T(8,128)(2,1)S(1)}, bf16[336,128]{1,0:T(8,128)(2,1)S(1)}, u32[]{:S(2)}, u32[]{:S(2)}) collective-permute-start(bf16[336,128]{1,0:T(8,128)(2,1)S(1)} %project.1), channel_id=1, source_target_pairs={{0,16},{16,0},{32,48},{48,32},{64,80},{80,64},{96,112},{112,96},{1... | collective-permute-start | bytes 258056 | tf_op jit(solution)/shard_map/ppermute | solution.py:501
  47.1 5.1 %collective-permute-start.7 = (bf16[336,128]{1,0:T(8,128)(2,1)S(1)}, bf16[336,128]{1,0:T(8,128)(2,1)S(1)}, u32[]{:S(2)}, u32[]{:S(2)}) collective-permute-start(bf16[336,128]{1,0:T(8,128)(2,1)S(1)} %add_convert_fusion.own_ref), channel_id=1, source_target_pairs={{0,32},{16,48},{32,64},{48,80},{64,96},{80,112},{96,128},{112,144}... | collective-permute-start | bytes 258056 | tf_op jit(solution)/shard_map/ppermute | solution.py:504
  47.9 4.3 %collective-permute-start.6 = (bf16[336,128]{1,0:T(8,128)(2,1)S(1)}, bf16[336,128]{1,0:T(8,128)(2,1)S(1)}, u32[]{:S(2)}, u32[]{:S(2)}) collective-permute-start(bf16[336,128]{1,0:T(8,128)(2,1)S(1)} %add_convert_fusion.own_ref), channel_id=1, source_target_pairs={{0,224},{16,240},{32,0},{48,16},{64,32},{80,48},{96,64},{112,80},{... | collective-permute-start | bytes 258056 | tf_op jit(solution)/shard_map/ppermute | solution.py:503
  52.5 6.5 %collective-permute-start.8 = (bf16[200,128]{1,0:T(8,128)(2,1)S(1)}, bf16[200,128]{1,0:T(8,128)(2,1)S(1)}, u32[]{:S(2)}, u32[]{:S(2)}) collective-permute-start(bf16[200,128]{1,0:T(8,128)(2,1)S(1)} %get-tuple-element.31), channel_id=1, source_target_pairs={{0,160},{16,176},{32,192},{48,208},{64,224},{80,240},{96,0},{112,1... | collective-permute-start | bytes 153608 | tf_op jit(solution)/shard_map/ppermute | solution.py:506
  53.9 5.2 %collective-permute-start.9 = (bf16[200,128]{1,0:T(8,128)(2,1)S(1)}, bf16[200,128]{1,0:T(8,128)(2,1)S(1)}, u32[]{:S(2)}, u32[]{:S(2)}) collective-permute-start(bf16[200,128]{1,0:T(8,128)(2,1)S(1)} %get-tuple-element.32), channel_id=1, source_target_pairs={{0,64},{16,80},{32,96},{48,112},{64,128},{80,144},{96,160},{112,17... | collective-permute-start | bytes 153608 | tf_op jit(solution)/shard_map/ppermute | solution.py:507
  58.9 22.2 %copy-start = (bf16[1,2048,448]{1,2,0:T(8,128)(2,1)S(1)}, bf16[1,2048,448]{1,2,0:T(8,128)(2,1)}, u32[]{:S(2)}) copy-start(bf16[1,2048,448]{1,2,0:T(8,128)(2,1)} %param.27) | copy-start | bytes 5505028

commit v7 on v6

--- a/solution.py
+++ b/solution.py
@@ -83,88 +83,148 @@
     return 3 * n + (n // 2 + 7) // 8 * 8
 
 
+def chosen_mask(ctx, picked, tokens):
+    rows = picked.shape[0]
+    per = tokens // BLOCK
+    block_of = iota((rows, tokens), 1) // BLOCK
+    mask = jnp.zeros((rows, tokens), f32)
+    for b in range(per):
+        hit = jnp.max(jnp.where(picked == ctx * per + b, 1.0, 0.0), axis=1, keepdims=True)
+        mask = jnp.where(block_of == b, hit, mask)
+    return mask
+
+
+def scores_of(query, keys):
+    return dot(query, keys, ((0,), (0,))) * SCORE_SCALE
+
+
+def partial_row(core, scores, keys, chosen):
+    masked = jnp.where(chosen, scores, NEG)
+    peak = jnp.max(masked, axis=1, keepdims=True)
+    expo = jnp.where(chosen, jnp.exp(masked - peak), 0.0)
+    total = jnp.sum(expo, axis=1, keepdims=True)
+    weighted = dot(expo.astype(bf16), keys[:LAT], ((1,), (1,)))
+    wide = jnp.concatenate([weighted, stats_tile(peak, total)], axis=1).reshape(8, 2, 8, WIDE)
+    return jnp.where(core == 0, wide[:, 0], wide[:, 1]), jnp.where(core == 0, wide[:, 1], wide[:, 0])
+
+
+def store_pair(i, even, odd, mine_ref, other_ref):
+    lines = slice(8 * i - 8, 8 * i + 8)
+    mine_ref[:, lines, :] = jnp.concatenate([even[0], odd[0]], axis=1)
+    other_ref[:, lines, :] = jnp.concatenate([even[1], odd[1]], axis=1).astype(bf16)
+
+
 def attention_kernel(
-    ctx_ref, blocks_hbm, query_hbm, cache_hbm, mine_ref, other_ref, blocks_ref, query_ref, cache_ref, sems, sem
+    ctx_ref, blocks_hbm, query_hbm, cache_hbm, mine_ref, other_ref, blocks_ref, query_rest, cache_rest,
+    query_ref, cache_ref, sems, sem,
 ):
-    rows, _, tokens = cache_ref.shape
+    here, _, tokens = cache_ref.shape
+    rows = cache_hbm.shape[0]
     load_blocks = pltpu.make_async_copy(blocks_hbm, blocks_ref, sem)
-    copies = [
-        (
-            pltpu.make_async_copy(query_hbm.at[r], query_ref.at[r], sems.at[0, r]),
-            pltpu.make_async_copy(cache_hbm.at[r], cache_ref.at[r], sems.at[1, r]),
+    copies = []
+    for r in range(rows):
+        query_to = query_ref.at[r] if r < here else query_rest.at[r - here]
+        cache_to = cache_ref.at[r] if r < here else cache_rest.at[r - here]
+        copies.append(
+            (
+                pltpu.make_async_copy(query_hbm.at[r], query_to, sems.at[0, r]),
+                pltpu.make_async_copy(cache_hbm.at[r], cache_to, sems.at[1, r]),
+            )
         )
-        for r in range(rows)
-    ]
 
     def start(r):
         for copy in copies[r]:
             copy.start()
 
+    def ready(r):
+        for copy in copies[r]:
+            copy.wait()
+        if r + 3 < rows:
+            start(r + 3)
+
     start(0)
     load_blocks.start()
-    for r in range(1, 3):
-        start(r)
+    start(1)
+    start(2)
     ctx = ctx_ref[0]
     core = lax.rem(ctx, 2)
-    per = tokens // BLOCK
-
-    def scores_of(i):
-        for copy in copies[i]:
-            copy.wait()
-        if i + 3 < rows:
-            start(i + 3)
-        return dot(query_ref[i], cache_ref[i], ((0,), (0,))) * SCORE_SCALE
-
-    def partial(i, scores, mask):
-        chosen = mask[i : i + 1, :] > 0.0
-        masked = jnp.where(chosen, scores, NEG)
-        peak = jnp.max(masked, axis=1, keepdims=True)
-        expo = jnp.where(chosen, jnp.exp(masked - peak), 0.0)
-        total = jnp.sum(expo, axis=1, keepdims=True)
-        weighted = dot(expo.astype(bf16), cache_ref[i, :LAT], ((1,), (1,)))
-        wide = jnp.concatenate([weighted, stats_tile(peak, total)], axis=1).reshape(8, 2, 8, WIDE)
-        return jnp.where(core == 0, wide[:, 0], wide[:, 1]), jnp.where(core == 0, wide[:, 1], wide[:, 0])
-
-    scores = scores_of(0)
+    ready(0)
+    scores = scores_of(query_ref[0], cache_ref[0])
     load_blocks.wait()
-    block_of = iota((rows, tokens), 1) // BLOCK
-    mask = jnp.zeros((rows, tokens), f32)
-    picked = blocks_ref[...]
-    for b in range(per):
-        hit = jnp.max(jnp.where(picked == ctx * per + b, 1.0, 0.0), axis=1, keepdims=True)
-        mask = jnp.where(block_of == b, hit, mask)
-    for i in range(rows):
-        later = scores_of(i + 1) if i + 1 < rows else None
-        mine, other = partial(i, scores, mask)
+    mask = chosen_mask(ctx, blocks_ref[...], tokens)
+    even = None
+    for i in range(here):
+        later = None
+        if i + 1 < here:
+            ready(i + 1)
+            later = scores_of(query_ref[i + 1], cache_ref[i + 1])
+        row = partial_row(core, scores, cache_ref[i], mask[i : i + 1, :] > 0.0)
         if i % 2 == 0:
-            mine_even, other_even = mine, other
+            even = row
         else:
-            lines = slice(8 * i - 8, 8 * i + 8)
-            mine_ref[:, lines, :] = jnp.concatenate([mine_even, mine], axis=1)
-            other_ref[:, lines, :] = jnp.concatenate([other_even, other], axis=1).astype(bf16)
+            store_pair(i, even, row, mine_ref, other_ref)
         scores = later
+    for r in range(here, rows):
+        ready(r)
+
+
+def rest_kernel(ctx_ref, blocks_ref, query_ref, cache_ref, mine_ref, other_ref):
+    count, _, tokens = cache_ref.shape
+    ctx = ctx_ref[0]
+    core = lax.rem(ctx, 2)
+    rows = blocks_ref.shape[0]
+    mask = chosen_mask(ctx, blocks_ref[...], tokens)
+    scores = [scores_of(query_ref[i], cache_ref[i]) for i in range(count)]
+    even = None
+    for i in range(count):
+        at = rows - count + i
+        row = partial_row(core, scores[i], cache_ref[i], mask[at : at + 1, :] > 0.0)
+        if i % 2 == 0:
+            even = row
+        else:
+            store_pair(i, even, row, mine_ref, other_ref)
+
+
+def halves_out(rows):
+    return [
+        jax.ShapeDtypeStruct((8, rows * 8, WIDE), f32),
+        jax.ShapeDtypeStruct((8, rows * 8, WIDE), bf16),
+    ]
 
 
 def attention(ctx, blocks, query, cache):
     rows = query.shape[0]
+    here, rest = rows - 2, 2
     return pl.pallas_call(
         attention_kernel,
         in_specs=[SMEM, HBM, HBM, HBM],
-        out_specs=[VMEM] * 2,
-        out_shape=[
-            jax.ShapeDtypeStruct((8, rows * 8, WIDE), f32),
-            jax.ShapeDtypeStruct((8, rows * 8, WIDE), bf16),
+        out_specs=[VMEM] * 5,
+        out_shape=halves_out(here)
+        + [
+            jax.ShapeDtypeStruct(blocks.shape, jnp.int32),
+            jax.ShapeDtypeStruct((rest,) + query.shape[1:], bf16),
+            jax.ShapeDtypeStruct((rest,) + cache.shape[1:], bf16),
         ],
         scratch_shapes=[
-            pltpu.VMEM(blocks.shape, jnp.int32),
-            pltpu.VMEM(query.shape, bf16),
-            pltpu.VMEM(cache.shape, bf16),
+            pltpu.VMEM((here,) + query.shape[1:], bf16),
+            pltpu.VMEM((here,) + cache.shape[1:], bf16),
             pltpu.SemaphoreType.DMA((2, rows)),
             pltpu.SemaphoreType.DMA,
         ],
         compiler_params=params(16),
         name="attention",
     )(ctx, in_hbm(blocks), in_hbm(query), in_hbm(cache))
+
+
+def attention_rest(ctx, blocks, query, cache):
+    return pl.pallas_call(
+        rest_kernel,
+        in_specs=[SMEM] + [VMEM] * 3,
+        out_specs=[VMEM] * 2,
+        out_shape=halves_out(query.shape[0]),
+        compiler_params=params(),
+        name="attention_rest",
+    )(ctx, blocks, query, cache)
 
 
 def side_kernel(
@@ -233,30 +293,27 @@
     return jnp.concatenate([summed, stats_tile(peak, total)], axis=1)
 
 
-def pair_kernel(ctx_ref, mine_ref, other_ref, keep_ref, up_ref, down_ref):
+def pair_kernel(offsets, ctx_ref, mine_ref, other_ref, mine_rest, other_rest, *out_refs):
     n = mine_ref.shape[0]
     z = ctx_ref[0] // 2
-    for ref, offsets in ((up_ref, (1, 6, 3)), (down_ref, (7, 4)), (keep_ref, (0, 5, 2))):
-        for i, offset in enumerate(offsets):
+    for ref, group in zip(out_refs[-len(offsets) :], offsets):
+        for i, offset in enumerate(group):
             there = lax.rem(z + offset, n)
-            both = merge([mine_ref[there], other_ref[there].astype(f32)])
-            ref[i] = widen(*both).astype(ref.dtype)
-
-
-def pair(ctx, mine, other):
-    rest = mine.shape[1:]
-    return pl.pallas_call(
-        pair_kernel,
-        in_specs=[SMEM, VMEM, VMEM],
-        out_specs=[VMEM] * 3,
-        out_shape=[
-            jax.ShapeDtypeStruct((3,) + rest, f32),
-            jax.ShapeDtypeStruct((3,) + rest, bf16),
-            jax.ShapeDtypeStruct((2,) + rest, bf16),
-        ],
+            mine = jnp.concatenate([mine_ref[there], mine_rest[there]], axis=0)
+            other = jnp.concatenate([other_ref[there].astype(f32), other_rest[there].astype(f32)], axis=0)
+            ref[i] = widen(*merge([mine, other])).astype(ref.dtype)
+
+
+def pair(ctx, parts, offsets, kind, after=()):
+    rows = parts[0].shape[1] + parts[2].shape[1]
+    return pl.pallas_call(
+        functools.partial(pair_kernel, offsets),
+        in_specs=[SMEM] + [VMEM] * 4 + [ANY] * len(after),
+        out_specs=[VMEM] * len(offsets),
+        out_shape=[jax.ShapeDtypeStruct((len(group), rows, WIDE), kind) for group in offsets],
         compiler_params=params(),
         name="pair",
-    )(ctx, mine, other)
+    )(ctx, *parts, *after)
 
 
 def relay_kernel(keep_ref, below_ref, above_ref, up_ref, down_ref):
@@ -482,11 +539,15 @@
     def along_z(shift):
         return [(i, (i + shift) % n_ctx) for i in range(n_ctx)]
 
-    mine, other = attention(
+    mine, other, blocks, query, cache = attention(
         ctx, chosen_blocks, jnp.swapaxes(lat_query, 1, 2), jnp.swapaxes(cache, 1, 2)
     )
+    mine_rest, other_rest = attention_rest(ctx, blocks, query, cache)
     other = lax.ppermute(other, "ctx", other_core)
-    keep, up, down = pair(ctx, mine, other)
+    other_rest = lax.ppermute(other_rest, "ctx", other_core)
+    parts = (mine, other, mine_rest, other_rest)
+    up, down = pair(ctx, parts, ((1, 6, 3), (7, 4)), bf16)
+    (keep,) = pair(ctx, parts, ((0, 5, 2),), f32, (down,))
     below = lax.ppermute(up, "ctx", along_z(2))
     above = lax.ppermute(down, "ctx", along_z(-2))
     up, down = relay(keep, below, above)

time: 102 us -> 102 us (level)
    ppermute x1, waiting for transfers between devices: 1.49 us -> 0.01 us  [local(): other = lax.ppermute(other, 'ctx', other_core)]
    ppermute x0 -> x1, waiting for transfers between devices: none -> 1.38 us  [local(): other_rest = lax.ppermute(other_rest, 'ctx', other_core)]
  transfers between devices with their start and end apart: 10 -> 11, of which waited for: 8 -> 8; matrix products, arithmetic and copies ran while one was open for 0% -> 0% of each run, Pallas kernels for 4% -> 5%
where the time goes in v7:
time: 102 us; the launch traced here: 101 us
  blocking collectives  54 us (53%)
  starting transfers between devices  21.3 us (21%)
  waiting for transfers between devices  12.7 us (12%)
  Pallas kernels  12.4 us (12%)
    all_to_all x1, blocking collectives, local(): outs = lax.all_to_all(outs, 'ctx', 0, 0)  18.7 us
    all_to_all x1, blocking collectives, local(): vals = lax.all_to_all(vals, 'exp', 0, 0)  14.2 us
    all_to_all x1, blocking collectives, local(): terms = lax.all_to_all(terms, 'exp', 0, 0)  11.2 us
    all_to_all x1, blocking collectives, local(): act = lax.all_to_all(activation(terms), 'exp', 0, 0)  9.86 us
    ppermute x1, starting transfers between devices, local(): above = lax.ppermute(down, 'ctx', along_z(-2))  3.91 us
    ppermute x1, starting transfers between devices, local(): own = part.astype(f32) + lax.ppermute(part, 'ctx', other_core).astype(f32)  3.38 us
    ppermute x1, starting transfers between devices, local(): other = lax.ppermute(other, 'ctx', other_core)  3.33 us
    pallas_call x1, Pallas kernels, attention(): pl.pallas_call(attention_kernel, in_specs=[SMEM, HBM, HBM, HBM], out_spec...  3.22 us
  transfers between devices with their start and end apart: 11, of which 8 were waited for; matrix products, arithmetic and copies ran while one was open for 0% of the time, Pallas kernels for 5%

profile of v7, /device:TPU:1, one launch (start us, length us, event | category | flops | bytes accessed | tf_op | source)
XLA Modules:
  0.0 101.4 jit_solution(4749733070152222016)
XLA Ops:
  0.7 3.2 %attention.1 = (f32[8,32,640]{2,1,0:T(8,128)S(1)}, bf16[8,32,640]{2,1,0:T(8,128)(2,1)S(1)}, s32[6,32]{1,0:T(8,128)S(1)}, bf16[2,576,128]{2,1,0:T(8,128)(2,1)S(1)}, bf16[2,576,384]{2,1,0:T(8,128)(2,1)S(1)}) custom-call(s32[1]{0:T(128)} %bitcast.ctx_ref, s32[6,32]{1,0:T(8,128)} %blocks_hbm.1, bf16[6,576,128]{2,1,0:T(8,128)(2,1)} %bitcast.18, ...), custom_call_target="tpu_custom_call" | custom-call | tf_op jit(solution)/shard_map/attention/pallas_call | solution.py:198
  3.9 3.3 %collective-permute-start = (bf16[8,32,640]{2,1,0:T(8,128)(2,1)S(1)}, bf16[8,32,640]{2,1,0:T(8,128)(2,1)S(1)}, u32[]{:S(2)}, u32[]{:S(2)}) collective-permute-start(bf16[8,32,640]{2,1,0:T(8,128)(2,1)S(1)} %get-tuple-element.25), channel_id=1, source_target_pairs={{0,16},{16,0},{32,48},{48,32},{64,80},{80,64},{96,112},{112,96},{1... | collective-permute-start | bytes 983048 | tf_op jit(solution)/shard_map/ppermute | solution.py:546
  8.1 1.4 %collective-permute-done.1.other_rest = bf16[8,16,640]{2,1,0:T(8,128)(2,1)S(1)} collective-permute-done((bf16[8,16,640]{2,1,0:T(8,128)(2,1)S(1)}, bf16[8,16,640]{2,1,0:T(8,128)(2,1)S(1)}, u32[]{:S(2)}, u32[]{:S(2)}) %collective-permute-start.1) | collective-permute-done | bytes 163872 | tf_op jit(solution)/shard_map/ppermute | solution.py:547
  9.9 3.9 %collective-permute-start.3 = (bf16[2,48,640]{2,1,0:T(8,128)(2,1)S(1)}, bf16[2,48,640]{2,1,0:T(8,128)(2,1)S(1)}, u32[]{:S(2)}, u32[]{:S(2)}) collective-permute-start(bf16[2,48,640]{2,1,0:T(8,128)(2,1)S(1)} %get-tuple-element.31.out_refs_0_), channel_id=1, source_target_pairs={{0,224},{16,240},{32,0},{48,16},{64,32},{80,48},{96,64},{112,80},{... | collective-permute-start | bytes 368648 | tf_op jit(solution)/shard_map/ppermute | solution.py:552
  14.0 2.4 %collective-permute-done.3.above_ref = bf16[2,48,640]{2,1,0:T(8,128)(2,1)S(1)} collective-permute-done((bf16[2,48,640]{2,1,0:T(8,128)(2,1)S(1)}, bf16[2,48,640]{2,1,0:T(8,128)(2,1)S(1)}, u32[]{:S(2)}, u32[]{:S(2)}) %collective-permute-start.3) | collective-permute-done | bytes 122912 | tf_op jit(solution)/shard_map/ppermute | solution.py:552
  16.4 2.2 %collective-permute-done.2.below_ref = bf16[3,48,640]{2,1,0:T(8,128)(2,1)S(1)} collective-permute-done((bf16[3,48,640]{2,1,0:T(8,128)(2,1)S(1)}, bf16[3,48,640]{2,1,0:T(8,128)(2,1)S(1)}, u32[]{:S(2)}, u32[]{:S(2)}) %collective-permute-start.2) | collective-permute-done | bytes 184352 | tf_op jit(solution)/shard_map/ppermute | solution.py:551
  18.8 2.2 %collective-permute-start.5 = (bf16[48,640]{1,0:T(8,128)(2,1)S(1)}, bf16[48,640]{1,0:T(8,128)(2,1)S(1)}, u32[]{:S(2)}, u32[]{:S(2)}) collective-permute-start(bf16[48,640]{1,0:T(8,128)(2,1)S(1)} %get-tuple-element.35), channel_id=1, source_target_pairs={{0,160},{16,176},{32,192},{48,208},{64,224},{80,240},{96,0},{112,1... | collective-permute-start | bytes 184328 | tf_op jit(solution)/shard_map/ppermute | solution.py:555
  21.0 1.2 %collective-permute-start.4 = (bf16[48,640]{1,0:T(8,128)(2,1)S(1)}, bf16[48,640]{1,0:T(8,128)(2,1)S(1)}, u32[]{:S(2)}, u32[]{:S(2)}) collective-permute-start(bf16[48,640]{1,0:T(8,128)(2,1)S(1)} %get-tuple-element.33._), channel_id=1, source_target_pairs={{0,64},{16,80},{32,96},{48,112},{64,128},{80,144},{96,160},{112,17... | collective-permute-start | bytes 184328 | tf_op jit(solution)/shard_map/ppermute | solution.py:554
  22.2 2.0 %side.1 = (f32[6,384]{1,0:T(8,128)}, bf16[2,56,96]{2,1,0:T(8,128)(2,1)S(1)}, bf16[56,96]{1,0:T(8,128)(2,1)S(1)}, bf16[128,48]{1,0:T(8,128)(2,1)S(1)}, f32[48,128]{1,0:T(8,128)S(1)}) custom-call(s32[1]{0:T(128)} %bitcast.ctx_ref, s32[4,96]{1,0:T(4,128)S(1)} %bitcast.14, f32[4,96]{1,0:T(4,128)S(1)} %bitcast.15, bf16[6,64,128]{2,1,0:T(8,128)(2,1)S(1)} %copy-done.4, ...), custom_call_target="tpu_custom_call" | custom-call | tf_op jit(solution)/shard_map/side/pallas_call | solution.py:268
  24.2 1.8 %collective-permute-done.5.far_above_ref = bf16[48,640]{1,0:T(8,128)(2,1)S(1)} collective-permute-done((bf16[48,640]{1,0:T(8,128)(2,1)S(1)}, bf16[48,640]{1,0:T(8,128)(2,1)S(1)}, u32[]{:S(2)}, u32[]{:S(2)}) %collective-permute-start.5) | collective-permute-done | bytes 61472 | tf_op jit(solution)/shard_map/ppermute | solution.py:555
  26.0 0.9 collective-permute-done.4.far_below_ref
  27.5 14.2 %all_to_all.20.values_ref = bf16[16,16,512]{2,1,0:T(8,128)(2,1)S(1)} all-to-all(bf16[16,16,512]{2,1,0:T(8,128)(2,1)S(1)} %values.1), channel_id=1, replica_groups=mesh['ctx'=16,'exp'=16] {'exp'}, dimensions={0} | all-to-all | bytes 524288 | tf_op jit(solution)/shard_map/all_to_all | solution.py:560
  42.2 3.4 %collective-permute-start.6 = (bf16[336,128]{1,0:T(8,128)(2,1)S(1)}, bf16[336,128]{1,0:T(8,128)(2,1)S(1)}, u32[]{:S(2)}, u32[]{:S(2)}) collective-permute-start(bf16[336,128]{1,0:T(8,128)(2,1)S(1)} %project.1), channel_id=1, source_target_pairs={{0,16},{16,0},{32,48},{48,32},{64,80},{80,64},{96,112},{112,96},{1... | collective-permute-start | bytes 258056 | tf_op jit(solution)/shard_map/ppermute | solution.py:562
  45.6 0.9 collective-permute-done.6
  46.5 1.1 %collective-permute-start.8 = (bf16[336,128]{1,0:T(8,128)(2,1)S(1)}, bf16[336,128]{1,0:T(8,128)(2,1)S(1)}, u32[]{:S(2)}, u32[]{:S(2)}) collective-permute-start(bf16[336,128]{1,0:T(8,128)(2,1)S(1)} %add_convert_fusion.own_ref), channel_id=1, source_target_pairs={{0,32},{16,48},{32,64},{48,80},{64,96},{80,112},{96,128},{112,144}... | collective-permute-start | bytes 258056 | tf_op jit(solution)/shard_map/ppermute | solution.py:565
  47.7 1.6 %collective-permute-start.7 = (bf16[336,128]{1,0:T(8,128)(2,1)S(1)}, bf16[336,128]{1,0:T(8,128)(2,1)S(1)}, u32[]{:S(2)}, u32[]{:S(2)}) collective-permute-start(bf16[336,128]{1,0:T(8,128)(2,1)S(1)} %add_convert_fusion.own_ref), channel_id=1, source_target_pairs={{0,224},{16,240},{32,0},{48,16},{64,32},{80,48},{96,64},{112,80},{... | collective-permute-start | bytes 258056 | tf_op jit(solution)/shard_map/ppermute | solution.py:564
  49.3 2.3 %collective-permute-done.8.below_ref = bf16[336,128]{1,0:T(8,128)(2,1)S(1)} collective-permute-done((bf16[336,128]{1,0:T(8,128)(2,1)S(1)}, bf16[336,128]{1,0:T(8,128)(2,1)S(1)}, u32[]{:S(2)}, u32[]{:S(2)}) %collective-permute-start.8) | collective-permute-done | bytes 86048 | tf_op jit(solution)/shard_map/ppermute | solution.py:565
  51.9 1.8 %collective-permute-start.9 = (bf16[200,128]{1,0:T(8,128)(2,1)S(1)}, bf16[200,128]{1,0:T(8,128)(2,1)S(1)}, u32[]{:S(2)}, u32[]{:S(2)}) collective-permute-start(bf16[200,128]{1,0:T(8,128)(2,1)S(1)} %get-tuple-element.39), channel_id=1, source_target_pairs={{0,160},{16,176},{32,192},{48,208},{64,224},{80,240},{96,0},{112,1... | collective-permute-start | bytes 153608 | tf_op jit(solution)/shard_map/ppermute | solution.py:567
  53.7 2.6 %collective-permute-start.10 = (bf16[200,128]{1,0:T(8,128)(2,1)S(1)}, bf16[200,128]{1,0:T(8,128)(2,1)S(1)}, u32[]{:S(2)}, u32[]{:S(2)}) collective-permute-start(bf16[200,128]{1,0:T(8,128)(2,1)S(1)} %get-tuple-element.40), channel_id=1, source_target_pairs={{0,64},{16,80},{32,96},{48,112},{64,128},{80,144},{96,160},{112,17... | collective-permute-start | bytes 153608 | tf_op jit(solution)/shard_map/ppermute | solution.py:568
  56.3 2.0 %base.1 = (f32[56,448]{1,0:T(8,128)S(1)}, bf16[448,4096]{1,0:T(8,128)(2,1)S(1)}) custom-call(bf16[336,128]{1,0:T(8,128)(2,1)S(1)} %add_convert_fusion.own_ref, bf16[336,128]{1,0:T(8,128)(2,1)S(1)} %collective-permute-done.7.above_ref, bf16[336,128]{1,0:T(8,128)(2,1)S(1)} %collective-permute-done.8.below_ref, bf16[96,448]{1,0:T(8,128)(2,1)S(1)} %copy-done.5, ...), custom_call_target="tpu_custom_call" | custom-call | tf_op jit(solution)/shard_map/base/pallas_call | solution.py:419
  59.9 11.2 %all_to_all.21.parts_ref = bf16[16,56,256]{2,1,0:T(8,128)(2,1)S(1)} all-to-all(bf16[16,56,256]{2,1,0:T(8,128)(2,1)S(1)} %get-tuple-element.42), channel_id=1, replica_groups=mesh['ctx'=16,'exp'=16] {'exp'}, dimensions={0} | all-to-all | bytes 917504 | tf_op jit(solution)/shard_map/all_to_all | solution.py:571
  71.3 9.9 %all_to_all.22.act_ref = bf16[16,48,128]{2,1,0:T(8,128)(2,1)S(1)} all-to-all(bf16[16,48,128]{2,1,0:T(8,128)(2,1)S(1)} %activation.1), channel_id=1, replica_groups=mesh['ctx'=16,'exp'=16] {'exp'}, dimensions={0} | all-to-all | bytes 393216 | tf_op jit(solution)/shard_map/all_to_all | solution.py:572
  81.1 0.9 expert_out.1
  82.0 18.7 %all_to_all.23.parts_ref = bf16[16,16,256]{2,1,0:T(8,128)(2,1)S(1)} all-to-all(bf16[16,16,256]{2,1,0:T(8,128)(2,1)S(1)} %expert_out.1), channel_id=1, replica_groups=mesh['ctx'=16,'exp'=16] {'ctx'}, dimensions={0} | all-to-all | bytes 262144 | tf_op jit(solution)/shard_map/all_to_all | solution.py:574
  (37 shorter events, 5.3 us)
Async XLA Ops:
  0.6 21.5 %copy-start.3 = (bf16[6,384,128]{2,1,0:T(8,128)(2,1)S(1)}, bf16[6,384,128]{2,1,0:T(8,128)(2,1)}, u32[]{:S(2)}) copy-start(bf16[6,384,128]{2,1,0:T(8,128)(2,1)} %keys_ref.1) | copy-start | bytes 1769476
  0.6 21.5 %copy-start.4 = (bf16[6,64,128]{2,1,0:T(8,128)(2,1)S(1)}, bf16[6,64,128]{2,1,0:T(8,128)(2,1)}, u32[]{:S(2)}) copy-start(bf16[6,64,128]{2,1,0:T(8,128)(2,1)} %iq_ref.1) | copy-start | bytes 294916
  0.7 21.5 %copy-start.6 = (f32[6,64]{1,0:T(8,128)S(1)}, f32[6,64]{1,0:T(8,128)}, u32[]{:S(2)}) copy-start(f32[6,64]{1,0:T(8,128)} %iw_ref.1) | copy-start | bytes 4612
  0.7 21.5 %copy-start.8 = (s32[96,4]{0,1:T(4,128)S(1)}, s32[96,4]{0,1:T(4,128)}, u32[]{:S(2)}) copy-start(s32[96,4]{0,1:T(4,128)} %param.24) | copy-start | bytes 4612
  0.7 21.5 %copy-start.9 = (f32[96,4]{0,1:T(4,128)S(1)}, f32[96,4]{0,1:T(4,128)}, u32[]{:S(2)}) copy-start(f32[96,4]{0,1:T(4,128)} %param.25) | copy-start | bytes 4612
  3.9 23.0 %copy-start.1 = (bf16[8,512,128]{2,1,0:T(8,128)(2,1)S(1)}, bf16[8,512,128]{2,1,0:T(8,128)(2,1)}, u32[]{:S(2)}) copy-start(bf16[8,512,128]{2,1,0:T(8,128)(2,1)} %w_ref.1) | copy-start | bytes 3145732
  3.9 5.6 %collective-permute-start = (bf16[8,32,640]{2,1,0:T(8,128)(2,1)S(1)}, bf16[8,32,640]{2,1,0:T(8,128)(2,1)S(1)}, u32[]{:S(2)}, u32[]{:S(2)}) collective-permute-start(bf16[8,32,640]{2,1,0:T(8,128)(2,1)S(1)} %get-tuple-element.25), channel_id=1, source_target_pairs={{0,16},{16,0},{32,48},{48,32},{64,80},{80,64},{96,112},{112,96},{1... | collective-permute-start | bytes 983048 | tf_op jit(solution)/shard_map/ppermute | solution.py:546
  8.0 1.5 %collective-permute-start.1 = (bf16[8,16,640]{2,1,0:T(8,128)(2,1)S(1)}, bf16[8,16,640]{2,1,0:T(8,128)(2,1)S(1)}, u32[]{:S(2)}, u32[]{:S(2)}) collective-permute-start(bf16[8,16,640]{2,1,0:T(8,128)(2,1)S(1)} %get-tuple-element.30), channel_id=1, source_target_pairs={{0,16},{16,0},{32,48},{48,32},{64,80},{80,64},{96,112},{112,96},{1... | collective-permute-start | bytes 491528 | tf_op jit(solution)/shard_map/ppermute | solution.py:547
  9.5 32.2 %copy-start.2 = (bf16[1024,448]{0,1:T(8,128)(2,1)S(1)}, bf16[1024,448]{0,1:T(8,128)(2,1)}, u32[]{:S(2)}) copy-start(bf16[1024,448]{0,1:T(8,128)(2,1)} %param.21) | copy-start | bytes 2752516
  9.8 8.8 %collective-permute-start.2 = (bf16[3,48,640]{2,1,0:T(8,128)(2,1)S(1)}, bf16[3,48,640]{2,1,0:T(8,128)(2,1)S(1)}, u32[]{:S(2)}, u32[]{:S(2)}) collective-permute-start(bf16[3,48,640]{2,1,0:T(8,128)(2,1)S(1)} %get-tuple-element.32), channel_id=1, source_target_pairs={{0,32},{16,48},{32,64},{48,80},{64,96},{80,112},{96,128},{112,144}... | collective-permute-start | bytes 552968 | tf_op jit(solution)/shard_map/ppermute | solution.py:551
  9.9 46.4 %copy-start.5 = (bf16[96,448]{1,0:T(8,128)(2,1)S(1)}, bf16[96,448]{1,0:T(8,128)(2,1)}, u32[]{:S(2)}) copy-start(bf16[96,448]{1,0:T(8,128)(2,1)} %hidden_ref.1) | copy-start | bytes 258052
  9.9 6.5 %collective-permute-start.3 = (bf16[2,48,640]{2,1,0:T(8,128)(2,1)S(1)}, bf16[2,48,640]{2,1,0:T(8,128)(2,1)S(1)}, u32[]{:S(2)}, u32[]{:S(2)}) collective-permute-start(bf16[2,48,640]{2,1,0:T(8,128)(2,1)S(1)} %get-tuple-element.31.out_refs_0_), channel_id=1, source_target_pairs={{0,224},{16,240},{32,0},{48,16},{64,32},{80,48},{96,64},{112,80},{... | collective-permute-start | bytes 368648 | tf_op jit(solution)/shard_map/ppermute | solution.py:552
  18.8 7.2 %collective-permute-start.5 = (bf16[48,640]{1,0:T(8,128)(2,1)S(1)}, bf16[48,640]{1,0:T(8,128)(2,1)S(1)}, u32[]{:S(2)}, u32[]{:S(2)}) collective-permute-start(bf16[48,640]{1,0:T(8,128)(2,1)S(1)} %get-tuple-element.35), channel_id=1, source_target_pairs={{0,160},{16,176},{32,192},{48,208},{64,224},{80,240},{96,0},{112,1... | collective-permute-start | bytes 184328 | tf_op jit(solution)/shard_map/ppermute | solution.py:555
  21.0 6.0 %collective-permute-start.4 = (bf16[48,640]{1,0:T(8,128)(2,1)S(1)}, bf16[48,640]{1,0:T(8,128)(2,1)S(1)}, u32[]{:S(2)}, u32[]{:S(2)}) collective-permute-start(bf16[48,640]{1,0:T(8,128)(2,1)S(1)} %get-tuple-element.33._), channel_id=1, source_target_pairs={{0,64},{16,80},{32,96},{48,112},{64,128},{80,144},{96,160},{112,17... | collective-permute-start | bytes 184328 | tf_op jit(solution)/shard_map/ppermute | solution.py:554
  27.5 31.7 %copy-start.7 = (f32[448]{0:T(512)S(1)}, f32[448]{0:T(512)}, u32[]{:S(2)}) copy-start(f32[448]{0:T(512)} %param.23) | copy-start | bytes 5380
  42.2 4.3 %collective-permute-start.6 = (bf16[336,128]{1,0:T(8,128)(2,1)S(1)}, bf16[336,128]{1,0:T(8,128)(2,1)S(1)}, u32[]{:S(2)}, u32[]{:S(2)}) collective-permute-start(bf16[336,128]{1,0:T(8,128)(2,1)S(1)} %project.1), channel_id=1, source_target_pairs={{0,16},{16,0},{32,48},{48,32},{64,80},{80,64},{96,112},{112,96},{1... | collective-permute-start | bytes 258056 | tf_op jit(solution)/shard_map/ppermute | solution.py:562
  46.5 5.1 %collective-permute-start.8 = (bf16[336,128]{1,0:T(8,128)(2,1)S(1)}, bf16[336,128]{1,0:T(8,128)(2,1)S(1)}, u32[]{:S(2)}, u32[]{:S(2)}) collective-permute-start(bf16[336,128]{1,0:T(8,128)(2,1)S(1)} %add_convert_fusion.own_ref), channel_id=1, source_target_pairs={{0,32},{16,48},{32,64},{48,80},{64,96},{80,112},{96,128},{112,144}... | collective-permute-start | bytes 258056 | tf_op jit(solution)/shard_map/ppermute | solution.py:565
  47.7 3.9 %collective-permute-start.7 = (bf16[336,128]{1,0:T(8,128)(2,1)S(1)}, bf16[336,128]{1,0:T(8,128)(2,1)S(1)}, u32[]{:S(2)}, u32[]{:S(2)}) collective-permute-start(bf16[336,128]{1,0:T(8,128)(2,1)S(1)} %add_convert_fusion.own_ref), channel_id=1, source_target_pairs={{0,224},{16,240},{32,0},{48,16},{64,32},{80,48},{96,64},{112,80},{... | collective-permute-start | bytes 258056 | tf_op jit(solution)/shard_map/ppermute | solution.py:564
  51.9 6.5 %collective-permute-start.9 = (bf16[200,128]{1,0:T(8,128)(2,1)S(1)}, bf16[200,128]{1,0:T(8,128)(2,1)S(1)}, u32[]{:S(2)}, u32[]{:S(2)}) collective-permute-start(bf16[200,128]{1,0:T(8,128)(2,1)S(1)} %get-tuple-element.39), channel_id=1, source_target_pairs={{0,160},{16,176},{32,192},{48,208},{64,224},{80,240},{96,0},{112,1... | collective-permute-start | bytes 153608 | tf_op jit(solution)/shard_map/ppermute | solution.py:567
  53.7 5.5 %collective-permute-start.10 = (bf16[200,128]{1,0:T(8,128)(2,1)S(1)}, bf16[200,128]{1,0:T(8,128)(2,1)S(1)}, u32[]{:S(2)}, u32[]{:S(2)}) collective-permute-start(bf16[200,128]{1,0:T(8,128)(2,1)S(1)} %get-tuple-element.40), channel_id=1, source_target_pairs={{0,64},{16,80},{32,96},{48,112},{64,128},{80,144},{96,160},{112,17... | collective-permute-start | bytes 153608 | tf_op jit(solution)/shard_map/ppermute | solution.py:568
  58.3 22.8 %copy-start = (bf16[1,2048,448]{1,2,0:T(8,128)(2,1)S(1)}, bf16[1,2048,448]{1,2,0:T(8,128)(2,1)}, u32[]{:S(2)}) copy-start(bf16[1,2048,448]{1,2,0:T(8,128)(2,1)} %param.27) | copy-start | bytes 5505028

commit v8 on v7

--- a/solution.py
+++ b/solution.py
@@ -293,6 +293,23 @@
     return jnp.concatenate([summed, stats_tile(peak, total)], axis=1)
 
 
+def first_eight():
+    return jnp.where(iota((8, 128), 0) == iota((8, 128), 1), 1.0, 0.0)
+
+
+def to_lines(peak, total, summed):
+    stats = dot(first_eight(), stats_tile(peak, total), ((1,), (1,)))
+    stats = jnp.concatenate([stats, jnp.zeros((8, 128 - stats.shape[1]), f32)], axis=1)
+    return jnp.concatenate([summed[:, at : at + 128] for at in range(0, LAT, 128)] + [stats], axis=0)
+
+
+def from_lines(x):
+    x = x.astype(f32)
+    rows = (x.shape[0] - 8) // 4
+    stats = dot(x[4 * rows :], first_eight(), ((0,), (0,)))[:rows]
+    return jnp.concatenate([x[k * rows : (k + 1) * rows] for k in range(4)] + [stats], axis=1)
+
+
 def pair_kernel(offsets, ctx_ref, mine_ref, other_ref, mine_rest, other_rest, *out_refs):
     n = mine_ref.shape[0]
     z = ctx_ref[0] // 2
@@ -301,25 +318,27 @@
             there = lax.rem(z + offset, n)
             mine = jnp.concatenate([mine_ref[there], mine_rest[there]], axis=0)
             other = jnp.concatenate([other_ref[there].astype(f32), other_rest[there].astype(f32)], axis=0)
-            ref[i] = widen(*merge([mine, other])).astype(ref.dtype)
+            shape = widen if ref.shape[2] == WIDE else to_lines
+            ref[i] = shape(*merge([mine, other])).astype(ref.dtype)
 
 
 def pair(ctx, parts, offsets, kind, after=()):
     rows = parts[0].shape[1] + parts[2].shape[1]
+    shape = (rows, WIDE) if kind == f32 else (4 * rows + 8, 128)
     return pl.pallas_call(
         functools.partial(pair_kernel, offsets),
         in_specs=[SMEM] + [VMEM] * 4 + [ANY] * len(after),
         out_specs=[VMEM] * len(offsets),
-        out_shape=[jax.ShapeDtypeStruct((len(group), rows, WIDE), kind) for group in offsets],
+        out_shape=[jax.ShapeDtypeStruct((len(group),) + shape, kind) for group in offsets],
         compiler_params=params(),
         name="pair",
     )(ctx, *parts, *after)
 
 
 def relay_kernel(keep_ref, below_ref, above_ref, up_ref, down_ref):
-    down = merge([keep_ref[1], below_ref[1].astype(f32), above_ref[1].astype(f32)])
-    down_ref[...] = widen(*down).astype(bf16)
-    up_ref[...] = widen(*merge([keep_ref[2], below_ref[2].astype(f32)])).astype(bf16)
+    down = merge([keep_ref[1], from_lines(below_ref[1]), from_lines(above_ref[1])])
+    down_ref[...] = to_lines(*down).astype(bf16)
+    up_ref[...] = to_lines(*merge([keep_ref[2], from_lines(below_ref[2])])).astype(bf16)
 
 
 def relay(keep, below, above):
@@ -327,15 +346,15 @@
         relay_kernel,
         in_specs=[VMEM] * 3,
         out_specs=[VMEM] * 2,
-        out_shape=[jax.ShapeDtypeStruct(keep.shape[1:], bf16)] * 2,
+        out_shape=[jax.ShapeDtypeStruct(below.shape[1:], bf16)] * 2,
         compiler_params=params(),
         name="relay",
     )(keep, below, above)
 
 
 def values_kernel(keep_ref, below_ref, above_ref, far_below_ref, far_above_ref, w_ref, _, out_ref):
-    parts = [keep_ref[0], below_ref[0], above_ref[0], far_below_ref[...], far_above_ref[...]]
-    _, total, summed = merge([x.astype(f32) for x in parts])
+    parts = [below_ref[0], above_ref[0], far_below_ref[...], far_above_ref[...]]
+    _, total, summed = merge([keep_ref[0]] + [from_lines(x) for x in parts])
     lat = (summed / total).astype(bf16)
     rows = lat.shape[0]
     row, col = iota((64, rows), 0), iota((64, rows), 1)

time: 102 us -> 101 us (level)
  waiting for transfers between devices: 12.7 us -> 10.9 us
    ppermute x1, waiting for transfers between devices: 1.79 us -> 0.01 us  [local(): far_above = lax.ppermute(down, 'ctx', along_z(-UP))]
  transfers between devices with their start and end apart: 11 -> 11, of which waited for: 8 -> 7; matrix products, arithmetic and copies ran while one was open for 0% -> 0% of each run, Pallas kernels for 5% -> 5%
where the time goes in v8:
time: 101 us
  blocking collectives  54.5 us (54%)
  starting transfers between devices  21.8 us (22%)
  Pallas kernels  13 us (13%)
  waiting for transfers between devices  10.9 us (11%)
    all_to_all x1, blocking collectives, local(): outs = lax.all_to_all(outs, 'ctx', 0, 0)  18.9 us
    all_to_all x1, blocking collectives, local(): vals = lax.all_to_all(vals, 'exp', 0, 0)  14.3 us
    all_to_all x1, blocking collectives, local(): terms = lax.all_to_all(terms, 'exp', 0, 0)  11.5 us
    all_to_all x1, blocking collectives, local(): act = lax.all_to_all(activation(terms), 'exp', 0, 0)  9.78 us
    ppermute x1, starting transfers between devices, local(): above = lax.ppermute(down, 'ctx', along_z(-2))  3.91 us
    ppermute x1, starting transfers between devices, local(): own = part.astype(f32) + lax.ppermute(part, 'ctx', other_core).astype(f32)  3.77 us
    ppermute x1, starting transfers between devices, local(): other = lax.ppermute(other, 'ctx', other_core)  3.33 us
    pallas_call x1, Pallas kernels, attention(): pl.pallas_call(attention_kernel, in_specs=[SMEM, HBM, HBM, HBM], out_spec...  3.22 us
  transfers between devices with their start and end apart: 11, of which 7 were waited for; matrix products, arithmetic and copies ran while one was open for 0% of the time, Pallas kernels for 5%

profile of v8, /device:TPU:1, one launch (start us, length us, event | category | flops | bytes accessed | tf_op | source)
XLA Modules:
  0.0 101.1 jit_solution(14551718653203981193)
XLA Ops:
  0.7 3.2 %attention.1 = (f32[8,32,640]{2,1,0:T(8,128)S(1)}, bf16[8,32,640]{2,1,0:T(8,128)(2,1)S(1)}, s32[6,32]{1,0:T(8,128)S(1)}, bf16[2,576,128]{2,1,0:T(8,128)(2,1)S(1)}, bf16[2,576,384]{2,1,0:T(8,128)(2,1)S(1)}) custom-call(s32[1]{0:T(128)} %bitcast.ctx_ref, s32[6,32]{1,0:T(8,128)} %blocks_hbm.1, bf16[6,576,128]{2,1,0:T(8,128)(2,1)} %bitcast.18, ...), custom_call_target="tpu_custom_call" | custom-call | tf_op jit(solution)/shard_map/attention/pallas_call | solution.py:198
  3.9 3.3 %collective-permute-start = (bf16[8,32,640]{2,1,0:T(8,128)(2,1)S(1)}, bf16[8,32,640]{2,1,0:T(8,128)(2,1)S(1)}, u32[]{:S(2)}, u32[]{:S(2)}) collective-permute-start(bf16[8,32,640]{2,1,0:T(8,128)(2,1)S(1)} %get-tuple-element.25), channel_id=1, source_target_pairs={{0,16},{16,0},{32,48},{48,32},{64,80},{80,64},{96,112},{112,96},{1... | collective-permute-start | bytes 983048 | tf_op jit(solution)/shard_map/ppermute | solution.py:565
  7.3 0.8 attention_rest.1
  8.1 1.4 %collective-permute-done.1.other_rest = bf16[8,16,640]{2,1,0:T(8,128)(2,1)S(1)} collective-permute-done((bf16[8,16,640]{2,1,0:T(8,128)(2,1)S(1)}, bf16[8,16,640]{2,1,0:T(8,128)(2,1)S(1)}, u32[]{:S(2)}, u32[]{:S(2)}) %collective-permute-start.1) | collective-permute-done | bytes 163872 | tf_op jit(solution)/shard_map/ppermute | solution.py:566
  10.0 3.9 %collective-permute-start.3 = (bf16[2,200,128]{2,1,0:T(8,128)(2,1)S(1)}, bf16[2,200,128]{2,1,0:T(8,128)(2,1)S(1)}, u32[]{:S(2)}, u32[]{:S(2)}) collective-permute-start(bf16[2,200,128]{2,1,0:T(8,128)(2,1)S(1)} %get-tuple-element.31.out_refs_0_), channel_id=1, source_target_pairs={{0,224},{16,240},{32,0},{48,16},{64,32},{80,48},{96,64},{112,80},{... | collective-permute-start | bytes 307208 | tf_op jit(solution)/shard_map/ppermute | solution.py:571
  14.1 1.9 %collective-permute-done.3.above_ref = bf16[2,200,128]{2,1,0:T(8,128)(2,1)S(1)} collective-permute-done((bf16[2,200,128]{2,1,0:T(8,128)(2,1)S(1)}, bf16[2,200,128]{2,1,0:T(8,128)(2,1)S(1)}, u32[]{:S(2)}, u32[]{:S(2)}) %collective-permute-start.3) | collective-permute-done | bytes 102432 | tf_op jit(solution)/shard_map/ppermute | solution.py:571
  16.0 2.0 %collective-permute-done.2.below_ref = bf16[3,200,128]{2,1,0:T(8,128)(2,1)S(1)} collective-permute-done((bf16[3,200,128]{2,1,0:T(8,128)(2,1)S(1)}, bf16[3,200,128]{2,1,0:T(8,128)(2,1)S(1)}, u32[]{:S(2)}, u32[]{:S(2)}) %collective-permute-start.2) | collective-permute-done | bytes 153632 | tf_op jit(solution)/shard_map/ppermute | solution.py:570
  18.5 2.1 %collective-permute-start.5 = (bf16[200,128]{1,0:T(8,128)(2,1)S(1)}, bf16[200,128]{1,0:T(8,128)(2,1)S(1)}, u32[]{:S(2)}, u32[]{:S(2)}) collective-permute-start(bf16[200,128]{1,0:T(8,128)(2,1)S(1)} %get-tuple-element.35), channel_id=1, source_target_pairs={{0,160},{16,176},{32,192},{48,208},{64,224},{80,240},{96,0},{112,1... | collective-permute-start | bytes 153608 | tf_op jit(solution)/shard_map/ppermute | solution.py:574
  20.6 1.4 %collective-permute-start.4 = (bf16[200,128]{1,0:T(8,128)(2,1)S(1)}, bf16[200,128]{1,0:T(8,128)(2,1)S(1)}, u32[]{:S(2)}, u32[]{:S(2)}) collective-permute-start(bf16[200,128]{1,0:T(8,128)(2,1)S(1)} %get-tuple-element.33._), channel_id=1, source_target_pairs={{0,64},{16,80},{32,96},{48,112},{64,128},{80,144},{96,160},{112,17... | collective-permute-start | bytes 153608 | tf_op jit(solution)/shard_map/ppermute | solution.py:573
  22.0 2.0 %side.1 = (f32[6,384]{1,0:T(8,128)}, bf16[2,56,96]{2,1,0:T(8,128)(2,1)S(1)}, bf16[56,96]{1,0:T(8,128)(2,1)S(1)}, bf16[128,48]{1,0:T(8,128)(2,1)S(1)}, f32[48,128]{1,0:T(8,128)S(1)}) custom-call(s32[1]{0:T(128)} %bitcast.ctx_ref, s32[4,96]{1,0:T(4,128)S(1)} %bitcast.13, f32[4,96]{1,0:T(4,128)S(1)} %bitcast.14, bf16[6,64,128]{2,1,0:T(8,128)(2,1)S(1)} %copy-done.4, ...), custom_call_target="tpu_custom_call" | custom-call | tf_op jit(solution)/shard_map/side/pallas_call | solution.py:268
  24.1 1.7 %collective-permute-done.4.far_below_ref = bf16[200,128]{1,0:T(8,128)(2,1)S(1)} collective-permute-done((bf16[200,128]{1,0:T(8,128)(2,1)S(1)}, bf16[200,128]{1,0:T(8,128)(2,1)S(1)}, u32[]{:S(2)}, u32[]{:S(2)}) %collective-permute-start.4) | collective-permute-done | bytes 51232 | tf_op jit(solution)/shard_map/ppermute | solution.py:573
  26.6 14.3 %all_to_all.20.values_ref = bf16[16,16,512]{2,1,0:T(8,128)(2,1)S(1)} all-to-all(bf16[16,16,512]{2,1,0:T(8,128)(2,1)S(1)} %values.1), channel_id=1, replica_groups=mesh['ctx'=16,'exp'=16] {'exp'}, dimensions={0} | all-to-all | bytes 524288 | tf_op jit(solution)/shard_map/all_to_all | solution.py:579
  41.4 3.8 %collective-permute-start.6 = (bf16[336,128]{1,0:T(8,128)(2,1)S(1)}, bf16[336,128]{1,0:T(8,128)(2,1)S(1)}, u32[]{:S(2)}, u32[]{:S(2)}) collective-permute-start(bf16[336,128]{1,0:T(8,128)(2,1)S(1)} %project.1), channel_id=1, source_target_pairs={{0,16},{16,0},{32,48},{48,32},{64,80},{80,64},{96,112},{112,96},{1... | collective-permute-start | bytes 258056 | tf_op jit(solution)/shard_map/ppermute | solution.py:581
  45.1 0.9 collective-permute-done.6
  46.1 1.3 %collective-permute-start.8 = (bf16[336,128]{1,0:T(8,128)(2,1)S(1)}, bf16[336,128]{1,0:T(8,128)(2,1)S(1)}, u32[]{:S(2)}, u32[]{:S(2)}) collective-permute-start(bf16[336,128]{1,0:T(8,128)(2,1)S(1)} %add_convert_fusion.own_ref), channel_id=1, source_target_pairs={{0,32},{16,48},{32,64},{48,80},{64,96},{80,112},{96,128},{112,144}... | collective-permute-start | bytes 258056 | tf_op jit(solution)/shard_map/ppermute | solution.py:584
  47.4 1.5 %collective-permute-start.7 = (bf16[336,128]{1,0:T(8,128)(2,1)S(1)}, bf16[336,128]{1,0:T(8,128)(2,1)S(1)}, u32[]{:S(2)}, u32[]{:S(2)}) collective-permute-start(bf16[336,128]{1,0:T(8,128)(2,1)S(1)} %add_convert_fusion.own_ref), channel_id=1, source_target_pairs={{0,224},{16,240},{32,0},{48,16},{64,32},{80,48},{96,64},{112,80},{... | collective-permute-start | bytes 258056 | tf_op jit(solution)/shard_map/ppermute | solution.py:583
  48.9 2.3 %collective-permute-done.8.below_ref = bf16[336,128]{1,0:T(8,128)(2,1)S(1)} collective-permute-done((bf16[336,128]{1,0:T(8,128)(2,1)S(1)}, bf16[336,128]{1,0:T(8,128)(2,1)S(1)}, u32[]{:S(2)}, u32[]{:S(2)}) %collective-permute-start.8) | collective-permute-done | bytes 86048 | tf_op jit(solution)/shard_map/ppermute | solution.py:584
  51.5 2.0 %collective-permute-start.9 = (bf16[200,128]{1,0:T(8,128)(2,1)S(1)}, bf16[200,128]{1,0:T(8,128)(2,1)S(1)}, u32[]{:S(2)}, u32[]{:S(2)}) collective-permute-start(bf16[200,128]{1,0:T(8,128)(2,1)S(1)} %get-tuple-element.39), channel_id=1, source_target_pairs={{0,160},{16,176},{32,192},{48,208},{64,224},{80,240},{96,0},{112,1... | collective-permute-start | bytes 153608 | tf_op jit(solution)/shard_map/ppermute | solution.py:586
  53.5 2.4 %collective-permute-start.10 = (bf16[200,128]{1,0:T(8,128)(2,1)S(1)}, bf16[200,128]{1,0:T(8,128)(2,1)S(1)}, u32[]{:S(2)}, u32[]{:S(2)}) collective-permute-start(bf16[200,128]{1,0:T(8,128)(2,1)S(1)} %get-tuple-element.40), channel_id=1, source_target_pairs={{0,64},{16,80},{32,96},{48,112},{64,128},{80,144},{96,160},{112,17... | collective-permute-start | bytes 153608 | tf_op jit(solution)/shard_map/ppermute | solution.py:587
  55.9 2.0 %base.1 = (f32[56,448]{1,0:T(8,128)S(1)}, bf16[448,4096]{1,0:T(8,128)(2,1)S(1)}) custom-call(bf16[336,128]{1,0:T(8,128)(2,1)S(1)} %add_convert_fusion.own_ref, bf16[336,128]{1,0:T(8,128)(2,1)S(1)} %collective-permute-done.7.above_ref, bf16[336,128]{1,0:T(8,128)(2,1)S(1)} %collective-permute-done.8.below_ref, bf16[96,448]{1,0:T(8,128)(2,1)S(1)} %copy-done.5, ...), custom_call_target="tpu_custom_call" | custom-call | tf_op jit(solution)/shard_map/base/pallas_call | solution.py:438
  59.3 11.5 %all_to_all.21.parts_ref = bf16[16,56,256]{2,1,0:T(8,128)(2,1)S(1)} all-to-all(bf16[16,56,256]{2,1,0:T(8,128)(2,1)S(1)} %get-tuple-element.42), channel_id=1, replica_groups=mesh['ctx'=16,'exp'=16] {'exp'}, dimensions={0} | all-to-all | bytes 917504 | tf_op jit(solution)/shard_map/all_to_all | solution.py:590
  70.9 9.8 %all_to_all.22.act_ref = bf16[16,48,128]{2,1,0:T(8,128)(2,1)S(1)} all-to-all(bf16[16,48,128]{2,1,0:T(8,128)(2,1)S(1)} %activation.1), channel_id=1, replica_groups=mesh['ctx'=16,'exp'=16] {'exp'}, dimensions={0} | all-to-all | bytes 393216 | tf_op jit(solution)/shard_map/all_to_all | solution.py:591
  80.7 0.9 expert_out.1
  81.6 18.9 %all_to_all.23.parts_ref = bf16[16,16,256]{2,1,0:T(8,128)(2,1)S(1)} all-to-all(bf16[16,16,256]{2,1,0:T(8,128)(2,1)S(1)} %expert_out.1), channel_id=1, replica_groups=mesh['ctx'=16,'exp'=16] {'ctx'}, dimensions={0} | all-to-all | bytes 262144 | tf_op jit(solution)/shard_map/all_to_all | solution.py:593
  (37 shorter events, 4.9 us)
Async XLA Ops:
  0.6 21.4 %copy-start.3 = (bf16[6,384,128]{2,1,0:T(8,128)(2,1)S(1)}, bf16[6,384,128]{2,1,0:T(8,128)(2,1)}, u32[]{:S(2)}) copy-start(bf16[6,384,128]{2,1,0:T(8,128)(2,1)} %keys_ref.1) | copy-start | bytes 1769476
  0.6 21.4 %copy-start.4 = (bf16[6,64,128]{2,1,0:T(8,128)(2,1)S(1)}, bf16[6,64,128]{2,1,0:T(8,128)(2,1)}, u32[]{:S(2)}) copy-start(bf16[6,64,128]{2,1,0:T(8,128)(2,1)} %iq_ref.1) | copy-start | bytes 294916
  0.7 21.4 %copy-start.6 = (f32[6,64]{1,0:T(8,128)S(1)}, f32[6,64]{1,0:T(8,128)}, u32[]{:S(2)}) copy-start(f32[6,64]{1,0:T(8,128)} %iw_ref.1) | copy-start | bytes 4612
  0.7 21.4 %copy-start.7 = (s32[96,4]{0,1:T(4,128)S(1)}, s32[96,4]{0,1:T(4,128)}, u32[]{:S(2)}) copy-start(s32[96,4]{0,1:T(4,128)} %param.24) | copy-start | bytes 4612
  0.7 21.3 %copy-start.8 = (f32[96,4]{0,1:T(4,128)S(1)}, f32[96,4]{0,1:T(4,128)}, u32[]{:S(2)}) copy-start(f32[96,4]{0,1:T(4,128)} %param.25) | copy-start | bytes 4612
  3.9 21.9 %copy-start.1 = (bf16[8,512,128]{2,1,0:T(8,128)(2,1)S(1)}, bf16[8,512,128]{2,1,0:T(8,128)(2,1)}, u32[]{:S(2)}) copy-start(bf16[8,512,128]{2,1,0:T(8,128)(2,1)} %w_ref.1) | copy-start | bytes 3145732
  3.9 5.6 %collective-permute-start = (bf16[8,32,640]{2,1,0:T(8,128)(2,1)S(1)}, bf16[8,32,640]{2,1,0:T(8,128)(2,1)S(1)}, u32[]{:S(2)}, u32[]{:S(2)}) collective-permute-start(bf16[8,32,640]{2,1,0:T(8,128)(2,1)S(1)} %get-tuple-element.25), channel_id=1, source_target_pairs={{0,16},{16,0},{32,48},{48,32},{64,80},{80,64},{96,112},{112,96},{1... | collective-permute-start | bytes 983048 | tf_op jit(solution)/shard_map/ppermute | solution.py:565
  8.0 1.5 %collective-permute-start.1 = (bf16[8,16,640]{2,1,0:T(8,128)(2,1)S(1)}, bf16[8,16,640]{2,1,0:T(8,128)(2,1)S(1)}, u32[]{:S(2)}, u32[]{:S(2)}) collective-permute-start(bf16[8,16,640]{2,1,0:T(8,128)(2,1)S(1)} %get-tuple-element.30), channel_id=1, source_target_pairs={{0,16},{16,0},{32,48},{48,32},{64,80},{80,64},{96,112},{112,96},{1... | collective-permute-start | bytes 491528 | tf_op jit(solution)/shard_map/ppermute | solution.py:566
  9.5 31.4 %copy-start.2 = (bf16[1024,448]{0,1:T(8,128)(2,1)S(1)}, bf16[1024,448]{0,1:T(8,128)(2,1)}, u32[]{:S(2)}) copy-start(bf16[1024,448]{0,1:T(8,128)(2,1)} %param.21) | copy-start | bytes 2752516
  9.9 8.1 %collective-permute-start.2 = (bf16[3,200,128]{2,1,0:T(8,128)(2,1)S(1)}, bf16[3,200,128]{2,1,0:T(8,128)(2,1)S(1)}, u32[]{:S(2)}, u32[]{:S(2)}) collective-permute-start(bf16[3,200,128]{2,1,0:T(8,128)(2,1)S(1)} %get-tuple-element.32), channel_id=1, source_target_pairs={{0,32},{16,48},{32,64},{48,80},{64,96},{80,112},{96,128},{112,144}... | collective-permute-start | bytes 460808 | tf_op jit(solution)/shard_map/ppermute | solution.py:570
  9.9 45.9 %copy-start.5 = (bf16[96,448]{1,0:T(8,128)(2,1)S(1)}, bf16[96,448]{1,0:T(8,128)(2,1)}, u32[]{:S(2)}) copy-start(bf16[96,448]{1,0:T(8,128)(2,1)} %hidden_ref.1) | copy-start | bytes 258052
  10.0 6.0 %collective-permute-start.3 = (bf16[2,200,128]{2,1,0:T(8,128)(2,1)S(1)}, bf16[2,200,128]{2,1,0:T(8,128)(2,1)S(1)}, u32[]{:S(2)}, u32[]{:S(2)}) collective-permute-start(bf16[2,200,128]{2,1,0:T(8,128)(2,1)S(1)} %get-tuple-element.31.out_refs_0_), channel_id=1, source_target_pairs={{0,224},{16,240},{32,0},{48,16},{64,32},{80,48},{96,64},{112,80},{... | collective-permute-start | bytes 307208 | tf_op jit(solution)/shard_map/ppermute | solution.py:571
  18.5 5.6 %collective-permute-start.5 = (bf16[200,128]{1,0:T(8,128)(2,1)S(1)}, bf16[200,128]{1,0:T(8,128)(2,1)S(1)}, u32[]{:S(2)}, u32[]{:S(2)}) collective-permute-start(bf16[200,128]{1,0:T(8,128)(2,1)S(1)} %get-tuple-element.35), channel_id=1, source_target_pairs={{0,160},{16,176},{32,192},{48,208},{64,224},{80,240},{96,0},{112,1... | collective-permute-start | bytes 153608 | tf_op jit(solution)/shard_map/ppermute | solution.py:574
  20.6 5.2 %collective-permute-start.4 = (bf16[200,128]{1,0:T(8,128)(2,1)S(1)}, bf16[200,128]{1,0:T(8,128)(2,1)S(1)}, u32[]{:S(2)}, u32[]{:S(2)}) collective-permute-start(bf16[200,128]{1,0:T(8,128)(2,1)S(1)} %get-tuple-element.33._), channel_id=1, source_target_pairs={{0,64},{16,80},{32,96},{48,112},{64,128},{80,144},{96,160},{112,17... | collective-permute-start | bytes 153608 | tf_op jit(solution)/shard_map/ppermute | solution.py:573
  26.6 32.0 %copy-start.9 = (f32[448]{0:T(512)S(1)}, f32[448]{0:T(512)}, u32[]{:S(2)}) copy-start(f32[448]{0:T(512)} %param.23) | copy-start | bytes 5380
  41.4 4.7 %collective-permute-start.6 = (bf16[336,128]{1,0:T(8,128)(2,1)S(1)}, bf16[336,128]{1,0:T(8,128)(2,1)S(1)}, u32[]{:S(2)}, u32[]{:S(2)}) collective-permute-start(bf16[336,128]{1,0:T(8,128)(2,1)S(1)} %project.1), channel_id=1, source_target_pairs={{0,16},{16,0},{32,48},{48,32},{64,80},{80,64},{96,112},{112,96},{1... | collective-permute-start | bytes 258056 | tf_op jit(solution)/shard_map/ppermute | solution.py:581
  46.1 5.1 %collective-permute-start.8 = (bf16[336,128]{1,0:T(8,128)(2,1)S(1)}, bf16[336,128]{1,0:T(8,128)(2,1)S(1)}, u32[]{:S(2)}, u32[]{:S(2)}) collective-permute-start(bf16[336,128]{1,0:T(8,128)(2,1)S(1)} %add_convert_fusion.own_ref), channel_id=1, source_target_pairs={{0,32},{16,48},{32,64},{48,80},{64,96},{80,112},{96,128},{112,144}... | collective-permute-start | bytes 258056 | tf_op jit(solution)/shard_map/ppermute | solution.py:584
  47.4 3.8 %collective-permute-start.7 = (bf16[336,128]{1,0:T(8,128)(2,1)S(1)}, bf16[336,128]{1,0:T(8,128)(2,1)S(1)}, u32[]{:S(2)}, u32[]{:S(2)}) collective-permute-start(bf16[336,128]{1,0:T(8,128)(2,1)S(1)} %add_convert_fusion.own_ref), channel_id=1, source_target_pairs={{0,224},{16,240},{32,0},{48,16},{64,32},{80,48},{96,64},{112,80},{... | collective-permute-start | bytes 258056 | tf_op jit(solution)/shard_map/ppermute | solution.py:583
  51.5 6.5 %collective-permute-start.9 = (bf16[200,128]{1,0:T(8,128)(2,1)S(1)}, bf16[200,128]{1,0:T(8,128)(2,1)S(1)}, u32[]{:S(2)}, u32[]{:S(2)}) collective-permute-start(bf16[200,128]{1,0:T(8,128)(2,1)S(1)} %get-tuple-element.39), channel_id=1, source_target_pairs={{0,160},{16,176},{32,192},{48,208},{64,224},{80,240},{96,0},{112,1... | collective-permute-start | bytes 153608 | tf_op jit(solution)/shard_map/ppermute | solution.py:586
  53.5 5.1 %collective-permute-start.10 = (bf16[200,128]{1,0:T(8,128)(2,1)S(1)}, bf16[200,128]{1,0:T(8,128)(2,1)S(1)}, u32[]{:S(2)}, u32[]{:S(2)}) collective-permute-start(bf16[200,128]{1,0:T(8,128)(2,1)S(1)} %get-tuple-element.40), channel_id=1, source_target_pairs={{0,64},{16,80},{32,96},{48,112},{64,128},{80,144},{96,160},{112,17... | collective-permute-start | bytes 153608 | tf_op jit(solution)/shard_map/ppermute | solution.py:587
  57.9 22.8 %copy-start = (bf16[1,2048,448]{1,2,0:T(8,128)(2,1)S(1)}, bf16[1,2048,448]{1,2,0:T(8,128)(2,1)}, u32[]{:S(2)}) copy-start(bf16[1,2048,448]{1,2,0:T(8,128)(2,1)} %param.27) | copy-start | bytes 5505028

commit v9 on v8

--- a/solution.py
+++ b/solution.py
@@ -462,14 +462,13 @@
     hi, mid, low = split3(squares)
     line = iota(squares.shape, 0)
     parts = jnp.where(line == 0, hi, jnp.where(line == 1, mid, jnp.where(line == 2, low, 0.0)))
-    parts = jnp.concatenate([parts, jnp.zeros((8, 256 - CAP), f32)], axis=1)
+    parts = jnp.concatenate([parts, jnp.zeros((8, 128 - CAP), f32)], axis=1)
     for e in range(0, n, 2):
         gate = dot(rows, w_ref[:, 128 * e : 128 * e + 256])
         up = dot(rows, w_ref[:, half + 128 * e : half + 128 * e + 256])
         for i in range(2):
             here = slice(128 * i, 128 * i + 128)
-            both = jnp.concatenate([gate[:, here], up[:, here]], axis=1)
-            out_ref[e + i] = jnp.concatenate([both, parts], axis=0).astype(bf16)
+            out_ref[e + i] = jnp.concatenate([gate[:, here], up[:, here], parts], axis=0).astype(bf16)
 
 
 def expert_in(near, far_up, far_down, gain, w_in, n_exp):
@@ -479,7 +478,7 @@
         in_specs=[VMEM] * 5,
         out_specs=[VMEM] * 2,
         out_shape=[
-            jax.ShapeDtypeStruct((n_exp, CAP + 8, 256), bf16),
+            jax.ShapeDtypeStruct((n_exp, 2 * CAP + 8, 128), bf16),
             jax.ShapeDtypeStruct((8, width), f32),
         ],
         compiler_params=params(),
@@ -489,11 +488,11 @@
 
 def act_kernel(parts_ref, out_ref):
     x = jnp.sum(parts_ref[...].astype(f32), axis=0)
-    line = x[CAP : CAP + 1, :CAP] + x[CAP + 1 : CAP + 2, :CAP] + x[CAP + 2 : CAP + 3, :CAP]
+    line = sum(x[2 * CAP + k : 2 * CAP + k + 1, :CAP] for k in range(3))
     diagonal = iota((CAP, CAP), 0) == iota((CAP, CAP), 1)
     squares = jnp.sum(jnp.where(diagonal, line, 0.0), axis=1, keepdims=True)
     inv = lax.rsqrt(squares / D + EPS)
-    gate, up = x[:CAP, :128] * inv, x[:CAP, 128:] * inv
+    gate, up = x[:CAP] * inv, x[CAP : 2 * CAP] * inv
     act = (jax.nn.silu(gate) * up).astype(bf16)
     for e in range(out_ref.shape[0]):
         out_ref[e] = act

time: 101 us -> 101 us (level)
  no operation moved by 1% of the time
where the time goes in v9:
time: 101 us
  blocking collectives  54.3 us (54%)
  starting transfers between devices  21.8 us (22%)
  Pallas kernels  13 us (13%)
  waiting for transfers between devices  10.9 us (11%)
    all_to_all x1, blocking collectives, local(): outs = lax.all_to_all(outs, 'ctx', 0, 0)  19 us
    all_to_all x1, blocking collectives, local(): vals = lax.all_to_all(vals, 'exp', 0, 0)  14.3 us
    all_to_all x1, blocking collectives, local(): terms = lax.all_to_all(terms, 'exp', 0, 0)  11.2 us
    all_to_all x1, blocking collectives, local(): act = lax.all_to_all(activation(terms), 'exp', 0, 0)  9.78 us
    ppermute x1, starting transfers between devices, local(): above = lax.ppermute(down, 'ctx', along_z(-2))  3.91 us
    ppermute x1, starting transfers between devices, local(): own = part.astype(f32) + lax.ppermute(part, 'ctx', other_core).astype(f32)  3.77 us
    ppermute x1, starting transfers between devices, local(): other = lax.ppermute(other, 'ctx', other_core)  3.33 us
    pallas_call x1, Pallas kernels, attention(): pl.pallas_call(attention_kernel, in_specs=[SMEM, HBM, HBM, HBM], out_spec...  3.22 us
  transfers between devices with their start and end apart: 11, of which 7 were waited for; matrix products, arithmetic and copies ran while one was open for 0% of the time, Pallas kernels for 5%

profile of v9, /device:TPU:1, one launch (start us, length us, event | category | flops | bytes accessed | tf_op | source)
XLA Modules:
  0.0 100.9 jit_solution(11353550253349556915)
XLA Ops:
  0.7 3.2 %attention.1 = (f32[8,32,640]{2,1,0:T(8,128)S(1)}, bf16[8,32,640]{2,1,0:T(8,128)(2,1)S(1)}, s32[6,32]{1,0:T(8,128)S(1)}, bf16[2,576,128]{2,1,0:T(8,128)(2,1)S(1)}, bf16[2,576,384]{2,1,0:T(8,128)(2,1)S(1)}) custom-call(s32[1]{0:T(128)} %bitcast.ctx_ref, s32[6,32]{1,0:T(8,128)} %blocks_hbm.1, bf16[6,576,128]{2,1,0:T(8,128)(2,1)} %bitcast.18, ...), custom_call_target="tpu_custom_call" | custom-call | tf_op jit(solution)/shard_map/attention/pallas_call | solution.py:198
  3.9 3.3 %collective-permute-start = (bf16[8,32,640]{2,1,0:T(8,128)(2,1)S(1)}, bf16[8,32,640]{2,1,0:T(8,128)(2,1)S(1)}, u32[]{:S(2)}, u32[]{:S(2)}) collective-permute-start(bf16[8,32,640]{2,1,0:T(8,128)(2,1)S(1)} %get-tuple-element.25), channel_id=1, source_target_pairs={{0,16},{16,0},{32,48},{48,32},{64,80},{80,64},{96,112},{112,96},{1... | collective-permute-start | bytes 983048 | tf_op jit(solution)/shard_map/ppermute | solution.py:564
  7.3 0.8 attention_rest.1
  8.1 1.4 %collective-permute-done.1.other_rest = bf16[8,16,640]{2,1,0:T(8,128)(2,1)S(1)} collective-permute-done((bf16[8,16,640]{2,1,0:T(8,128)(2,1)S(1)}, bf16[8,16,640]{2,1,0:T(8,128)(2,1)S(1)}, u32[]{:S(2)}, u32[]{:S(2)}) %collective-permute-start.1) | collective-permute-done | bytes 163872 | tf_op jit(solution)/shard_map/ppermute | solution.py:565
  10.0 3.9 %collective-permute-start.3 = (bf16[2,200,128]{2,1,0:T(8,128)(2,1)S(1)}, bf16[2,200,128]{2,1,0:T(8,128)(2,1)S(1)}, u32[]{:S(2)}, u32[]{:S(2)}) collective-permute-start(bf16[2,200,128]{2,1,0:T(8,128)(2,1)S(1)} %get-tuple-element.31.out_refs_0_), channel_id=1, source_target_pairs={{0,224},{16,240},{32,0},{48,16},{64,32},{80,48},{96,64},{112,80},{... | collective-permute-start | bytes 307208 | tf_op jit(solution)/shard_map/ppermute | solution.py:570
  14.1 1.9 %collective-permute-done.3.above_ref = bf16[2,200,128]{2,1,0:T(8,128)(2,1)S(1)} collective-permute-done((bf16[2,200,128]{2,1,0:T(8,128)(2,1)S(1)}, bf16[2,200,128]{2,1,0:T(8,128)(2,1)S(1)}, u32[]{:S(2)}, u32[]{:S(2)}) %collective-permute-start.3) | collective-permute-done | bytes 102432 | tf_op jit(solution)/shard_map/ppermute | solution.py:570
  16.0 2.0 %collective-permute-done.2.below_ref = bf16[3,200,128]{2,1,0:T(8,128)(2,1)S(1)} collective-permute-done((bf16[3,200,128]{2,1,0:T(8,128)(2,1)S(1)}, bf16[3,200,128]{2,1,0:T(8,128)(2,1)S(1)}, u32[]{:S(2)}, u32[]{:S(2)}) %collective-permute-start.2) | collective-permute-done | bytes 153632 | tf_op jit(solution)/shard_map/ppermute | solution.py:569
  18.5 2.1 %collective-permute-start.5 = (bf16[200,128]{1,0:T(8,128)(2,1)S(1)}, bf16[200,128]{1,0:T(8,128)(2,1)S(1)}, u32[]{:S(2)}, u32[]{:S(2)}) collective-permute-start(bf16[200,128]{1,0:T(8,128)(2,1)S(1)} %get-tuple-element.35), channel_id=1, source_target_pairs={{0,160},{16,176},{32,192},{48,208},{64,224},{80,240},{96,0},{112,1... | collective-permute-start | bytes 153608 | tf_op jit(solution)/shard_map/ppermute | solution.py:573
  20.6 1.4 %collective-permute-start.4 = (bf16[200,128]{1,0:T(8,128)(2,1)S(1)}, bf16[200,128]{1,0:T(8,128)(2,1)S(1)}, u32[]{:S(2)}, u32[]{:S(2)}) collective-permute-start(bf16[200,128]{1,0:T(8,128)(2,1)S(1)} %get-tuple-element.33._), channel_id=1, source_target_pairs={{0,64},{16,80},{32,96},{48,112},{64,128},{80,144},{96,160},{112,17... | collective-permute-start | bytes 153608 | tf_op jit(solution)/shard_map/ppermute | solution.py:572
  22.0 2.0 %side.1 = (f32[6,384]{1,0:T(8,128)}, bf16[2,56,96]{2,1,0:T(8,128)(2,1)S(1)}, bf16[56,96]{1,0:T(8,128)(2,1)S(1)}, bf16[128,48]{1,0:T(8,128)(2,1)S(1)}, f32[48,128]{1,0:T(8,128)S(1)}) custom-call(s32[1]{0:T(128)} %bitcast.ctx_ref, s32[4,96]{1,0:T(4,128)S(1)} %bitcast.13, f32[4,96]{1,0:T(4,128)S(1)} %bitcast.14, bf16[6,64,128]{2,1,0:T(8,128)(2,1)S(1)} %copy-done.4, ...), custom_call_target="tpu_custom_call" | custom-call | tf_op jit(solution)/shard_map/side/pallas_call | solution.py:268
  24.1 1.7 %collective-permute-done.4.far_below_ref = bf16[200,128]{1,0:T(8,128)(2,1)S(1)} collective-permute-done((bf16[200,128]{1,0:T(8,128)(2,1)S(1)}, bf16[200,128]{1,0:T(8,128)(2,1)S(1)}, u32[]{:S(2)}, u32[]{:S(2)}) %collective-permute-start.4) | collective-permute-done | bytes 51232 | tf_op jit(solution)/shard_map/ppermute | solution.py:572
  26.6 14.3 %all_to_all.20.values_ref = bf16[16,16,512]{2,1,0:T(8,128)(2,1)S(1)} all-to-all(bf16[16,16,512]{2,1,0:T(8,128)(2,1)S(1)} %values.1), channel_id=1, replica_groups=mesh['ctx'=16,'exp'=16] {'exp'}, dimensions={0} | all-to-all | bytes 524288 | tf_op jit(solution)/shard_map/all_to_all | solution.py:578
  41.4 3.8 %collective-permute-start.6 = (bf16[336,128]{1,0:T(8,128)(2,1)S(1)}, bf16[336,128]{1,0:T(8,128)(2,1)S(1)}, u32[]{:S(2)}, u32[]{:S(2)}) collective-permute-start(bf16[336,128]{1,0:T(8,128)(2,1)S(1)} %project.1), channel_id=1, source_target_pairs={{0,16},{16,0},{32,48},{48,32},{64,80},{80,64},{96,112},{112,96},{1... | collective-permute-start | bytes 258056 | tf_op jit(solution)/shard_map/ppermute | solution.py:580
  45.1 0.9 collective-permute-done.6
  46.1 1.3 %collective-permute-start.8 = (bf16[336,128]{1,0:T(8,128)(2,1)S(1)}, bf16[336,128]{1,0:T(8,128)(2,1)S(1)}, u32[]{:S(2)}, u32[]{:S(2)}) collective-permute-start(bf16[336,128]{1,0:T(8,128)(2,1)S(1)} %add_convert_fusion.own_ref), channel_id=1, source_target_pairs={{0,32},{16,48},{32,64},{48,80},{64,96},{80,112},{96,128},{112,144}... | collective-permute-start | bytes 258056 | tf_op jit(solution)/shard_map/ppermute | solution.py:583
  47.4 1.5 %collective-permute-start.7 = (bf16[336,128]{1,0:T(8,128)(2,1)S(1)}, bf16[336,128]{1,0:T(8,128)(2,1)S(1)}, u32[]{:S(2)}, u32[]{:S(2)}) collective-permute-start(bf16[336,128]{1,0:T(8,128)(2,1)S(1)} %add_convert_fusion.own_ref), channel_id=1, source_target_pairs={{0,224},{16,240},{32,0},{48,16},{64,32},{80,48},{96,64},{112,80},{... | collective-permute-start | bytes 258056 | tf_op jit(solution)/shard_map/ppermute | solution.py:582
  48.9 2.3 %collective-permute-done.8.below_ref = bf16[336,128]{1,0:T(8,128)(2,1)S(1)} collective-permute-done((bf16[336,128]{1,0:T(8,128)(2,1)S(1)}, bf16[336,128]{1,0:T(8,128)(2,1)S(1)}, u32[]{:S(2)}, u32[]{:S(2)}) %collective-permute-start.8) | collective-permute-done | bytes 86048 | tf_op jit(solution)/shard_map/ppermute | solution.py:583
  51.5 2.0 %collective-permute-start.9 = (bf16[200,128]{1,0:T(8,128)(2,1)S(1)}, bf16[200,128]{1,0:T(8,128)(2,1)S(1)}, u32[]{:S(2)}, u32[]{:S(2)}) collective-permute-start(bf16[200,128]{1,0:T(8,128)(2,1)S(1)} %get-tuple-element.39), channel_id=1, source_target_pairs={{0,160},{16,176},{32,192},{48,208},{64,224},{80,240},{96,0},{112,1... | collective-permute-start | bytes 153608 | tf_op jit(solution)/shard_map/ppermute | solution.py:585
  53.5 2.4 %collective-permute-start.10 = (bf16[200,128]{1,0:T(8,128)(2,1)S(1)}, bf16[200,128]{1,0:T(8,128)(2,1)S(1)}, u32[]{:S(2)}, u32[]{:S(2)}) collective-permute-start(bf16[200,128]{1,0:T(8,128)(2,1)S(1)} %get-tuple-element.40), channel_id=1, source_target_pairs={{0,64},{16,80},{32,96},{48,112},{64,128},{80,144},{96,160},{112,17... | collective-permute-start | bytes 153608 | tf_op jit(solution)/shard_map/ppermute | solution.py:586
  55.9 2.0 %base.1 = (f32[56,448]{1,0:T(8,128)S(1)}, bf16[448,4096]{1,0:T(8,128)(2,1)S(1)}) custom-call(bf16[336,128]{1,0:T(8,128)(2,1)S(1)} %add_convert_fusion.own_ref, bf16[336,128]{1,0:T(8,128)(2,1)S(1)} %collective-permute-done.7.above_ref, bf16[336,128]{1,0:T(8,128)(2,1)S(1)} %collective-permute-done.8.below_ref, bf16[96,448]{1,0:T(8,128)(2,1)S(1)} %copy-done.5, ...), custom_call_target="tpu_custom_call" | custom-call | tf_op jit(solution)/shard_map/base/pallas_call | solution.py:438
  59.3 11.2 %all_to_all.21.parts_ref = bf16[16,104,128]{2,1,0:T(8,128)(2,1)S(1)} all-to-all(bf16[16,104,128]{2,1,0:T(8,128)(2,1)S(1)} %get-tuple-element.42), channel_id=1, replica_groups=mesh['ctx'=16,'exp'=16] {'exp'}, dimensions={0} | all-to-all | bytes 851968 | tf_op jit(solution)/shard_map/all_to_all | solution.py:589
  70.6 9.8 %all_to_all.22.act_ref = bf16[16,48,128]{2,1,0:T(8,128)(2,1)S(1)} all-to-all(bf16[16,48,128]{2,1,0:T(8,128)(2,1)S(1)} %activation.1), channel_id=1, replica_groups=mesh['ctx'=16,'exp'=16] {'exp'}, dimensions={0} | all-to-all | bytes 393216 | tf_op jit(solution)/shard_map/all_to_all | solution.py:590
  80.4 0.9 expert_out.1
  81.3 19.0 %all_to_all.23.parts_ref = bf16[16,16,256]{2,1,0:T(8,128)(2,1)S(1)} all-to-all(bf16[16,16,256]{2,1,0:T(8,128)(2,1)S(1)} %expert_out.1), channel_id=1, replica_groups=mesh['ctx'=16,'exp'=16] {'ctx'}, dimensions={0} | all-to-all | bytes 262144 | tf_op jit(solution)/shard_map/all_to_all | solution.py:592
  (37 shorter events, 4.9 us)
Async XLA Ops:
  0.6 21.4 %copy-start.3 = (bf16[6,384,128]{2,1,0:T(8,128)(2,1)S(1)}, bf16[6,384,128]{2,1,0:T(8,128)(2,1)}, u32[]{:S(2)}) copy-start(bf16[6,384,128]{2,1,0:T(8,128)(2,1)} %keys_ref.1) | copy-start | bytes 1769476
  0.6 21.4 %copy-start.4 = (bf16[6,64,128]{2,1,0:T(8,128)(2,1)S(1)}, bf16[6,64,128]{2,1,0:T(8,128)(2,1)}, u32[]{:S(2)}) copy-start(bf16[6,64,128]{2,1,0:T(8,128)(2,1)} %iq_ref.1) | copy-start | bytes 294916
  0.7 21.4 %copy-start.6 = (f32[6,64]{1,0:T(8,128)S(1)}, f32[6,64]{1,0:T(8,128)}, u32[]{:S(2)}) copy-start(f32[6,64]{1,0:T(8,128)} %iw_ref.1) | copy-start | bytes 4612
  0.7 21.4 %copy-start.7 = (s32[96,4]{0,1:T(4,128)S(1)}, s32[96,4]{0,1:T(4,128)}, u32[]{:S(2)}) copy-start(s32[96,4]{0,1:T(4,128)} %param.24) | copy-start | bytes 4612
  0.7 21.3 %copy-start.8 = (f32[96,4]{0,1:T(4,128)S(1)}, f32[96,4]{0,1:T(4,128)}, u32[]{:S(2)}) copy-start(f32[96,4]{0,1:T(4,128)} %param.25) | copy-start | bytes 4612
  3.9 21.9 %copy-start.1 = (bf16[8,512,128]{2,1,0:T(8,128)(2,1)S(1)}, bf16[8,512,128]{2,1,0:T(8,128)(2,1)}, u32[]{:S(2)}) copy-start(bf16[8,512,128]{2,1,0:T(8,128)(2,1)} %w_ref.1) | copy-start | bytes 3145732
  3.9 5.6 %collective-permute-start = (bf16[8,32,640]{2,1,0:T(8,128)(2,1)S(1)}, bf16[8,32,640]{2,1,0:T(8,128)(2,1)S(1)}, u32[]{:S(2)}, u32[]{:S(2)}) collective-permute-start(bf16[8,32,640]{2,1,0:T(8,128)(2,1)S(1)} %get-tuple-element.25), channel_id=1, source_target_pairs={{0,16},{16,0},{32,48},{48,32},{64,80},{80,64},{96,112},{112,96},{1... | collective-permute-start | bytes 983048 | tf_op jit(solution)/shard_map/ppermute | solution.py:564
  8.0 1.5 %collective-permute-start.1 = (bf16[8,16,640]{2,1,0:T(8,128)(2,1)S(1)}, bf16[8,16,640]{2,1,0:T(8,128)(2,1)S(1)}, u32[]{:S(2)}, u32[]{:S(2)}) collective-permute-start(bf16[8,16,640]{2,1,0:T(8,128)(2,1)S(1)} %get-tuple-element.30), channel_id=1, source_target_pairs={{0,16},{16,0},{32,48},{48,32},{64,80},{80,64},{96,112},{112,96},{1... | collective-permute-start | bytes 491528 | tf_op jit(solution)/shard_map/ppermute | solution.py:565
  9.5 31.4 %copy-start.2 = (bf16[1024,448]{0,1:T(8,128)(2,1)S(1)}, bf16[1024,448]{0,1:T(8,128)(2,1)}, u32[]{:S(2)}) copy-start(bf16[1024,448]{0,1:T(8,128)(2,1)} %param.21) | copy-start | bytes 2752516
  9.9 8.1 %collective-permute-start.2 = (bf16[3,200,128]{2,1,0:T(8,128)(2,1)S(1)}, bf16[3,200,128]{2,1,0:T(8,128)(2,1)S(1)}, u32[]{:S(2)}, u32[]{:S(2)}) collective-permute-start(bf16[3,200,128]{2,1,0:T(8,128)(2,1)S(1)} %get-tuple-element.32), channel_id=1, source_target_pairs={{0,32},{16,48},{32,64},{48,80},{64,96},{80,112},{96,128},{112,144}... | collective-permute-start | bytes 460808 | tf_op jit(solution)/shard_map/ppermute | solution.py:569
  9.9 45.9 %copy-start.5 = (bf16[96,448]{1,0:T(8,128)(2,1)S(1)}, bf16[96,448]{1,0:T(8,128)(2,1)}, u32[]{:S(2)}) copy-start(bf16[96,448]{1,0:T(8,128)(2,1)} %hidden_ref.1) | copy-start | bytes 258052
  10.0 6.0 %collective-permute-start.3 = (bf16[2,200,128]{2,1,0:T(8,128)(2,1)S(1)}, bf16[2,200,128]{2,1,0:T(8,128)(2,1)S(1)}, u32[]{:S(2)}, u32[]{:S(2)}) collective-permute-start(bf16[2,200,128]{2,1,0:T(8,128)(2,1)S(1)} %get-tuple-element.31.out_refs_0_), channel_id=1, source_target_pairs={{0,224},{16,240},{32,0},{48,16},{64,32},{80,48},{96,64},{112,80},{... | collective-permute-start | bytes 307208 | tf_op jit(solution)/shard_map/ppermute | solution.py:570
  18.5 5.6 %collective-permute-start.5 = (bf16[200,128]{1,0:T(8,128)(2,1)S(1)}, bf16[200,128]{1,0:T(8,128)(2,1)S(1)}, u32[]{:S(2)}, u32[]{:S(2)}) collective-permute-start(bf16[200,128]{1,0:T(8,128)(2,1)S(1)} %get-tuple-element.35), channel_id=1, source_target_pairs={{0,160},{16,176},{32,192},{48,208},{64,224},{80,240},{96,0},{112,1... | collective-permute-start | bytes 153608 | tf_op jit(solution)/shard_map/ppermute | solution.py:573
  20.6 5.2 %collective-permute-start.4 = (bf16[200,128]{1,0:T(8,128)(2,1)S(1)}, bf16[200,128]{1,0:T(8,128)(2,1)S(1)}, u32[]{:S(2)}, u32[]{:S(2)}) collective-permute-start(bf16[200,128]{1,0:T(8,128)(2,1)S(1)} %get-tuple-element.33._), channel_id=1, source_target_pairs={{0,64},{16,80},{32,96},{48,112},{64,128},{80,144},{96,160},{112,17... | collective-permute-start | bytes 153608 | tf_op jit(solution)/shard_map/ppermute | solution.py:572
  26.6 32.0 %copy-start.9 = (f32[448]{0:T(512)S(1)}, f32[448]{0:T(512)}, u32[]{:S(2)}) copy-start(f32[448]{0:T(512)} %param.23) | copy-start | bytes 5380
  41.4 4.7 %collective-permute-start.6 = (bf16[336,128]{1,0:T(8,128)(2,1)S(1)}, bf16[336,128]{1,0:T(8,128)(2,1)S(1)}, u32[]{:S(2)}, u32[]{:S(2)}) collective-permute-start(bf16[336,128]{1,0:T(8,128)(2,1)S(1)} %project.1), channel_id=1, source_target_pairs={{0,16},{16,0},{32,48},{48,32},{64,80},{80,64},{96,112},{112,96},{1... | collective-permute-start | bytes 258056 | tf_op jit(solution)/shard_map/ppermute | solution.py:580
  46.1 5.1 %collective-permute-start.8 = (bf16[336,128]{1,0:T(8,128)(2,1)S(1)}, bf16[336,128]{1,0:T(8,128)(2,1)S(1)}, u32[]{:S(2)}, u32[]{:S(2)}) collective-permute-start(bf16[336,128]{1,0:T(8,128)(2,1)S(1)} %add_convert_fusion.own_ref), channel_id=1, source_target_pairs={{0,32},{16,48},{32,64},{48,80},{64,96},{80,112},{96,128},{112,144}... | collective-permute-start | bytes 258056 | tf_op jit(solution)/shard_map/ppermute | solution.py:583
  47.4 3.8 %collective-permute-start.7 = (bf16[336,128]{1,0:T(8,128)(2,1)S(1)}, bf16[336,128]{1,0:T(8,128)(2,1)S(1)}, u32[]{:S(2)}, u32[]{:S(2)}) collective-permute-start(bf16[336,128]{1,0:T(8,128)(2,1)S(1)} %add_convert_fusion.own_ref), channel_id=1, source_target_pairs={{0,224},{16,240},{32,0},{48,16},{64,32},{80,48},{96,64},{112,80},{... | collective-permute-start | bytes 258056 | tf_op jit(solution)/shard_map/ppermute | solution.py:582
  51.5 6.5 %collective-permute-start.9 = (bf16[200,128]{1,0:T(8,128)(2,1)S(1)}, bf16[200,128]{1,0:T(8,128)(2,1)S(1)}, u32[]{:S(2)}, u32[]{:S(2)}) collective-permute-start(bf16[200,128]{1,0:T(8,128)(2,1)S(1)} %get-tuple-element.39), channel_id=1, source_target_pairs={{0,160},{16,176},{32,192},{48,208},{64,224},{80,240},{96,0},{112,1... | collective-permute-start | bytes 153608 | tf_op jit(solution)/shard_map/ppermute | solution.py:585
  53.5 5.1 %collective-permute-start.10 = (bf16[200,128]{1,0:T(8,128)(2,1)S(1)}, bf16[200,128]{1,0:T(8,128)(2,1)S(1)}, u32[]{:S(2)}, u32[]{:S(2)}) collective-permute-start(bf16[200,128]{1,0:T(8,128)(2,1)S(1)} %get-tuple-element.40), channel_id=1, source_target_pairs={{0,64},{16,80},{32,96},{48,112},{64,128},{80,144},{96,160},{112,17... | collective-permute-start | bytes 153608 | tf_op jit(solution)/shard_map/ppermute | solution.py:586
  57.9 22.5 %copy-start = (bf16[1,2048,448]{1,2,0:T(8,128)(2,1)S(1)}, bf16[1,2048,448]{1,2,0:T(8,128)(2,1)}, u32[]{:S(2)}) copy-start(bf16[1,2048,448]{1,2,0:T(8,128)(2,1)} %param.27) | copy-start | bytes 5505028
